TPU v7x, 128 devices: a whole 4x4x4 slice. The times are simulated.
128 devices in a mesh: section: 2 (over y_lo), expert: 16 (over x, z), shard: 4 (over y_hi, core).
Axes of the slice: x: 4, y: 4 (y_hi: 2, y_lo: 2; y = y_hi * 2 + y_lo), z: 4, core: 2. Of those that a mesh axis runs over, the one named last changes fastest.
Arguments:
- stream: bfloat16 [2, 2, 8192, 768], P('section', None, ('expert', 'shard')), may hold values from -6 to 6
- norm_gains: float32 [2, 2, 768], P('section'), may hold values from 0.25 to 1.75
- attn_qkv: bfloat16 [2, 3, 768, 768], P('section', None, None, 'shard'), may hold values from -0.21875 to 0.21875
- attn_out: bfloat16 [2, 768, 768], P('section', 'shard'), may hold values from -3.5 to 3.5
- rel_bias: float32 [2, 32, 12], P('section', None, 'shard'), may hold values from -4 to 4
- router: bfloat16 [2, 768, 32], P('section'), may hold values from -0.21875 to 0.21875
- expert_in: bfloat16 [2, 32, 768, 3072], P('section', 'expert', None, 'shard'), may hold values from -0.21875 to 0.21875
- expert_out: bfloat16 [2, 32, 3072, 768], P('section', 'expert', 'shard'), may hold values from -3.5 to 3.5
- routes: int32 [2, 2, 8192], P('section', None, ('expert', 'shard')), may hold values from 0 to 31, as said below
- slots: int32 [2, 2, 8192], P('section', None, ('expert', 'shard')), may hold values from 0 to 5, as said below
Outputs:
- end_rows: bfloat16 [2, 2, 8192, 768], P('section', None, ('expert', 'shard'))
- grad_gains: float32 [2, 2, 768], P('section')
- grad_qkv: float32 [2, 3, 768, 768], P('section', None, None, 'shard')
- grad_attn_out: float32 [2, 768, 768], P('section', 'shard')
- grad_bias: float32 [2, 32, 12], P('section', None, 'shard')
- grad_router: float32 [2, 768, 32], P('section')
- grad_expert_in: float32 [2, 32, 768, 3072], P('section', 'expert', None, 'shard')
- grad_expert_out: float32 [2, 32, 3072, 768], P('section', 'expert', 'shard')
Inputs may be any that keep to these rules, and one draw needn't show every extreme that they name: `routes`: within the rows of one device in one micro-batch (aligned blocks of 128 rows), each expert is named at most 6 times; in every micro-batch of every layer one expert is named exactly 6 times by the rows of every device. Rows of one device in one micro-batch that name the same expert hold distinct slots.
All inputs are finite; a program needn't handle non-finite values.
Results may differ from a plain program's by a relative error of at most 0.04.
Values may be sent and summed in bfloat16 or wider, within the bound.
A program may use at most 192 MiB of HBM per device.

v0:
```python
import jax
import jax.numpy as jnp
from jax import lax
from jax.sharding import PartitionSpec as P

HEAD_DIM = 64
LEN = 512


def from_partner(block, axis, apart):
    count = lax.axis_size(axis)
    route = []
    for low in range(count):
        high = low | 1 << apart
        if high != low and high < count:
            route += [(low, high), (high, low)]
    return lax.ppermute(block, axis, route)


def rms_norm(values, gain):
    return values * lax.rsqrt(jnp.mean(values * values, axis=-1, keepdims=True) + 1e-06) * gain


def bucket_of(offsets):
    distance = jnp.abs(offsets)
    far_bucket = 8 + sum(
        ((distance >= threshold).astype(jnp.int32) for threshold in (12, 16, 23, 32, 46, 64, 91))
    )
    near_far = jnp.where(distance < 8, distance, far_bucket)
    return near_far + 16 * (offsets > 0).astype(jnp.int32)


def bias_block(bias_table, first_row, row_count, length):
    span_width = length + row_count - 1
    offsets = jnp.arange(span_width, dtype=jnp.int32) - (row_count - 1) - first_row
    picked_bucket = (
        bucket_of(offsets)[:, None] == jnp.arange(bias_table.shape[0], dtype=jnp.int32)[None, :]
    ).astype(jnp.float32)
    by_offset = jnp.dot(picked_bucket, bias_table, precision=lax.Precision.HIGHEST).T
    head_count = bias_table.shape[1]
    repeated = jnp.broadcast_to(by_offset[:, None, :], (head_count, row_count, span_width)).reshape(
        head_count, row_count * span_width
    )
    skewed = repeated[:, row_count - 1 : row_count - 1 + row_count * (span_width - 1)].reshape(
        head_count, row_count, span_width - 1
    )
    return skewed[:, :, :length]


def split_heads(packed, which_one):
    return packed[:, which_one].reshape(packed.shape[0], -1, HEAD_DIM)


def attend(packed, bias_table, length):
    total_rows = packed.shape[0]
    head_count = bias_table.shape[1]
    queries = split_heads(packed, 0)
    key_rows = split_heads(packed, 1)
    value_rows = split_heads(packed, 2)
    block_rows = min(512, length)
    per_seq = length // block_rows

    def one_block(number):
        first_row = number % per_seq * block_rows
        scores = (
            jnp.einsum("qhd,khd->hqk", queries, key_rows, preferred_element_type=jnp.float32)
            * 0.125
        )
        scores = scores + bias_block(bias_table, first_row, block_rows, length)
        log_total = jax.nn.logsumexp(scores, axis=-1)
        chances = jnp.exp(scores - log_total[:, :, None]).astype(jnp.bfloat16)
        mixed_block = jnp.einsum(
            "hqk,khd->qhd", chances, value_rows, preferred_element_type=jnp.float32
        )
        return (
            mixed_block.astype(jnp.bfloat16).reshape(block_rows, head_count * HEAD_DIM),
            log_total,
        )

    mixed_heads, log_total = lax.map(
        one_block, jnp.arange(total_rows // block_rows, dtype=jnp.int32)
    )
    return (mixed_heads.reshape(total_rows, head_count * HEAD_DIM), log_total)


def attend_back(packed, log_total, mixed_grad, bias_table, length):
    total_rows = packed.shape[0]
    head_count = bias_table.shape[1]
    queries = split_heads(packed, 0)
    key_rows = split_heads(packed, 1)
    value_rows = split_heads(packed, 2)
    grad_rows = mixed_grad.reshape(total_rows, head_count, HEAD_DIM)
    block_rows = min(512, length)
    per_seq = length // block_rows

    def one_block(carried, number):
        key_grad, value_grad, table_grad = carried
        first_row = number % per_seq * block_rows
        scores = (
            jnp.einsum("qhd,khd->hqk", queries, key_rows, preferred_element_type=jnp.float32)
            * 0.125
        )
        scores = scores + bias_block(bias_table, first_row, block_rows, length)
        chances = jnp.exp(scores - log_total[number][:, :, None])
        grad_weights = jnp.einsum(
            "qhd,khd->hqk", grad_rows, value_rows, preferred_element_type=jnp.float32
        )
        grad_scores = chances * (
            grad_weights - jnp.sum(chances * grad_weights, axis=-1, keepdims=True)
        )
        grad_scores = grad_scores.astype(jnp.bfloat16)
        query_grad = (
            jnp.einsum("hqk,khd->qhd", grad_scores, key_rows, preferred_element_type=jnp.float32)
            * 0.125
        )
        key_part = (
            jnp.einsum("hqk,qhd->khd", grad_scores, queries, preferred_element_type=jnp.float32)
            * 0.125
        )
        value_part = jnp.einsum(
            "hqk,qhd->khd",
            chances.astype(jnp.bfloat16),
            grad_rows,
            preferred_element_type=jnp.float32,
        )
        key_grad = key_grad + key_part
        value_grad = value_grad + value_part
        _, pull_back = jax.vjp(
            lambda source: bias_block(source, first_row, block_rows, length), bias_table
        )
        table_grad = table_grad + pull_back(grad_scores.astype(jnp.float32))[0]
        return ((key_grad, value_grad, table_grad), query_grad)

    empty_rows = jnp.zeros((total_rows, head_count, HEAD_DIM), jnp.float32)
    carried = (empty_rows, empty_rows, jnp.zeros_like(bias_table))
    (key_grad, value_grad, table_grad), query_grad = lax.scan(
        one_block, carried, jnp.arange(total_rows // block_rows, dtype=jnp.int32)
    )
    width = head_count * HEAD_DIM
    packed_grad = jnp.stack(
        [
            query_grad.reshape(total_rows, width),
            key_grad.reshape(total_rows, width),
            value_grad.reshape(total_rows, width),
        ],
        axis=1,
    )
    return (packed_grad.astype(jnp.bfloat16), table_grad)


def spread_matrix(route_ids, slot_ids, capacity, experts):
    target = slot_ids * experts + route_ids
    return (target[:, None] == jnp.arange(capacity * experts, dtype=jnp.int32)[None, :]).astype(
        jnp.bfloat16
    )


def expert_pass(buffer, inner, terms):
    source = lax.all_gather(buffer, "shard", axis=0, tiled=True)
    arrived = lax.all_to_all(source, "expert", split_axis=1, concat_axis=0, tiled=True)
    inner_state = inner(arrived)
    partial_value = terms(inner_state, 0, arrived.shape[0])
    returned = lax.all_to_all(
        partial_value.astype(jnp.bfloat16), "expert", split_axis=0, concat_axis=1, tiled=True
    ).astype(partial_value.dtype)
    summed = lax.psum_scatter(
        returned.astype(jnp.bfloat16), "shard", scatter_dimension=0, tiled=True
    )
    return (summed, inner_state, arrived)


def gelu_tanh(values):
    return jax.nn.gelu(values, approximate=True)


def layer_forward(incoming, route_ids, slot_ids, section_weights):
    gains, qkv_weight, out_weight, bias_table, router_weight, inner_weight, outer_weight = (
        section_weights
    )
    residual = incoming.astype(jnp.float32)
    normed = rms_norm(residual, gains[0]).astype(jnp.bfloat16)
    normed_all = lax.all_gather(normed, "shard", axis=0, tiled=True)
    packed = jnp.einsum(
        "nd,kdc->nkc", normed_all, qkv_weight, preferred_element_type=jnp.float32
    ).astype(jnp.bfloat16)
    mixed_heads, log_total = attend(packed, bias_table, LEN)
    attended = lax.psum_scatter(
        jnp.dot(mixed_heads, out_weight, preferred_element_type=jnp.float32).astype(jnp.bfloat16),
        "shard",
        scatter_dimension=0,
        tiled=True,
    ).astype(jnp.float32)
    middle = residual + attended
    normed_two = rms_norm(middle, gains[1]).astype(jnp.bfloat16)
    logits = jnp.dot(normed_two, router_weight, preferred_element_type=jnp.float32)
    router_prob = jax.nn.softmax(logits, axis=-1)
    experts = router_weight.shape[1]
    chosen = (route_ids[:, None] == jnp.arange(experts, dtype=jnp.int32)[None, :]).astype(
        jnp.float32
    )
    gating = jnp.sum(router_prob * chosen, axis=-1)
    capacity = 3 * residual.shape[0] // (2 * experts)
    spread = spread_matrix(route_ids, slot_ids, capacity, experts)
    buffer = jnp.einsum("rs,rd->sd", spread, normed_two, preferred_element_type=jnp.float32)
    buffer = buffer.astype(jnp.bfloat16).reshape(capacity, experts, -1)

    def forward_inner(row_set):
        pre_act = jnp.einsum(
            "ned,edf->nef", row_set, inner_weight, preferred_element_type=jnp.float32
        )
        return (gelu_tanh(pre_act).astype(jnp.bfloat16),)

    def forward_terms(inner_state, offset, amount):
        hidden = inner_state[0]
        return jnp.einsum("nef,efd->ned", hidden, outer_weight, preferred_element_type=jnp.float32)

    returned, _, owner_rows = expert_pass(buffer, forward_inner, forward_terms)
    expert_rows = jnp.dot(
        spread, returned.reshape(capacity * experts, -1), preferred_element_type=jnp.float32
    )
    output = middle + gating[:, None] * expert_rows
    kept_forward = (
        normed_all,
        packed,
        mixed_heads,
        log_total,
        middle,
        normed_two,
        router_prob,
        gating,
        expert_rows,
        owner_rows,
    )
    return (output, kept_forward)


def layer_backward(grad_out, incoming, route_ids, slot_ids, kept_forward, section_weights):
    gains, qkv_weight, out_weight, bias_table, router_weight, inner_weight, outer_weight = (
        section_weights
    )
    (
        normed_all,
        packed,
        mixed_heads,
        log_total,
        middle,
        normed_two,
        router_prob,
        gating,
        expert_rows,
        owner_rows,
    ) = kept_forward
    residual = incoming.astype(jnp.float32)
    experts = router_weight.shape[1]
    capacity = 3 * residual.shape[0] // (2 * experts)
    spread = spread_matrix(route_ids, slot_ids, capacity, experts)
    chosen = (route_ids[:, None] == jnp.arange(experts, dtype=jnp.int32)[None, :]).astype(
        jnp.float32
    )
    grad_expert = (gating[:, None] * grad_out).astype(jnp.bfloat16)
    grad_buffer = jnp.einsum("rs,rd->sd", spread, grad_expert, preferred_element_type=jnp.float32)
    grad_buffer = grad_buffer.astype(jnp.bfloat16).reshape(capacity, experts, -1)

    def backward_inner(grad_rows):
        pre_act = jnp.einsum(
            "ned,edf->nef", owner_rows, inner_weight, preferred_element_type=jnp.float32
        )
        hidden, pull_back = jax.vjp(gelu_tanh, pre_act)
        hidden_low = hidden.astype(jnp.bfloat16)
        outer_grad = jnp.einsum(
            "nef,ned->efd", hidden_low, grad_rows, preferred_element_type=jnp.float32
        )
        hidden_grad = jnp.einsum(
            "ned,efd->nef", grad_rows, outer_weight, preferred_element_type=jnp.float32
        )
        pre_grad = pull_back(hidden_grad)[0].astype(jnp.bfloat16)
        inner_grad = jnp.einsum(
            "ned,nef->edf", owner_rows, pre_grad, preferred_element_type=jnp.float32
        )
        return (pre_grad, inner_grad, outer_grad)

    def backward_terms(inner_state, offset, amount):
        pre_grad = inner_state[0]
        return jnp.einsum(
            "nef,edf->ned", pre_grad, inner_weight, preferred_element_type=jnp.float32
        )

    grad_slots, inner_state, _ = expert_pass(grad_buffer, backward_inner, backward_terms)
    gate_grad = jnp.sum(grad_out * expert_rows, axis=-1)
    logit_grad = ((gate_grad * gating)[:, None] * (chosen - router_prob)).astype(jnp.bfloat16)
    router_grad = jnp.einsum(
        "rd,re->de", normed_two, logit_grad, preferred_element_type=jnp.float32
    )
    normed_two_grad = jnp.einsum(
        "re,de->rd", logit_grad, router_weight, preferred_element_type=jnp.float32
    )
    normed_two_grad = normed_two_grad + jnp.dot(
        spread, grad_slots.reshape(capacity * experts, -1), preferred_element_type=jnp.float32
    )
    _, pull_two = jax.vjp(rms_norm, middle, gains[1])
    middle_part, gain_two = pull_two(normed_two_grad)
    middle_grad = grad_out + middle_part
    grad_all = lax.all_gather(middle_grad.astype(jnp.bfloat16), "shard", axis=0, tiled=True)
    out_grad = jnp.einsum("nc,nd->cd", mixed_heads, grad_all, preferred_element_type=jnp.float32)
    mixed_grad = jnp.einsum(
        "nd,cd->nc", grad_all, out_weight, preferred_element_type=jnp.float32
    ).astype(jnp.bfloat16)
    packed_grad, table_grad = attend_back(packed, log_total, mixed_grad, bias_table, LEN)
    qkv_grad = jnp.einsum(
        "nd,nkc->kdc", normed_all, packed_grad, preferred_element_type=jnp.float32
    )
    normed_grad = lax.psum_scatter(
        jnp.einsum(
            "nkc,kdc->nd", packed_grad, qkv_weight, preferred_element_type=jnp.float32
        ).astype(jnp.bfloat16),
        "shard",
        scatter_dimension=0,
        tiled=True,
    ).astype(jnp.float32)
    _, pull_one = jax.vjp(rms_norm, residual, gains[0])
    residual_part, gain_one = pull_one(normed_grad)
    input_grad = middle_grad + residual_part
    weight_grads = (
        jnp.stack([gain_one, gain_two]),
        qkv_grad,
        out_grad,
        table_grad,
        router_grad,
        inner_state[1],
        inner_state[2],
    )
    return (input_grad, weight_grads)


def across(values):
    return from_partner(values, "section", 0)


def per_device(
    stream, norm_gains, attn_qkv, attn_out, rel_bias, router, expert_in, expert_out, routes, slots
):
    section_weights = (
        norm_gains[0],
        attn_qkv[0],
        attn_out[0],
        rel_bias[0],
        router[0],
        expert_in[0],
        expert_out[0],
    )
    micro_count = stream.shape[1]
    section_number = lax.axis_index("section")
    is_first = section_number == 0
    received = jnp.zeros_like(stream[0, 0])
    saved = []
    produced = []
    for moment in range(micro_count + 1):
        own_rows = stream[0, min(moment, micro_count - 1)]
        incoming = jnp.where(is_first, own_rows, received)
        micro_index = jnp.clip(moment - section_number, 0, micro_count - 1)
        route_ids = lax.dynamic_index_in_dim(routes[0], micro_index, 0, keepdims=False)
        slot_ids = lax.dynamic_index_in_dim(slots[0], micro_index, 0, keepdims=False)
        output, kept_forward = layer_forward(incoming, route_ids, slot_ids, section_weights)
        output = output.astype(jnp.bfloat16)
        saved.append((incoming, route_ids, slot_ids, kept_forward))
        produced.append(output)
        if moment < micro_count:
            received = across(output)
    returned = jnp.zeros_like(stream[0, 0])
    totals = None
    input_grads = []
    for moment in range(micro_count + 1):
        live_flag = jnp.where(is_first, moment >= 1, moment < micro_count).astype(jnp.float32)
        own_rows = stream[0, min(moment, micro_count - 1)].astype(jnp.float32)
        grad_out = jnp.where(is_first, returned.astype(jnp.float32), own_rows) * live_flag
        early_saved = saved[max(moment - 1, 0)]
        late_saved = saved[min(moment + 1, micro_count)]
        picked = jax.tree.map(
            lambda early_part, late_part: jnp.where(is_first, early_part, late_part),
            early_saved,
            late_saved,
        )
        incoming, route_ids, slot_ids, kept_forward = picked
        input_grad, weight_grads = layer_backward(
            grad_out, incoming, route_ids, slot_ids, kept_forward, section_weights
        )
        totals = weight_grads if totals is None else jax.tree.map(jnp.add, totals, weight_grads)
        grad_low = input_grad.astype(jnp.bfloat16)
        if moment >= 1:
            input_grads.append(grad_low)
        if moment < micro_count:
            returned = across(grad_low)
    end_rows = jnp.stack(
        [
            jnp.where(is_first, input_grads[micro], produced[micro + 1])
            for micro in range(micro_count)
        ]
    )[None]
    gain_grad, qkv_grad, out_grad, table_grad, router_grad, inner_grad, outer_grad = totals
    qkv_grad, out_grad, table_grad = (
        lax.psum(qkv_grad.astype(jnp.bfloat16), "expert").astype(jnp.float32),
        lax.psum(out_grad.astype(jnp.bfloat16), "expert").astype(jnp.float32),
        lax.psum(table_grad.astype(jnp.bfloat16), "expert").astype(jnp.float32),
    )
    gain_grad, router_grad = lax.psum((gain_grad, router_grad), ("expert", "shard"))
    return (
        end_rows,
        gain_grad[None],
        qkv_grad[None],
        out_grad[None],
        table_grad[None],
        router_grad[None],
        inner_grad[None],
        outer_grad[None],
    )


def solution(mesh):
    return jax.shard_map(
        per_device,
        mesh=mesh,
        in_specs=(
            P("section", None, ("expert", "shard"), None),
            P("section", None, None),
            P("section", None, None, "shard"),
            P("section", "shard", None),
            P("section", None, "shard"),
            P("section", None, None),
            P("section", "expert", None, "shard"),
            P("section", "expert", "shard", None),
            P("section", None, ("expert", "shard")),
            P("section", None, ("expert", "shard")),
        ),
        out_specs=(
            P("section", None, ("expert", "shard"), None),
            P("section", None, None),
            P("section", None, None, "shard"),
            P("section", "shard", None),
            P("section", None, "shard"),
            P("section", None, None),
            P("section", "expert", None, "shard"),
            P("section", "expert", "shard", None),
        ),
        check_vma=False,
    )
```

profile of v0, /device:TPU:0, one launch (start us, length us, event | category | flops | bytes accessed | tf_op | source)
XLA Modules:
  0.0 1722.5 jit_solution(5124989031140882830)
XLA Ops:
  28.0 13.5 reshape.641
  50.9 13.3 reshape.642
  79.1 30.4 %reduce-scatter.13.cloned.1.call-done = bf16[128,768]{1,0:T(8,128)(2,1)} async-done(((bf16[512,768]{1,0:T(8,128)(2,1)}), bf16[128,768]{1,0:T(8,128)(2,1)}) %reduce-scatter.13.cloned.1.call-update) | async-done | bytes 196624 | tf_op jit(solution)/shard_map/reduce_scatter | solution.py:187
  113.5 21.0 %all-gather.7.cloned.1.call-done = bf16[24,32,768]{2,1,0:T(8,128)(2,1)} async-done(((bf16[6,32,768]{2,1,0:T(8,128)(2,1)}), bf16[24,32,768]{2,1,0:T(8,128)(2,1)}) %all-gather.7.cloned.1.call-update) | async-done | bytes 1179664 | tf_op jit(solution)/shard_map/all_gather | solution.py:159
  136.4 25.9 %all_to_all.216 = bf16[24,32,768]{2,0,1:T(8,128)(2,1)S(1)} all-to-all(bf16[24,32,768]{2,0,1:T(8,128)(2,1)S(1)} %copy.170), channel_id=1, replica_groups=mesh['section'=2,'expert'=16,'shard'=4] {'expert'}, dimensions={1} | all-to-all | bytes 2359296 | tf_op jit(solution)/shard_map/all_to_all | solution.py:160
  170.0 21.0 %all_to_all.217 = bf16[384,2,768]{2,1,0:T(2,128)(2,1)S(1)} all-to-all(bf16[384,2,768]{2,1,0:T(2,128)(2,1)S(1)} %copy.172), channel_id=1, replica_groups=mesh['section'=2,'expert'=16,'shard'=4] {'expert'}, dimensions={0} | all-to-all | bytes 2359296 | tf_op jit(solution)/shard_map/all_to_all | solution.py:163
  193.0 28.5 %reduce-scatter.15.cloned.1.call-done = bf16[6,32,768]{2,1,0:T(8,128)(2,1)} async-done(((bf16[24,32,768]{2,1,0:T(8,128)(2,1)}), bf16[6,32,768]{2,1,0:T(8,128)(2,1)}) %reduce-scatter.15.cloned.1.call-update) | async-done | bytes 294928 | tf_op jit(solution)/shard_map/reduce_scatter | solution.py:166
  248.6 30.4 %reduce-scatter.17.cloned.1.call-done = bf16[128,768]{1,0:T(8,128)(2,1)} async-done(((bf16[512,768]{1,0:T(8,128)(2,1)}), bf16[128,768]{1,0:T(8,128)(2,1)}) %reduce-scatter.17.cloned.1.call-update) | async-done | bytes 196624 | tf_op jit(solution)/shard_map/reduce_scatter | solution.py:187
  282.9 21.0 %all-gather.9.cloned.1.call-done = bf16[24,32,768]{2,1,0:T(8,128)(2,1)} async-done(((bf16[6,32,768]{2,1,0:T(8,128)(2,1)}), bf16[24,32,768]{2,1,0:T(8,128)(2,1)}) %all-gather.9.cloned.1.call-update) | async-done | bytes 1179664 | tf_op jit(solution)/shard_map/all_gather | solution.py:159
  305.9 25.7 %all_to_all.218 = bf16[24,32,768]{2,0,1:T(8,128)(2,1)S(1)} all-to-all(bf16[24,32,768]{2,0,1:T(8,128)(2,1)S(1)} %copy.177), channel_id=1, replica_groups=mesh['section'=2,'expert'=16,'shard'=4] {'expert'}, dimensions={1} | all-to-all | bytes 2359296 | tf_op jit(solution)/shard_map/all_to_all | solution.py:160
  338.8 21.0 %all_to_all.219 = bf16[384,2,768]{2,1,0:T(2,128)(2,1)S(1)} all-to-all(bf16[384,2,768]{2,1,0:T(2,128)(2,1)S(1)} %copy.179), channel_id=1, replica_groups=mesh['section'=2,'expert'=16,'shard'=4] {'expert'}, dimensions={0} | all-to-all | bytes 2359296 | tf_op jit(solution)/shard_map/all_to_all | solution.py:163
  364.9 25.3 %reduce-scatter.19.cloned.1.call-done = bf16[6,32,768]{2,1,0:T(8,128)(2,1)} async-done(((bf16[24,32,768]{2,1,0:T(8,128)(2,1)}), bf16[6,32,768]{2,1,0:T(8,128)(2,1)}) %reduce-scatter.19.cloned.1.call-update) | async-done | bytes 294928 | tf_op jit(solution)/shard_map/reduce_scatter | solution.py:166
  418.9 30.3 %reduce-scatter.25.cloned.1.call-done = bf16[128,768]{1,0:T(8,128)(2,1)} async-done(((bf16[512,768]{1,0:T(8,128)(2,1)}), bf16[128,768]{1,0:T(8,128)(2,1)}) %reduce-scatter.25.cloned.1.call-update) | async-done | bytes 196624 | tf_op jit(solution)/shard_map/reduce_scatter | solution.py:187
  454.3 21.1 %all-gather.11.cloned.1.call-done = bf16[24,32,768]{2,1,0:T(8,128)(2,1)} async-done(((bf16[6,32,768]{2,1,0:T(8,128)(2,1)}), bf16[24,32,768]{2,1,0:T(8,128)(2,1)}) %all-gather.11.cloned.1.call-update) | async-done | bytes 1179664 | tf_op jit(solution)/shard_map/all_gather | solution.py:159
  489.4 15.7 all-to-all-done.4
  513.3 20.7 %all_to_all.220 = bf16[384,2,768]{2,1,0:T(2,128)(2,1)S(1)} all-to-all(bf16[384,2,768]{2,1,0:T(2,128)(2,1)S(1)} %copy.185), channel_id=1, replica_groups=mesh['section'=2,'expert'=16,'shard'=4] {'expert'}, dimensions={0} | all-to-all | bytes 2359296 | tf_op jit(solution)/shard_map/all_to_all | solution.py:163
  539.7 24.7 %reduce-scatter.21.cloned.1.call-done = bf16[6,32,768]{2,1,0:T(8,128)(2,1)} async-done(((bf16[24,32,768]{2,1,0:T(8,128)(2,1)}), bf16[6,32,768]{2,1,0:T(8,128)(2,1)}) %reduce-scatter.21.cloned.1.call-update) | async-done | bytes 294928 | tf_op jit(solution)/shard_map/reduce_scatter | solution.py:166
  631.9 20.8 %all_to_all.221 = bf16[384,2,768]{2,1,0:T(2,128)(2,1)S(1)} all-to-all(bf16[384,2,768]{2,1,0:T(2,128)(2,1)S(1)} %copy.195), channel_id=1, replica_groups=mesh['section'=2,'expert'=16,'shard'=4] {'expert'}, dimensions={0} | all-to-all | bytes 2359296 | tf_op jit(solution)/shard_map/all_to_all | solution.py:163
  667.3 15.8 reduce-scatter.27.cloned.1.call-done
  688.7 20.9 %all-gather.15.cloned.1.call-done = bf16[24,32,768]{2,1,0:T(8,128)(2,1)} async-done(((bf16[6,32,768]{2,1,0:T(8,128)(2,1)}), bf16[24,32,768]{2,1,0:T(8,128)(2,1)}) %all-gather.15.cloned.1.call-update) | async-done | bytes 1179664 | tf_op jit(solution)/shard_map/all_gather | solution.py:159
  723.3 15.9 all-to-all-done.8
  747.5 20.7 %all_to_all.222 = bf16[384,2,768]{2,1,0:T(2,128)(2,1)S(1)} all-to-all(bf16[384,2,768]{2,1,0:T(2,128)(2,1)S(1)} %copy.201), channel_id=1, replica_groups=mesh['section'=2,'expert'=16,'shard'=4] {'expert'}, dimensions={0} | all-to-all | bytes 2359296 | tf_op jit(solution)/shard_map/all_to_all | solution.py:163
  775.2 23.4 %reduce-scatter.29.cloned.1.call-done = bf16[6,32,768]{2,1,0:T(8,128)(2,1)} async-done(((bf16[24,32,768]{2,1,0:T(8,128)(2,1)}), bf16[6,32,768]{2,1,0:T(8,128)(2,1)}) %reduce-scatter.29.cloned.1.call-update) | async-done | bytes 294928 | tf_op jit(solution)/shard_map/reduce_scatter | solution.py:166
  822.6 28.6 %reduce-scatter.31.cloned.1.call-done = bf16[128,768]{1,0:T(8,128)(2,1)} async-done(((bf16[512,768]{1,0:T(8,128)(2,1)}), bf16[128,768]{1,0:T(8,128)(2,1)}) %reduce-scatter.31.cloned.1.call-update) | async-done | bytes 196624 | tf_op jit(solution)/shard_map/reduce_scatter | solution.py:312
  867.4 21.1 %all-gather.17.cloned.1.call-done = bf16[24,32,768]{2,1,0:T(8,128)(2,1)} async-done(((bf16[6,32,768]{2,1,0:T(8,128)(2,1)}), bf16[24,32,768]{2,1,0:T(8,128)(2,1)}) %all-gather.17.cloned.1.call-update) | async-done | bytes 1179664 | tf_op jit(solution)/shard_map/all_gather | solution.py:159
  904.4 14.0 all-to-all-done.10
  972.8 13.6 reshape.677
  1066.0 13.3 reshape.679
  1130.9 13.2 reshape.681
  1147.8 40.6 %psum.38 = bf16[1,32,3]{1,2,0:T(4,128)(2,1)S(1)} all-reduce(bf16[1,32,3]{1,2,0:T(4,128)(2,1)S(1)} %fusion.187), channel_id=1, replica_groups=mesh['section'=2,'expert'=16,'shard'=4] {'expert'}, use_global_device_ids=true, to_apply=%region_63.64 | all-reduce | flops 96 | bytes 384 | tf_op jit(solution)/shard_map/psum | solution.py:403
  1195.5 165.2 %psum.35 = f32[1,2,768]{2,1,0:T(2,128)} all-reduce(f32[1,2,768]{2,1,0:T(2,128)S(1)} %fusion.322), channel_id=1, replica_groups=mesh['section'=2,'expert'=16,'shard'=4] {'expert','shard'}, use_global_device_ids=true, to_apply=%region_57.58 | all-reduce | flops 1536 | bytes 12288 | tf_op jit(solution)/shard_map/psum | solution.py:405
  1363.5 350.2 %all-reduce.10.cloned.1.call-done = f32[1,768,32]{1,2,0:T(8,128)} async-done(((f32[1,768,32]{1,2,0:T(8,128)}), f32[1,768,32]{1,2,0:T(8,128)}) %all-reduce.10.cloned.1.call-update) | async-done | bytes 98320 | tf_op jit(solution)/shard_map/psum | solution.py:405
  (621 shorter events, 539.0 us)
Async XLA Ops:
  7.2 102.3 %reduce-scatter.13.cloned.1.call-start = ((), (), s32[]{:S(2)}) async-start(), calls=%async_computation.24 | async-start | bytes 983040 | tf_op jit(solution)/shard_map/reduce_scatter | solution.py:187
  77.3 57.2 %all-gather.7.cloned.1.call-start = ((), (), s32[]{:S(2)}) async-start(), calls=%async_computation.25 | async-start | bytes 1474560 | tf_op jit(solution)/shard_map/all_gather | solution.py:159
  113.4 108.1 %reduce-scatter.15.cloned.1.call-start = ((), (), s32[]{:S(2)}) async-start(), calls=%async_computation.26 | async-start | bytes 1474560 | tf_op jit(solution)/shard_map/reduce_scatter | solution.py:166
  192.6 86.3 %reduce-scatter.17.cloned.1.call-start = ((), (), s32[]{:S(2)}) async-start(), calls=%async_computation.27 | async-start | bytes 983040 | tf_op jit(solution)/shard_map/reduce_scatter | solution.py:187
  223.6 6.6 collective-permute-start
  248.5 55.4 %all-gather.9.cloned.1.call-start = ((), (), s32[]{:S(2)}) async-start(), calls=%async_computation.28 | async-start | bytes 1474560 | tf_op jit(solution)/shard_map/all_gather | solution.py:159
  282.9 107.3 %reduce-scatter.19.cloned.1.call-start = ((), (), s32[]{:S(2)}) async-start(), calls=%async_computation.29 | async-start | bytes 1474560 | tf_op jit(solution)/shard_map/reduce_scatter | solution.py:166
  361.3 88.0 %reduce-scatter.25.cloned.1.call-start = ((), (), s32[]{:S(2)}) async-start(), calls=%async_computation.33 | async-start | bytes 983040 | tf_op jit(solution)/shard_map/reduce_scatter | solution.py:187
  392.4 6.6 collective-permute-start.2
  418.9 56.5 %all-gather.11.cloned.1.call-start = ((), (), s32[]{:S(2)}) async-start(), calls=%async_computation.30 | async-start | bytes 1474560 | tf_op jit(solution)/shard_map/all_gather | solution.py:159
  478.3 26.8 %all-to-all-start.4 = ((bf16[24,32,768]{2,0,1:T(8,128)(2,1)}), bf16[24,32,768]{2,0,1:T(8,128)(2,1)}, u32[]{:S(2)}, u32[]{:S(2)}) async-start(bf16[24,32,768]{2,0,1:T(8,128)(2,1)} %copy.183), calls=%async_computation.8 | async-start | bytes 2359296 | tf_op jit(solution)/shard_map/all_to_all | solution.py:160
  485.3 79.1 %reduce-scatter.21.cloned.1.call-start = ((), (), s32[]{:S(2)}) async-start(), calls=%async_computation.31 | async-start | bytes 1474560 | tf_op jit(solution)/shard_map/reduce_scatter | solution.py:166
  535.5 56.7 %all-gather.13.cloned.1.call-start = ((), (), s32[]{:S(2)}) async-start(), calls=%async_computation.34 | async-start | bytes 1474560 | tf_op jit(solution)/shard_map/all_gather | solution.py:159
  595.2 26.8 %all-to-all-start.6 = ((bf16[24,32,768]{2,0,1:T(8,128)(2,1)}), bf16[24,32,768]{2,0,1:T(8,128)(2,1)}, u32[]{:S(2)}, u32[]{:S(2)}) async-start(bf16[24,32,768]{2,0,1:T(8,128)(2,1)} %copy.193), calls=%async_computation.13 | async-start | bytes 2359296 | tf_op jit(solution)/shard_map/all_to_all | solution.py:160
  602.2 55.4 %reduce-scatter.23.cloned.1.call-start = ((), (), s32[]{:S(2)}) async-start(), calls=%async_computation.32 | async-start | bytes 983040 | tf_op jit(solution)/shard_map/reduce_scatter | solution.py:312
  609.6 73.5 %reduce-scatter.27.cloned.1.call-start = ((), (), s32[]{:S(2)}) async-start(), calls=%async_computation.35 | async-start | bytes 1474560 | tf_op jit(solution)/shard_map/reduce_scatter | solution.py:166
  654.2 55.3 %all-gather.15.cloned.1.call-start = ((), (), s32[]{:S(2)}) async-start(), calls=%async_computation.36 | async-start | bytes 1474560 | tf_op jit(solution)/shard_map/all_gather | solution.py:159
  661.4 5.9 collective-permute-start.1
  712.5 26.8 %all-to-all-start.8 = ((bf16[24,32,768]{2,0,1:T(8,128)(2,1)}), bf16[24,32,768]{2,0,1:T(8,128)(2,1)}, u32[]{:S(2)}, u32[]{:S(2)}) async-start(bf16[24,32,768]{2,0,1:T(8,128)(2,1)} %copy.199), calls=%async_computation.16 | async-start | bytes 2359296 | tf_op jit(solution)/shard_map/all_to_all | solution.py:160
  719.5 79.0 %reduce-scatter.29.cloned.1.call-start = ((), (), s32[]{:S(2)}) async-start(), calls=%async_computation.37 | async-start | bytes 1474560 | tf_op jit(solution)/shard_map/reduce_scatter | solution.py:166
  769.7 81.5 %reduce-scatter.31.cloned.1.call-start = ((), (), s32[]{:S(2)}) async-start(), calls=%async_computation.38 | async-start | bytes 983040 | tf_op jit(solution)/shard_map/reduce_scatter | solution.py:312
  821.4 67.0 %all-gather.17.cloned.1.call-start = ((), (), s32[]{:S(2)}) async-start(), calls=%async_computation.39 | async-start | bytes 1474560 | tf_op jit(solution)/shard_map/all_gather | solution.py:159
  855.7 6.9 collective-permute-start.3
  891.4 27.0 %all-to-all-start.10 = ((bf16[24,32,768]{2,0,1:T(8,128)(2,1)}), bf16[24,32,768]{2,0,1:T(8,128)(2,1)}, u32[]{:S(2)}, u32[]{:S(2)}) async-start(bf16[24,32,768]{2,0,1:T(8,128)(2,1)} %copy.208), calls=%async_computation.20 | async-start | bytes 2359296 | tf_op jit(solution)/shard_map/all_to_all | solution.py:160
  927.7 34.8 %all-to-all-start.11 = ((bf16[384,2,768]{2,1,0:T(2,128)(2,1)}), bf16[384,2,768]{2,1,0:T(2,128)(2,1)}, u32[]{:S(2)}, u32[]{:S(2)}) async-start(bf16[384,2,768]{2,1,0:T(2,128)(2,1)} %copy.210), calls=%async_computation.21 | async-start | bytes 2359296 | tf_op jit(solution)/shard_map/all_to_all | solution.py:163
  932.1 70.9 %reduce-scatter.33.cloned.1.call-start = ((), (), s32[]{:S(2)}) async-start(), calls=%async_computation.40 | async-start | bytes 1474560 | tf_op jit(solution)/shard_map/reduce_scatter | solution.py:166
  965.2 224.4 %all-reduce.12.cloned.1.call-start = ((), (), s32[]{:S(2)}) async-start(), calls=%async_computation.43 | async-start | bytes 2359296 | tf_op jit(solution)/shard_map/psum | solution.py:401
  1026.2 166.8 %reduce-scatter.35.cloned.1.call-start = ((), (), s32[]{:S(2)}) async-start(), calls=%async_computation.41 | async-start | bytes 983040 | tf_op jit(solution)/shard_map/reduce_scatter | solution.py:312
  1058.7 655.0 %all-reduce.10.cloned.1.call-start = ((), (), s32[]{:S(2)}) async-start(), calls=%async_computation.42 | async-start | bytes 196608 | tf_op jit(solution)/shard_map/psum | solution.py:405
  1147.4 214.0 %copy-start.42 = (bf16[128,768]{1,0:T(8,128)(2,1)S(1)}, bf16[128,768]{1,0:T(8,128)(2,1)}, u32[]{:S(2)}) copy-start(bf16[128,768]{1,0:T(8,128)(2,1)} %copy-done.41) | copy-start | bytes 589828
  1147.4 213.9 %copy-start.53 = (f32[128,768]{1,0:T(8,128)S(1)}, f32[128,768]{1,0:T(8,128)}, u32[]{:S(2)}) copy-start(f32[128,768]{1,0:T(8,128)} %get-tuple-element.319) | copy-start | bytes 1179652
  1147.4 213.9 %copy-start.73 = (bf16[128,768]{1,0:T(8,128)(2,1)S(1)}, bf16[128,768]{1,0:T(8,128)(2,1)}, u32[]{:S(2)}) copy-start(bf16[128,768]{1,0:T(8,128)(2,1)} %reduce-scatter.25.cloned.1.call-done) | copy-start | bytes 589828
  (160 other events, 1830.5 us)
Sparse Core Ops, SparseCore 0:
  77.5 32.0 reduce-scatter.12
  113.5 20.9 all-gather.6
  192.8 28.6 reduce-scatter.14
  248.7 30.2 reduce-scatter.16
  283.0 20.9 all-gather.8
  361.4 28.6 reduce-scatter.18
  419.0 30.2 reduce-scatter.24
  454.4 20.9 all-gather.10
  535.7 28.6 reduce-scatter.20
  571.3 20.9 all-gather.12
  609.8 29.8 reduce-scatter.22
  654.3 28.7 reduce-scatter.26
  688.8 20.7 all-gather.14
  769.8 28.6 reduce-scatter.28
  821.5 29.6 reduce-scatter.30
  867.5 20.9 all-gather.16
  965.4 32.1 reduce-scatter.32
  1026.3 87.4 all-reduce.11
  1116.7 29.3 reduce-scatter.34
  1148.9 564.7 all-reduce.9
where the time goes:
time: 1730 us; the launch traced here: 1720 us
  waiting for transfers between devices  775 us (45%)
  blocking collectives  419 us (24%)
  local copies, waits for them, and re-layouts  217 us (13%)
  matrix products  160 us (9%)
  other arithmetic  98.3 us (6%)
  starting transfers between devices  37.3 us (2%)
    psum x1, waiting for transfers between devices, per_device(): lax.psum((gain_grad, router_grad), ('expert', 'shard'))  350 us
    psum x1, blocking collectives, per_device(): lax.psum((gain_grad, router_grad), ('expert', 'shard'))  165 us
    reduce_scatter x6, waiting for transfers between devices, expert_pass(): lax.psum_scatter(returned.astype(jnp.bfloat16), 'shard', scatter_dimensio...  118 us
    all_gather x6, waiting for transfers between devices, expert_pass(): source = lax.all_gather(buffer, 'shard', axis=0, tiled=True)  109 us
    all_to_all x5, blocking collectives, expert_pass(): lax.all_to_all(partial_value.astype(jnp.bfloat16), 'expert', split_axis=0...  104 us
    reduce_scatter x3, waiting for transfers between devices, layer_forward(): lax.psum_scatter(jnp.dot(mixed_heads, out_weight, preferred_element_type=...  91.1 us
    all_to_all x4, waiting for transfers between devices, expert_pass(): lax.all_to_all(source, 'expert', split_axis=1, concat_axis=0, tiled=True)  57.6 us
    reshape x4, local copies, waits for them, and re-layouts, bias_block(): jnp.broadcast_to(by_offset[:, None, :], (head_count, row_count, span_width))  53.5 us
  transfers between devices with their start and end apart: 29, of which 24 were waited for; matrix products, arithmetic and copies ran while one was open for 15% of the time, Pallas kernels for 0%

commit v1 on v0

v1 whole, which is shorter than its diff:
```python
import functools

import jax
import jax.numpy as jnp
import numpy as np
from jax import lax
from jax.experimental import pallas as pl
from jax.experimental.pallas import tpu as pltpu
from jax.sharding import PartitionSpec as P

HEAD_DIM = 64
HEADS_HERE = 3
LEN = 512
MICRO = 2
ROWS = 128
D = 768
HALF = 384
EXPERTS = 32
CAP = 6
OWNERS = 16
PIECE = 48
VMEM_BYTES = 48 * 1024 * 1024
MESH = pl.DeviceIdType.MESH
ANY = pl.BlockSpec(memory_space=pl.ANY)
VMEM = pl.BlockSpec(memory_space=pltpu.VMEM)


def remote(src, dst, send, recv, axis, index):
    return pltpu.make_async_remote_copy(
        src_ref=src, dst_ref=dst, send_sem=send, recv_sem=recv, device_id={axis: index}, device_id_type=MESH
    )


def greet(partners):
    barrier = pltpu.get_barrier_semaphore()
    for axis, index in partners:
        pl.semaphore_signal(barrier, inc=1, device_id={axis: index}, device_id_type=MESH)
    pl.semaphore_wait(barrier, len(partners))


def shard_places():
    me = lax.axis_index("shard")
    y, core = lax.div(me, 2), lax.rem(me, 2)
    return me, 2 * y + (1 - core), 2 * (1 - y) + core, 2 * (1 - y) + (1 - core)


def expert_places():
    me = lax.axis_index("expert")
    return me, lax.div(me, 4), lax.rem(me, 4)


def owner_at(x, z, dx, dz):
    return lax.rem(x + dx, 4) * 4 + lax.rem(z + dz, 4)


def all_owners(x, z):
    return [("expert", owner_at(x, z, dx, dz)) for dx in range(4) for dz in range(4) if dx or dz]


def when_active(active, old, out, sem, run):
    mine = lax.axis_index("section") == active

    @pl.when(mine)
    def _():
        run()

    if old is not None:

        @pl.when(jnp.logical_not(mine))
        def _():
            keep = pltpu.make_async_copy(old, out, sem)
            keep.start()
            keep.wait()


def gather_kernel(active, kept, x, *refs):
    old = refs[0] if kept else None
    out, local, send, recv = refs[-4:]

    def run():
        me, core, cross, diag = shard_places()
        greet([("shard", core), ("shard", cross)])
        far, near, own, on = [], [], [], []
        for m in range(MICRO):
            far.append(remote(x.at[m], out.at[m, me], send.at[m], recv.at[m], "shard", cross))
            far[m].start()
        for m in range(MICRO):
            near.append(remote(x.at[m], out.at[m, me], send.at[2 + m], recv.at[2 + m], "shard", core))
            near[m].start()
            own.append(pltpu.make_async_copy(x.at[m], out.at[m, me], local.at[m]))
            own[m].start()
        for m in range(MICRO):
            far[m].wait_recv()
            on.append(remote(out.at[m, cross], out.at[m, cross], send.at[4 + m], recv.at[4 + m], "shard", core))
            on[m].start()
        for m in range(MICRO):
            own[m].wait()
            far[m].wait_send()
            near[m].wait()
            on[m].wait()

    when_active(active, old, out, local.at[0], run)


def gather_rows(x, old, active, collective_id):
    return pl.pallas_call(
        functools.partial(gather_kernel, active, old is not None),
        out_shape=jax.ShapeDtypeStruct((MICRO, 4, ROWS, D), jnp.bfloat16),
        in_specs=[ANY] * (1 if old is None else 2),
        out_specs=ANY,
        scratch_shapes=[
            pltpu.SemaphoreType.DMA((2,)),
            pltpu.SemaphoreType.DMA((6,)),
            pltpu.SemaphoreType.DMA((6,)),
        ],
        compiler_params=pltpu.CompilerParams(
            collective_id=collective_id, has_side_effects=True, vmem_limit_bytes=VMEM_BYTES
        ),
        name="gather_rows",
    )(*([x] if old is None else [x, old]))


def scatter_kernel(active, kept, part, *refs):
    old = refs[0] if kept else None
    out, pair, mine, theirs, crossed, local, send, recv = refs[-8:]

    def run():
        me, core, cross, diag = shard_places()
        greet([("shard", core), ("shard", cross)])
        first, second, third = [], [], []
        for m in range(MICRO):
            first.append(remote(part.at[m, diag], theirs.at[m], send.at[m], recv.at[m], "shard", core))
            first[m].start()
        for m in range(MICRO):
            second.append(remote(part.at[m, core], mine.at[m], send.at[2 + m], recv.at[2 + m], "shard", core))
            second[m].start()
        for m in range(MICRO):
            first[m].wait_recv()
            pair[m] = (part[m, cross].astype(jnp.float32) + theirs[m].astype(jnp.float32)).astype(jnp.bfloat16)
            third.append(remote(pair.at[m], crossed.at[m], send.at[4 + m], recv.at[4 + m], "shard", cross))
            third[m].start()
        for m in range(MICRO):
            second[m].wait_recv()
            third[m].wait_recv()
            out[m] = (
                part[m, me].astype(jnp.float32) + mine[m].astype(jnp.float32) + crossed[m].astype(jnp.float32)
            )
        for m in range(MICRO):
            first[m].wait_send()
            second[m].wait_send()
            third[m].wait_send()

    when_active(active, old, out, local, run)


def scatter_rows(part, old, active, collective_id):
    return pl.pallas_call(
        functools.partial(scatter_kernel, active, old is not None),
        out_shape=jax.ShapeDtypeStruct((MICRO, ROWS, D), jnp.float32),
        in_specs=[VMEM] + ([] if old is None else [ANY]),
        out_specs=VMEM,
        scratch_shapes=[pltpu.VMEM((MICRO, ROWS, D), jnp.bfloat16)] * 4
        + [
            pltpu.SemaphoreType.DMA,
            pltpu.SemaphoreType.DMA((6,)),
            pltpu.SemaphoreType.DMA((6,)),
        ],
        compiler_params=pltpu.CompilerParams(
            collective_id=collective_id, has_side_effects=True, vmem_limit_bytes=VMEM_BYTES
        ),
        name="scatter_rows",
    )(*([part] if old is None else [part, old]))


def dispatch_kernel(active, kept, x, *refs):
    old = refs[0] if kept else None
    out, local, send_x, recv_x, send_y, recv_y = refs[-6:]

    def run():
        me, core, cross, diag = shard_places()
        here, px, pz = expert_places()
        greet([("shard", core), ("shard", cross)] + all_owners(px, pz))
        away = {}
        for dx in range(4):
            for dz in range(4):
                if dx or dz:
                    goal = owner_at(px, pz, dx, dz)
                    at = dx * 4 + dz
                    away[at] = remote(x.at[goal], out.at[me, here], send_x.at[at], recv_x.at[at], "expert", goal)
                    away[at].start()
        own = pltpu.make_async_copy(x.at[here], out.at[me, here], local)
        own.start()
        far, near, on = [], [], []
        for dx in range(4):
            if dx == 0:
                own.wait()
            for dz in range(4):
                if dx or dz:
                    away[dx * 4 + dz].wait_recv()
            rows = pl.ds(lax.rem(px + 4 - dx, 4) * 4, 4)
            block = out.at[me, rows]
            far.append(remote(block, block, send_y.at[dx], recv_y.at[dx], "shard", cross))
            far[dx].start()
            near.append(remote(block, block, send_y.at[4 + dx], recv_y.at[4 + dx], "shard", core))
            near[dx].start()
        for dx in range(4):
            far[dx].wait_recv()
            rows = pl.ds(lax.rem(px + 4 - dx, 4) * 4, 4)
            block = out.at[cross, rows]
            on.append(remote(block, block, send_y.at[8 + dx], recv_y.at[8 + dx], "shard", core))
            on[dx].start()
        for dx in range(4):
            far[dx].wait_send()
            near[dx].wait()
            on[dx].wait()
        for at in away:
            away[at].wait_send()

    when_active(active, old, out, local, run)


def dispatch(x, old, active, collective_id):
    return pl.pallas_call(
        functools.partial(dispatch_kernel, active, old is not None),
        out_shape=jax.ShapeDtypeStruct((4, OWNERS, PIECE, HALF), jnp.bfloat16),
        in_specs=[ANY] * (1 if old is None else 2),
        out_specs=ANY,
        scratch_shapes=[
            pltpu.SemaphoreType.DMA,
            pltpu.SemaphoreType.DMA((16,)),
            pltpu.SemaphoreType.DMA((16,)),
            pltpu.SemaphoreType.DMA((12,)),
            pltpu.SemaphoreType.DMA((12,)),
        ],
        compiler_params=pltpu.CompilerParams(
            collective_id=collective_id, has_side_effects=True, vmem_limit_bytes=VMEM_BYTES
        ),
        name="dispatch",
    )(*([x] if old is None else [x, old]))


def combine_kernel(active, kept, part, *refs):
    old = refs[0] if kept else None
    out, pair, mine, theirs, crossed, total, local, send_x, recv_x, send_y, recv_y = refs[-11:]

    def run():
        me, core, cross, diag = shard_places()
        here, px, pz = expert_places()
        greet([("shard", core), ("shard", cross)] + all_owners(px, pz))
        first, second, third, away = [], [], [], {}

        def rows(dx):
            return pl.ds(lax.rem(px + dx, 4) * 4, 4)

        order = (1, 2, 3, 0)
        for n, dx in enumerate(order):
            first.append(remote(part.at[diag, rows(dx)], theirs.at[n], send_y.at[n], recv_y.at[n], "shard", core))
            first[n].start()
            second.append(
                remote(part.at[core, rows(dx)], mine.at[n], send_y.at[4 + n], recv_y.at[4 + n], "shard", core)
            )
            second[n].start()
        for n, dx in enumerate(order):
            first[n].wait_recv()
            pair[n] = (part[cross, rows(dx)].astype(jnp.float32) + theirs[n].astype(jnp.float32)).astype(jnp.bfloat16)
            third.append(remote(pair.at[n], crossed.at[n], send_y.at[8 + n], recv_y.at[8 + n], "shard", cross))
            third[n].start()
        for n, dx in enumerate(order):
            second[n].wait_recv()
            third[n].wait_recv()
            total[n] = (
                part[me, rows(dx)].astype(jnp.float32) + mine[n].astype(jnp.float32) + crossed[n].astype(jnp.float32)
            ).astype(jnp.bfloat16)
            for dz in range(4):
                goal = owner_at(px, pz, dx, dz)
                source = total.at[n, lax.rem(pz + dz, 4)]
                at = dx * 4 + dz
                if at:
                    away[at] = remote(source, out.at[here], send_x.at[at], recv_x.at[at], "expert", goal)
                else:
                    away[at] = pltpu.make_async_copy(source, out.at[here], local)
                away[at].start()
        for n in range(4):
            first[n].wait_send()
            second[n].wait_send()
            third[n].wait_send()
        for at in away:
            away[at].wait()

    when_active(active, old, out, local, run)


def combine(part, old, active, collective_id):
    return pl.pallas_call(
        functools.partial(combine_kernel, active, old is not None),
        out_shape=jax.ShapeDtypeStruct((OWNERS, PIECE, HALF), jnp.bfloat16),
        in_specs=[VMEM] + ([] if old is None else [ANY]),
        out_specs=ANY,
        scratch_shapes=[pltpu.VMEM((4, 4, PIECE, HALF), jnp.bfloat16)] * 5
        + [
            pltpu.SemaphoreType.DMA,
            pltpu.SemaphoreType.DMA((16,)),
            pltpu.SemaphoreType.DMA((16,)),
            pltpu.SemaphoreType.DMA((12,)),
            pltpu.SemaphoreType.DMA((12,)),
        ],
        compiler_params=pltpu.CompilerParams(
            collective_id=collective_id, has_side_effects=True, vmem_limit_bytes=VMEM_BYTES
        ),
        name="combine",
    )(*([part] if old is None else [part, old]))


def reduce_kernel(big, small, table, big_out, small_out, table_out, *refs):
    big_in, big_sum, pair, small_have, small_in, small_sum, table_in, local, sends, recvs, pair_send, pair_recv = refs
    me, core, cross, diag = shard_places()
    here, px, pz = expert_places()
    greet([("shard", core), ("shard", cross)] + all_owners(px, pz))
    others = [(dx * 4 + dz, owner_at(px, pz, dx, dz)) for dx in range(4) for dz in range(4) if dx or dz]
    first = []
    for at, goal in others:
        first.append(remote(big.at[goal], big_in.at[here], sends.at[0, at], recvs.at[0, at], "expert", goal))
        first[-1].start()
        first.append(remote(table, table_in.at[here], sends.at[1, at], recvs.at[1, at], "expert", goal))
        first[-1].start()
    table_in[here] = table[...]
    near = remote(small, pair.at[0], pair_send.at[0], pair_recv.at[0], "shard", core)
    near.start()
    near.wait()
    small_have[...] = small[...] + pair[0]
    far = remote(small_have, pair.at[1], pair_send.at[1], pair_recv.at[1], "shard", cross)
    far.start()
    far.wait()
    small_have[...] = small_have[...] + pair[1]
    second = []
    for at, goal in others:
        second.append(
            remote(small_have.at[goal], small_in.at[here], sends.at[2, at], recvs.at[2, at], "expert", goal)
        )
        second[-1].start()
    small_in[here] = small_have[here]
    big_in[here] = big[here]
    for copy in first:
        copy.wait()
    big_sum[...] = jnp.sum(big_in[...].astype(jnp.float32), axis=0).astype(jnp.bfloat16)
    third = []
    for at, goal in others:
        third.append(remote(big_sum, big_out.at[here], sends.at[3, at], recvs.at[3, at], "expert", goal))
        third[-1].start()
    own = pltpu.make_async_copy(big_sum, big_out.at[here], local.at[0])
    own.start()
    for copy in second:
        copy.wait()
    small_sum[...] = jnp.sum(small_in[...], axis=0)
    for at, goal in others:
        third.append(remote(small_sum, small_out.at[here], sends.at[4, at], recvs.at[4, at], "expert", goal))
        third[-1].start()
    own_small = pltpu.make_async_copy(small_sum, small_out.at[here], local.at[1])
    own_small.start()
    table_out[...] = jnp.sum(table_in[...], axis=0)
    own.wait()
    own_small.wait()
    for copy in third:
        copy.wait()


def reduce_all(big, small, table, collective_id):
    return pl.pallas_call(
        reduce_kernel,
        out_shape=(
            jax.ShapeDtypeStruct(big.shape, big.dtype),
            jax.ShapeDtypeStruct(small.shape, small.dtype),
            jax.ShapeDtypeStruct(table.shape, table.dtype),
        ),
        in_specs=[VMEM] * 3,
        out_specs=(ANY, ANY, VMEM),
        scratch_shapes=[
            pltpu.VMEM(big.shape, big.dtype),
            pltpu.VMEM(big.shape[1:], big.dtype),
            pltpu.VMEM((2,) + small.shape, small.dtype),
            pltpu.VMEM(small.shape, small.dtype),
            pltpu.VMEM(small.shape, small.dtype),
            pltpu.VMEM(small.shape[1:], small.dtype),
            pltpu.VMEM((OWNERS,) + table.shape, table.dtype),
            pltpu.SemaphoreType.DMA((2,)),
            pltpu.SemaphoreType.DMA((5, 16)),
            pltpu.SemaphoreType.DMA((5, 16)),
            pltpu.SemaphoreType.DMA((2,)),
            pltpu.SemaphoreType.DMA((2,)),
        ],
        compiler_params=pltpu.CompilerParams(
            collective_id=collective_id, has_side_effects=True, vmem_limit_bytes=VMEM_BYTES
        ),
        name="reduce_all",
    )(big, small, table)


def dot(a, b, dims=((1,), (0,))):
    return lax.dot_general(a, b, (dims, ((), ())), preferred_element_type=jnp.float32)


NT = ((1,), (1,))
TN = ((0,), (0,))


def fill_bias(by_offset, bias):
    for head in range(HEADS_HERE):
        spread = jnp.broadcast_to(by_offset[pl.ds(head, 1), :], (LEN, 2 * LEN))
        bias[head] = pltpu.roll(spread, LEN + 1, 1, stride=1, stride_axis=0)[:, :LEN]


def head_of(array, head):
    return array[:, head * HEAD_DIM : (head + 1) * HEAD_DIM]


def softmax_rows(queries, keys, bias):
    scores = dot(queries, keys, NT) * 0.125 + bias
    raised = jnp.exp(scores - jnp.max(scores, axis=1, keepdims=True))
    return raised / jnp.sum(raised, axis=1, keepdims=True)


def attend_kernel(x_ref, qkv, wo, by_offset, packed, mixed, part, bias):
    @pl.when(pl.program_id(0) == 0)
    def _():
        fill_bias(by_offset, bias)

    x = x_ref[0].reshape(LEN, D)
    q, k, v = [dot(x, qkv[which]).astype(jnp.bfloat16) for which in range(3)]
    packed[0, 0] = q
    packed[0, 1] = k
    packed[0, 2] = v
    heads = []
    for head in range(HEADS_HERE):
        chances = softmax_rows(head_of(q, head), head_of(k, head), bias[head]).astype(jnp.bfloat16)
        heads.append(dot(chances, head_of(v, head)).astype(jnp.bfloat16))
    together = jnp.concatenate(heads, axis=1)
    mixed[0] = together
    part[0] = dot(together, wo[...]).astype(jnp.bfloat16).reshape(4, ROWS, D)


def whole(shape):
    return pl.BlockSpec(shape, lambda m: (0,) * len(shape))


def per_step(shape):
    return pl.BlockSpec((1,) + shape, lambda m: (m,) + (0,) * len(shape))


WIDTH = HEADS_HERE * HEAD_DIM


def attend(normed_all, qkv_weight, out_weight, by_offset):
    return pl.pallas_call(
        attend_kernel,
        grid=(MICRO,),
        out_shape=(
            jax.ShapeDtypeStruct((MICRO, 3, LEN, WIDTH), jnp.bfloat16),
            jax.ShapeDtypeStruct((MICRO, LEN, WIDTH), jnp.bfloat16),
            jax.ShapeDtypeStruct((MICRO, 4, ROWS, D), jnp.bfloat16),
        ),
        in_specs=[per_step((4, ROWS, D)), whole((3, D, WIDTH)), whole((WIDTH, D)), whole((8, 2 * LEN))],
        out_specs=(per_step((3, LEN, WIDTH)), per_step((LEN, WIDTH)), per_step((4, ROWS, D))),
        scratch_shapes=[pltpu.VMEM((HEADS_HERE, LEN, LEN), jnp.float32)],
        compiler_params=pltpu.CompilerParams(vmem_limit_bytes=VMEM_BYTES),
        name="attend",
    )(normed_all, qkv_weight, out_weight, by_offset)


def attend_back_kernel(weighted, grad_ref, x_ref, packed, mixed, qkv, wo, by_offset, *refs):
    if weighted:
        part, weight_grad, offset_grad, bias = refs
    else:
        part, bias = refs
    number = pl.program_id(0)

    @pl.when(number == 0)
    def _():
        fill_bias(by_offset, bias)
        if weighted:
            weight_grad[...] = jnp.zeros_like(weight_grad)
            offset_grad[...] = jnp.zeros_like(offset_grad)

    grad = grad_ref[0].reshape(LEN, D)
    mixed_grad = dot(grad, wo[...], NT).astype(jnp.bfloat16)
    q, k, v = packed[0, 0], packed[0, 1], packed[0, 2]
    q_grads, k_grads, v_grads = [], [], []
    if weighted:
        row = lax.broadcasted_iota(jnp.int32, (LEN, LEN), 0)
        column = lax.broadcasted_iota(jnp.int32, (LEN, LEN), 1)
        backwards = (row + column == LEN - 1).astype(jnp.bfloat16)
    for head in range(HEADS_HERE):
        q_head, k_head, v_head = head_of(q, head), head_of(k, head), head_of(v, head)
        grad_head = head_of(mixed_grad, head)
        chances = softmax_rows(q_head, k_head, bias[head])
        grad_chances = dot(grad_head, v_head, NT)
        weighed = jnp.sum(chances * grad_chances, axis=1, keepdims=True)
        grad_scores = (chances * (grad_chances - weighed)).astype(jnp.bfloat16)
        q_grads.append((dot(grad_scores, k_head) * 0.125).astype(jnp.bfloat16))
        k_grads.append((dot(grad_scores, q_head, TN) * 0.125).astype(jnp.bfloat16))
        v_grads.append(dot(chances.astype(jnp.bfloat16), grad_head, TN).astype(jnp.bfloat16))
        if weighted:
            turned = dot(backwards, grad_scores)
            wide = jnp.concatenate([turned, jnp.zeros_like(turned)], axis=1)
            aligned = pltpu.roll(wide, 0, 1, stride=1, stride_axis=0)
            offset_grad[pl.ds(head, 1), :] += jnp.sum(aligned, axis=0, keepdims=True)
    grads = [jnp.concatenate(pieces, axis=1) for pieces in (q_grads, k_grads, v_grads)]
    summed = dot(grads[0], qkv[0], NT) + dot(grads[1], qkv[1], NT) + dot(grads[2], qkv[2], NT)
    part[0] = summed.astype(jnp.bfloat16).reshape(4, ROWS, D)
    if weighted:
        x = x_ref[0].reshape(LEN, D)
        for which in range(3):
            weight_grad[which * WIDTH : (which + 1) * WIDTH, :] += dot(grads[which], x, TN)
        weight_grad[3 * WIDTH :, :] += dot(mixed[0], grad, TN)


def attend_back(weighted, grad_all, normed_all, packed, mixed, qkv_weight, out_weight, by_offset):
    out_shape = [jax.ShapeDtypeStruct((MICRO, 4, ROWS, D), jnp.bfloat16)]
    out_specs = [per_step((4, ROWS, D))]
    if weighted:
        out_shape += [
            jax.ShapeDtypeStruct((4 * WIDTH, D), jnp.float32),
            jax.ShapeDtypeStruct((8, 2 * LEN), jnp.float32),
        ]
        out_specs += [whole((4 * WIDTH, D)), whole((8, 2 * LEN))]
    return pl.pallas_call(
        functools.partial(attend_back_kernel, weighted),
        grid=(MICRO,),
        out_shape=out_shape,
        in_specs=[
            per_step((4, ROWS, D)),
            per_step((4, ROWS, D)),
            per_step((3, LEN, WIDTH)),
            per_step((LEN, WIDTH)),
            whole((3, D, WIDTH)),
            whole((WIDTH, D)),
            whole((8, 2 * LEN)),
        ],
        out_specs=out_specs,
        scratch_shapes=[pltpu.VMEM((HEADS_HERE, LEN, LEN), jnp.float32)],
        compiler_params=pltpu.CompilerParams(vmem_limit_bytes=VMEM_BYTES),
        name="attend_back",
    )(grad_all, normed_all, packed, mixed, qkv_weight, out_weight, by_offset)


GROUPS = 8
GROUP_ROWS = 8 * PIECE
SORTED = 8 * 12


def sorting():
    order = np.zeros((2, 2 * SORTED, GROUP_ROWS), np.float32)
    for e in range(2):
        for half in range(2):
            for sender in range(8):
                for at in range(12):
                    order[e, half * SORTED + sender * 12 + at, sender * PIECE + half * 24 + e * 12 + at] = 1
    return jnp.asarray(order, jnp.bfloat16)


def sort_in(order, arrived, rows):
    for group in range(GROUPS):
        picked = dot(order, arrived[group]).astype(jnp.bfloat16)
        where = pl.ds(group * SORTED, SORTED)
        rows[where, :HALF] = picked[:SORTED]
        rows[where, HALF:] = picked[SORTED:]


def sort_out(order, rows, out, expert):
    @pl.when(expert == 0)
    def _():
        out[...] = jnp.zeros_like(out)

    for group in range(GROUPS):
        where = pl.ds(group * SORTED, SORTED)
        both = jnp.concatenate([rows[where, :HALF], rows[where, HALF:]], axis=0)
        out[group] += dot(order, both, TN).astype(jnp.bfloat16)


SCALE = 0.7978845608028654
CUBIC = 0.044715
EXPERT_ROWS = GROUPS * SORTED
TILE = 256


def experts_kernel(order, arrived, inner, outer, part, rows, results):
    sort_in(order[0], arrived, rows)

    def one_tile(number, _):
        where = pl.ds(pl.multiple_of(number * TILE, TILE), TILE)
        pre = dot(rows[where, :], inner[0])
        hidden = 0.5 * pre * (1 + jnp.tanh(SCALE * (pre + CUBIC * pre * pre * pre)))
        results[where, :] = dot(hidden.astype(jnp.bfloat16), outer[0]).astype(jnp.bfloat16)
        return 0

    lax.fori_loop(0, EXPERT_ROWS // TILE, one_tile, 0)
    sort_out(order[0], results, part, pl.program_id(0))


def experts(arrived, order, inner_weight, outer_weight):
    return pl.pallas_call(
        experts_kernel,
        grid=(2,),
        out_shape=jax.ShapeDtypeStruct((GROUPS, GROUP_ROWS, HALF), jnp.bfloat16),
        in_specs=[
            per_step((2 * SORTED, GROUP_ROWS)),
            whole((GROUPS, GROUP_ROWS, HALF)),
            per_step((D, D)),
            per_step((D, D)),
        ],
        out_specs=whole((GROUPS, GROUP_ROWS, HALF)),
        scratch_shapes=[pltpu.VMEM((EXPERT_ROWS, D), jnp.bfloat16)] * 2,
        compiler_params=pltpu.CompilerParams(vmem_limit_bytes=VMEM_BYTES),
        name="experts",
    )(order, arrived.reshape(GROUPS, GROUP_ROWS, HALF), inner_weight, outer_weight).reshape(4, OWNERS, PIECE, HALF)


def experts_back_kernel(weighted, order, arrived, grad_arrived, inner, outer, *refs):
    if weighted:
        part, inner_grad, outer_grad, rows, grads, results, hiddens, pre_grads = refs
    else:
        part, rows, grads, results = refs
    sort_in(order[0], arrived, rows)
    sort_in(order[0], grad_arrived, grads)

    def one_tile(number, _):
        where = pl.ds(pl.multiple_of(number * TILE, TILE), TILE)
        pre = dot(rows[where, :], inner[0])
        squared = pre * pre
        bent = jnp.tanh(SCALE * pre * (1 + CUBIC * squared))
        slope = 0.5 * (1 + bent) + 0.5 * pre * (1 - bent * bent) * SCALE * (1 + 3 * CUBIC * squared)
        hidden_grad = dot(grads[where, :], outer[0], NT)
        pre_grad = (hidden_grad * slope).astype(jnp.bfloat16)
        results[where, :] = dot(pre_grad, inner[0], NT).astype(jnp.bfloat16)
        if weighted:
            hiddens[where, :] = (0.5 * pre * (1 + bent)).astype(jnp.bfloat16)
            pre_grads[where, :] = pre_grad
        return 0

    lax.fori_loop(0, EXPERT_ROWS // TILE, one_tile, 0)
    sort_out(order[0], results, part, pl.program_id(0))
    if weighted:

        def one_strip(number, _):
            where = pl.ds(pl.multiple_of(number * TILE, TILE), TILE)
            inner_grad[0, where, :] = dot(rows[:, where], pre_grads[...], TN)
            outer_grad[0, where, :] = dot(hiddens[:, where], grads[...], TN)
            return 0

        lax.fori_loop(0, D // TILE, one_strip, 0)


def experts_back(weighted, arrived, grad_arrived, order, inner_weight, outer_weight):
    out_shape = [jax.ShapeDtypeStruct((GROUPS, GROUP_ROWS, HALF), jnp.bfloat16)]
    out_specs = [whole((GROUPS, GROUP_ROWS, HALF))]
    if weighted:
        out_shape += [jax.ShapeDtypeStruct((2, D, D), jnp.float32)] * 2
        out_specs += [per_step((D, D))] * 2
    results = pl.pallas_call(
        functools.partial(experts_back_kernel, weighted),
        grid=(2,),
        out_shape=out_shape,
        in_specs=[
            per_step((2 * SORTED, GROUP_ROWS)),
            whole((GROUPS, GROUP_ROWS, HALF)),
            whole((GROUPS, GROUP_ROWS, HALF)),
            per_step((D, D)),
            per_step((D, D)),
        ],
        out_specs=out_specs,
        scratch_shapes=[pltpu.VMEM((EXPERT_ROWS, D), jnp.bfloat16)] * (5 if weighted else 3),
        compiler_params=pltpu.CompilerParams(vmem_limit_bytes=VMEM_BYTES),
        name="experts_back",
    )(
        order,
        arrived.reshape(GROUPS, GROUP_ROWS, HALF),
        grad_arrived.reshape(GROUPS, GROUP_ROWS, HALF),
        inner_weight,
        outer_weight,
    )
    return (results[0].reshape(4, OWNERS, PIECE, HALF),) + tuple(results[1:])


def rms_norm(values, gain):
    return values * lax.rsqrt(jnp.mean(values * values, axis=-1, keepdims=True) + 1e-06) * gain


def bucket_of(offsets):
    distance = jnp.abs(offsets)
    far_bucket = 8 + sum(
        ((distance >= threshold).astype(jnp.int32) for threshold in (12, 16, 23, 32, 46, 64, 91))
    )
    near_far = jnp.where(distance < 8, distance, far_bucket)
    return near_far + 16 * (offsets > 0).astype(jnp.int32)


def offset_buckets():
    offsets = jnp.arange(2 * LEN, dtype=jnp.int32) - (LEN - 1)
    return (bucket_of(offsets)[:, None] == jnp.arange(32, dtype=jnp.int32)[None, :]).astype(jnp.float32)


def spread_matrix(route_ids, slot_ids):
    row = jnp.arange(OWNERS * PIECE, dtype=jnp.int32)
    part = row // 6 % 8
    half, expert, micro = part // 4, part // 2 % 2, part % 2
    row_key = ((half * 2 + micro) * EXPERTS + row // PIECE * 2 + expert) * CAP + row % 6
    block = jnp.arange(4, dtype=jnp.int32)[:, None]
    token_key = route_ids * CAP + slot_ids
    column_key = (block * (EXPERTS * CAP) + jnp.concatenate([token_key, token_key], axis=0)).reshape(-1)
    return (row_key[:, None] == column_key[None, :]).astype(jnp.bfloat16)


def to_slots(spread, rows):
    stacked = jnp.concatenate([rows[:, :HALF], rows[:, HALF:]], axis=0)
    return dot(spread, stacked).astype(jnp.bfloat16).reshape(OWNERS, PIECE, HALF)


def from_slots(spread, slots):
    stacked = dot(spread, slots.reshape(OWNERS * PIECE, HALF), TN)
    return jnp.concatenate([stacked[: MICRO * ROWS], stacked[MICRO * ROWS :]], axis=1)


def flat(rows):
    return rows.reshape(MICRO * ROWS, D)


def stack(rows):
    return rows.reshape(MICRO, ROWS, D)


def layer_forward(incoming, common, weights, old, active, first_id):
    gains, qkv_weight, out_weight, by_offset, router_weight, inner_weight, outer_weight, order = weights
    spread, chosen = common
    old = old or (None,) * 4
    residual = incoming.astype(jnp.float32)
    normed = rms_norm(residual, gains[0]).astype(jnp.bfloat16)
    normed_all = gather_rows(stack(normed), old[0], active, first_id)
    packed, mixed, part = attend(normed_all, qkv_weight, out_weight, by_offset)
    attended = scatter_rows(part, old[1], active, first_id + 1)
    middle = residual + flat(attended)
    normed_two = rms_norm(middle, gains[1]).astype(jnp.bfloat16)
    arrived = dispatch(to_slots(spread, normed_two), old[2], active, first_id + 2)
    returned = combine(experts(arrived, order, inner_weight, outer_weight), old[3], active, first_id + 3)
    logits = dot(normed_two, router_weight)
    router_prob = jax.nn.softmax(logits, axis=-1)
    gating = jnp.sum(router_prob * chosen, axis=-1)
    expert_rows = from_slots(spread, returned)
    output = (middle + gating[:, None] * expert_rows).astype(jnp.bfloat16)
    kept = (normed_all, packed, mixed, middle, normed_two, router_prob, gating, expert_rows, arrived)
    return output, kept, (normed_all, attended, arrived, returned)


def layer_backward(weighted, grad_out, incoming, common, kept, weights, old, active, first_id):
    gains, qkv_weight, out_weight, by_offset, router_weight, inner_weight, outer_weight, order = weights
    spread, chosen = common
    normed_all, packed, mixed, middle, normed_two, router_prob, gating, expert_rows, arrived = kept
    old = old or (None,) * 4
    residual = incoming.astype(jnp.float32)
    grad_expert = (gating[:, None] * grad_out).astype(jnp.bfloat16)
    grad_arrived = dispatch(to_slots(spread, grad_expert), old[0], active, first_id)
    part, *expert_grads = experts_back(weighted, arrived, grad_arrived, order, inner_weight, outer_weight)
    grad_slots = combine(part, old[1], active, first_id + 1)
    gate_grad = jnp.sum(grad_out * expert_rows, axis=-1)
    logit_grad = ((gate_grad * gating)[:, None] * (chosen - router_prob)).astype(jnp.bfloat16)
    normed_two_grad = dot(logit_grad, router_weight, NT) + from_slots(spread, grad_slots)
    _, pull_two = jax.vjp(rms_norm, middle, gains[1])
    middle_part, gain_two = pull_two(normed_two_grad)
    middle_grad = grad_out + middle_part
    grad_all = gather_rows(stack(middle_grad.astype(jnp.bfloat16)), old[2], active, first_id + 2)
    part, *attend_grads = attend_back(
        weighted, grad_all, normed_all, packed, mixed, qkv_weight, out_weight, by_offset
    )
    normed_grad = scatter_rows(part, old[3], active, first_id + 3)
    _, pull_one = jax.vjp(rms_norm, residual, gains[0])
    residual_part, gain_one = pull_one(flat(normed_grad))
    input_grad = (middle_grad + residual_part).astype(jnp.bfloat16)
    if not weighted:
        return input_grad, None, (grad_arrived, grad_slots, grad_all, normed_grad)
    router_grad = dot(logit_grad, normed_two, TN)
    return input_grad, (gain_one, gain_two, router_grad, attend_grads, expert_grads), None


def per_device(
    stream, norm_gains, attn_qkv, attn_out, rel_bias, router, expert_in, expert_out, routes, slots
):
    buckets = offset_buckets()
    by_offset = lax.dot_general(
        rel_bias[0], buckets, (((0,), (1,)), ((), ())), precision=lax.Precision.HIGHEST
    )
    by_offset = jnp.concatenate([by_offset, jnp.zeros((5, 2 * LEN), jnp.float32)], axis=0)
    weights = (
        norm_gains[0],
        attn_qkv[0],
        attn_out[0],
        by_offset,
        router[0],
        expert_in[0],
        expert_out[0],
        sorting(),
    )
    spread = spread_matrix(routes[0], slots[0])
    chosen = (routes[0].reshape(-1)[:, None] == jnp.arange(EXPERTS, dtype=jnp.int32)[None, :]).astype(jnp.float32)
    common = (spread, chosen)
    is_first = lax.axis_index("section") == 0
    own = stream[0].reshape(MICRO * ROWS, D)

    early, _, held = layer_forward(own, common, weights, None, 0, 0)
    received = lax.ppermute(early, "section", [(0, 1)])
    incoming = jnp.where(is_first, own, received)
    output, kept, _ = layer_forward(incoming, common, weights, held, 1, 4)

    grad_out = own.astype(jnp.float32)
    late, _, held = layer_backward(False, grad_out, incoming, common, kept, weights, None, 1, 8)
    returned = lax.ppermute(late, "section", [(1, 0)])
    grad_out = jnp.where(is_first, returned, own).astype(jnp.float32)
    input_grad, grads, _ = layer_backward(True, grad_out, incoming, common, kept, weights, held, 0, 12)

    gain_one, gain_two, router_grad, (attend_grad, offset_grad), (inner_grad, outer_grad) = grads
    big = attend_grad.astype(jnp.bfloat16).reshape(OWNERS, PIECE, D)
    small = jnp.concatenate([router_grad, gain_one[None], gain_two[None]], axis=0)
    small = jnp.pad(small.reshape(-1), (0, 32768 - 34 * D))
    table = jnp.dot(offset_grad[:3], buckets, precision=lax.Precision.HIGHEST)
    table = jnp.pad(table, ((0, 5), (0, 96)))
    big, small, table = reduce_all(big, small.reshape(OWNERS, 8, 256), table, 16)
    big = big.reshape(4, WIDTH, D).astype(jnp.float32)
    small = small.reshape(-1)[: 34 * D].reshape(34, D)
    end_rows = jnp.where(is_first, input_grad, output).reshape(1, MICRO, ROWS, D)
    return (
        end_rows,
        small[32:][None],
        jnp.swapaxes(big[:3], 1, 2)[None],
        big[3][None],
        table[:3, :32].T[None],
        small[:32].T[None],
        inner_grad[None],
        outer_grad[None],
    )


def solution(mesh):
    return jax.shard_map(
        per_device,
        mesh=mesh,
        in_specs=(
            P("section", None, ("expert", "shard"), None),
            P("section", None, None),
            P("section", None, None, "shard"),
            P("section", "shard", None),
            P("section", None, "shard"),
            P("section", None, None),
            P("section", "expert", None, "shard"),
            P("section", "expert", "shard", None),
            P("section", None, ("expert", "shard")),
            P("section", None, ("expert", "shard")),
        ),
        out_specs=(
            P("section", None, ("expert", "shard"), None),
            P("section", None, None),
            P("section", None, None, "shard"),
            P("section", "shard", None),
            P("section", None, "shard"),
            P("section", None, None),
            P("section", "expert", None, "shard"),
            P("section", "expert", "shard", None),
        ),
        check_vma=False,
    )
```

time: 1730 us -> 572 us (0.33)
  waiting for transfers between devices: 775 us -> 179 us
  blocking collectives: 419 us -> 0 us
  Pallas kernels: 0 us -> 309 us
  local copies, waits for them, and re-layouts: 217 us -> 38.2 us
  matrix products: 160 us -> 9.25 us
  other arithmetic: 98.3 us -> 22.7 us
  starting transfers between devices: 37.3 us -> 2.73 us
    psum x2 -> x0, waiting for transfers between devices: 350 us -> none  [the longest x1 350 us: per_device(): lax.psum((gain_grad, router_grad), ('expert', 'shard'))]
    pallas_call x0 -> x25, Pallas kernels: none -> 309 us  [the longest x4 55 us: combine(): pl.pallas_call(functools.partial(combine_kernel, active, old is not None)...]
    reduce_scatter x12 -> x0, waiting for transfers between devices: 237 us -> none  [the longest x6 118 us: expert_pass(): lax.psum_scatter(returned.astype(jnp.bfloat16), 'shard', scatter_dimensio...]
    psum x2 -> x0, blocking collectives: 206 us -> none  [the longest x1 165 us: per_device(): lax.psum((gain_grad, router_grad), ('expert', 'shard'))]
    ppermute x4 -> x2, waiting for transfers between devices: 21 us -> 179 us  [the longest x1 170 us: per_device(): returned = lax.ppermute(late, 'section', [(1, 0)])]
    all_to_all x7 -> x0, blocking collectives: 156 us -> none  [the longest x5 104 us: expert_pass(): lax.all_to_all(partial_value.astype(jnp.bfloat16), 'expert', split_axis=0...]
    dot_general x79 -> x15, matrix products: 156 us -> 9.25 us  [the longest x13 8.44 us: dot(): lax.dot_general(a, b, (dims, ((), ())), preferred_element_type=jnp.float32)]
    all_gather x6 -> x0, waiting for transfers between devices: 109 us -> none  [expert_pass(): source = lax.all_gather(buffer, 'shard', axis=0, tiled=True)]
  transfers between devices with their start and end apart: 29 -> 2, of which waited for: 24 -> 2; matrix products, arithmetic and copies ran while one was open for 15% -> 0% of each run, Pallas kernels for 0% -> 0%
where the time goes in v1:
time: 572 us; the launch traced here: 563 us
  Pallas kernels  309 us (54%)
  waiting for transfers between devices  179 us (31%)
  local copies, waits for them, and re-layouts  38.2 us (7%)
  other arithmetic  22.7 us (4%)
  matrix products  9.25 us (2%)
    ppermute x1, waiting for transfers between devices, per_device(): returned = lax.ppermute(late, 'section', [(1, 0)])  170 us
    pallas_call x4, Pallas kernels, combine(): pl.pallas_call(functools.partial(combine_kernel, active, old is not None)...  55 us
    pallas_call x4, Pallas kernels, dispatch(): pl.pallas_call(functools.partial(dispatch_kernel, active, old is not None...  54.1 us
    pallas_call x1, Pallas kernels, reduce_all(): pl.pallas_call(reduce_kernel, out_shape=(jax.ShapeDtypeStruct(big.shape,...  41.1 us
    pallas_call x2, Pallas kernels, experts_back(): pl.pallas_call(functools.partial(experts_back_kernel, weighted), grid=(2,...  39.3 us
    pallas_call x4, Pallas kernels, scatter_rows(): pl.pallas_call(functools.partial(scatter_kernel, active, old is not None)...  29.4 us
    pallas_call x4, Pallas kernels, gather_rows(): pl.pallas_call(functools.partial(gather_kernel, active, old is not None),...  28.2 us
    pallas_call x2, Pallas kernels, attend_back(): pl.pallas_call(functools.partial(attend_back_kernel, weighted), grid=(MIC...  24.9 us
  transfers between devices with their start and end apart: 2, of which 2 were waited for; matrix products, arithmetic and copies ran while one was open for 0% of the time, Pallas kernels for 0%

profile of v1, /device:TPU:0, one launch (start us, length us, event | category | flops | bytes accessed | tf_op | source)
XLA Modules:
  0.0 562.9 jit_solution(3236280772798954447)
XLA Ops:
  5.2 14.4 %gather_rows.4.x_ref.refs_0_ = bf16[2,4,128,768]{3,2,1,0:T(8,128)(2,1)S(1)} custom-call(bf16[2,128,768]{2,1,0:T(8,128)(2,1)S(1)} %fusion.36.x), custom_call_target="tpu_custom_call" | custom-call | tf_op jit(solution)/shard_map/gather_rows/pallas_call | solution.py:106
  21.9 7.1 %attend.2 = (bf16[2,3,512,192]{3,2,1,0:T(8,128)(2,1)}, bf16[2,512,192]{2,1,0:T(8,128)(2,1)}, bf16[2,4,128,768]{3,2,1,0:T(8,128)(2,1)S(1)}) custom-call(bf16[2,4,128,768]{3,2,1,0:T(8,128)(2,1)} %copy-done.9, bf16[3,768,192]{2,1,0:T(8,128)(2,1)S(1)} %bitcast.105, bf16[192,768]{1,0:T(8,128)(2,1)S(1)} %bitcast.117, f32[8,1024]{1,0:T(8,128)S(1)} %concatenate.41.by_offset), custom_call_target="tpu_custom_call" | custom-call | tf_op jit(solution)/shard_map/attend/pallas_call | solution.py:453
  28.9 14.5 %scatter_rows.4.refs_0_ = f32[2,128,768]{2,1,0:T(8,128)S(1)} custom-call(bf16[2,4,128,768]{3,2,1,0:T(8,128)(2,1)S(1)} %get-tuple-element.21.part), custom_call_target="tpu_custom_call" | custom-call | tf_op jit(solution)/shard_map/scatter_rows/pallas_call | solution.py:157
  46.9 27.0 %dispatch.4.refs_0_ = bf16[4,16,48,384]{3,2,1,0:T(8,128)(2,1)S(1)} custom-call(bf16[16,48,384]{2,1,0:T(8,128)(2,1)S(1)} %bitcast.134), custom_call_target="tpu_custom_call" | custom-call | tf_op jit(solution)/shard_map/dispatch/pallas_call | solution.py:223
  73.9 12.1 %experts.2 = bf16[8,384,384]{2,1,0:T(8,128)(2,1)S(1)} custom-call(bf16[2,192,384]{2,1,0:T(8,128)(2,1)S(1)} %copy-done.16, bf16[8,384,384]{2,1,0:T(8,128)(2,1)S(1)} %bitcast.109, bf16[2,768,768]{2,1,0:T(8,128)(2,1)} %bitcast.137, bf16[2,768,768]{2,1,0:T(8,128)(2,1)} %bitcast.141), custom_call_target="tpu_custom_call" | custom-call | tf_op jit(solution)/shard_map/experts/pallas_call | solution.py:600
  86.0 26.8 %combine.4.refs_0_ = bf16[16,48,384]{2,1,0:T(8,128)(2,1)S(1)} custom-call(bf16[4,16,48,384]{3,2,1,0:T(8,128)(2,1)S(1)} %bitcast.113), custom_call_target="tpu_custom_call" | custom-call | tf_op jit(solution)/shard_map/combine/pallas_call | solution.py:294
  116.2 8.3 %collective-permute-done = bf16[256,768]{0,1:T(8,128)(2,1)S(1)} collective-permute-done((bf16[256,768]{0,1:T(8,128)(2,1)}, bf16[256,768]{0,1:T(8,128)(2,1)S(1)}, u32[]{:S(2)}, u32[]{:S(2)}) %collective-permute-start) | collective-permute-done | bytes 393248 | tf_op jit(solution)/shard_map/ppermute | solution.py:807
  125.4 1.9 fusion.33
  128.5 1.4 copy-done.10
  131.7 6.6 %attend.3 = (bf16[2,3,512,192]{3,2,1,0:T(8,128)(2,1)S(1)}, bf16[2,512,192]{2,1,0:T(8,128)(2,1)S(1)}, bf16[2,4,128,768]{3,2,1,0:T(8,128)(2,1)S(1)}) custom-call(bf16[2,4,128,768]{3,2,1,0:T(8,128)(2,1)} %copy-done.4, bf16[3,768,192]{2,1,0:T(8,128)(2,1)S(1)} %bitcast.106, bf16[192,768]{1,0:T(8,128)(2,1)S(1)} %bitcast.118, f32[8,1024]{1,0:T(8,128)S(1)} %concatenate.41.by_offset), custom_call_target="tpu_custom_call" | custom-call | tf_op jit(solution)/shard_map/attend/pallas_call | solution.py:453
  147.3 11.3 %experts.3 = bf16[8,384,384]{2,1,0:T(8,128)(2,1)S(1)} custom-call(bf16[2,192,384]{2,1,0:T(8,128)(2,1)S(1)} %copy-done.16, bf16[8,384,384]{2,1,0:T(8,128)(2,1)S(1)} %bitcast.102, bf16[2,768,768]{2,1,0:T(8,128)(2,1)} %bitcast.138, bf16[2,768,768]{2,1,0:T(8,128)(2,1)} %bitcast.142), custom_call_target="tpu_custom_call" | custom-call | tf_op jit(solution)/shard_map/experts/pallas_call | solution.py:600
  158.5 15.9 %experts_back.2 = bf16[8,384,384]{2,1,0:T(8,128)(2,1)S(1)} custom-call(bf16[2,192,384]{2,1,0:T(8,128)(2,1)S(1)} %copy-done.16, bf16[8,384,384]{2,1,0:T(8,128)(2,1)S(1)} %bitcast.103, bf16[8,384,384]{2,1,0:T(8,128)(2,1)} %bitcast.110, bf16[2,768,768]{2,1,0:T(8,128)(2,1)} %bitcast.139, bf16[2,768,768]{2,1,0:T(8,128)(2,1)} %bitcast.143), custom_call_target="tpu_custom_call" | custom-call | tf_op jit(solution)/shard_map/experts_back/pallas_call | solution.py:658
  179.1 2.0 copy.25
  181.1 1.9 copy.27
  183.0 1.4 fusion.39
  185.1 1.5 multiply_reduce_fusion.2
  188.7 2.0 copy.29
  192.1 10.3 %attend_back.2.part = bf16[2,4,128,768]{3,2,1,0:T(8,128)(2,1)S(1)} custom-call(bf16[2,4,128,768]{3,2,1,0:T(8,128)(2,1)S(1)} %gather_rows.6.grad_ref.refs_0_, bf16[2,4,128,768]{3,2,1,0:T(8,128)(2,1)} %copy-done.4, bf16[2,3,512,192]{3,2,1,0:T(8,128)(2,1)} %copy-done.14, bf16[2,512,192]{2,1,0:T(8,128)(2,1)S(1)} %copy-done.23, ...), custom_call_target="tpu_custom_call" | custom-call | tf_op jit(solution)/shard_map/attend_back/pallas_call | solution.py:525
  204.8 1.5 fusion.47
  207.5 2.1 fusion.41
  209.6 1.4 collective-permute-start.1
  211.1 170.4 %collective-permute-done.1 = bf16[256,768]{0,1:T(8,128)(2,1)S(1)} collective-permute-done((bf16[256,768]{0,1:T(8,128)(2,1)S(1)}, bf16[256,768]{0,1:T(8,128)(2,1)S(1)}, u32[]{:S(2)}, u32[]{:S(2)}) %collective-permute-start.1) | collective-permute-done | bytes 393248 | tf_op jit(solution)/shard_map/ppermute | solution.py:813
  384.3 25.9 %dispatch.7 = bf16[4,16,48,384]{3,2,1,0:T(8,128)(2,1)S(1)} custom-call(bf16[16,48,384]{2,1,0:T(8,128)(2,1)S(1)} %bitcast.133, bf16[4,16,48,384]{3,2,1,0:T(8,128)(2,1)S(1)} %copy-done.8), custom_call_target="tpu_custom_call" | custom-call | tf_op jit(solution)/shard_map/dispatch/pallas_call | solution.py:223
  411.5 23.4 %experts_back.3 = (bf16[8,384,384]{2,1,0:T(8,128)(2,1)S(1)}, f32[2,768,768]{2,1,0:T(8,128)}, f32[2,768,768]{2,1,0:T(8,128)}) custom-call(bf16[2,192,384]{2,1,0:T(8,128)(2,1)S(1)} %copy-done.17, bf16[8,384,384]{2,1,0:T(8,128)(2,1)S(1)} %bitcast.104, bf16[8,384,384]{2,1,0:T(8,128)(2,1)} %bitcast.115, bf16[2,768,768]{2,1,0:T(8,128)(2,1)} %bitcast.140, ...), custom_call_target="tpu_custom_call" | custom-call | tf_op jit(solution)/shard_map/experts_back/pallas_call | solution.py:658
  434.9 26.8 %combine.7 = bf16[16,48,384]{2,1,0:T(8,128)(2,1)S(1)} custom-call(bf16[4,16,48,384]{3,2,1,0:T(8,128)(2,1)S(1)} %bitcast.124, bf16[16,48,384]{2,1,0:T(8,128)(2,1)S(1)} %copy-done.21), custom_call_target="tpu_custom_call" | custom-call | tf_op jit(solution)/shard_map/combine/pallas_call | solution.py:294
  464.2 1.9 copy.32
  467.1 13.0 %gather_rows.7.grad_ref = bf16[2,4,128,768]{3,2,1,0:T(8,128)(2,1)S(1)} custom-call(bf16[2,128,768]{2,1,0:T(8,128)(2,1)S(1)} %bitcast.128, bf16[2,4,128,768]{3,2,1,0:T(8,128)(2,1)S(1)} %copy-done.12), custom_call_target="tpu_custom_call" | custom-call | tf_op jit(solution)/shard_map/gather_rows/pallas_call | solution.py:106
  480.1 14.7 %attend_back.3 = (bf16[2,4,128,768]{3,2,1,0:T(8,128)(2,1)S(1)}, f32[768,768]{1,0:T(8,128)}, f32[8,1024]{1,0:T(8,128)S(1)}) custom-call(bf16[2,4,128,768]{3,2,1,0:T(8,128)(2,1)S(1)} %gather_rows.7.grad_ref, bf16[2,4,128,768]{3,2,1,0:T(8,128)(2,1)} %copy-done.4, bf16[2,3,512,192]{3,2,1,0:T(8,128)(2,1)} %copy-done.14, bf16[2,512,192]{2,1,0:T(8,128)(2,1)S(1)} %copy-done.24, ...), custom_call_target="tpu_custom_call" | custom-call | tf_op jit(solution)/shard_map/attend_back/pallas_call | solution.py:525
  495.1 14.6 %scatter_rows.7 = f32[2,128,768]{2,1,0:T(8,128)S(1)} custom-call(bf16[2,4,128,768]{3,2,1,0:T(8,128)(2,1)S(1)} %get-tuple-element.26.part, f32[2,128,768]{2,1,0:T(8,128)S(1)} %scatter_rows.6.refs_0_), custom_call_target="tpu_custom_call" | custom-call | tf_op jit(solution)/shard_map/scatter_rows/pallas_call | solution.py:157
  511.9 1.8 convert_element_type.198
  513.7 41.1 %reduce_all.1 = (bf16[16,48,768]{2,1,0:T(8,128)(2,1)S(1)}, f32[16,8,256]{2,1,0:T(8,128)S(1)}, f32[8,128]{1,0:T(8,128)S(1)}) custom-call(bf16[16,48,768]{2,1,0:T(8,128)(2,1)S(1)} %bitcast.121, f32[16,8,256]{2,1,0:T(8,128)S(1)} %reshape.422.small, f32[8,128]{1,0:T(8,128)S(1)} %pad.10.table), custom_call_target="tpu_custom_call" | custom-call | tf_op jit(solution)/shard_map/reduce_all/pallas_call | solution.py:368
  558.1 1.5 fusion.68
  (260 shorter events, 54.3 us)
Async XLA Ops:
  0.6 113.0 %copy-start = (bf16[1,768,32]{1,2,0:T(8,128)(2,1)S(1)}, bf16[1,768,32]{1,2,0:T(8,128)(2,1)}, u32[]{:S(2)}) copy-start(bf16[1,768,32]{1,2,0:T(8,128)(2,1)} %param.16) | copy-start | bytes 147460
  0.7 174.4 %copy-start.75 = (s32[768]{0:T(1024)}, s32[768]{0:T(1024)S(1)}, u32[]{:S(2)}) copy-start(s32[768]{0:T(1024)S(1)} %fusion.107) | copy-start | bytes 9220
  0.7 20.6 %copy-start.73 = (s32[1024]{0:T(1024)}, s32[1024]{0:T(1024)S(1)}, u32[]{:S(2)}) copy-start(s32[1024]{0:T(1024)S(1)} %fusion.114) | copy-start | bytes 12292
  2.7 122.7 %copy-start.52 = (f32[768]{0:T(1024)}, f32[768]{0:T(1024)S(1)}, u32[]{:S(2)}) copy-start(f32[768]{0:T(1024)S(1)} %get-tuple-element.47) | copy-start | bytes 9220
  2.7 139.0 %copy-start.49 = (f32[768]{0:T(1024)}, f32[768]{0:T(1024)S(1)}, u32[]{:S(2)}) copy-start(f32[768]{0:T(1024)S(1)} %get-tuple-element.46) | copy-start | bytes 9220
  3.9 138.4 %copy-start.31 = (bf16[256,768]{0,1:T(8,128)(2,1)}, bf16[256,768]{0,1:T(8,128)(2,1)S(1)}, u32[]{:S(2)}) copy-start(bf16[256,768]{0,1:T(8,128)(2,1)S(1)} %copy.40) | copy-start | bytes 1179652
  3.9 16.8 %copy-start.47 = (bf16[1,3,768,192]{2,3,1,0:T(8,128)(2,1)S(1)}, bf16[1,3,768,192]{2,3,1,0:T(8,128)(2,1)}, u32[]{:S(2)}) copy-start(bf16[1,3,768,192]{2,3,1,0:T(8,128)(2,1)} %param.13) | copy-start | bytes 2654212
  5.2 16.1 %copy-start.84 = (f32[1,32,3]{1,0,2:T(1,128)S(1)}, f32[1,32,3]{1,0,2:T(1,128)}, u32[]{:S(2)}) copy-start(f32[1,32,3]{1,0,2:T(1,128)} %param.15) | copy-start | bytes 1156
  21.4 109.1 %copy-start.1 = (bf16[1,3,768,192]{3,2,1,0:T(8,128)(2,1)}, bf16[1,3,768,192]{3,2,1,0:T(8,128)(2,1)S(1)}, u32[]{:S(2)}) copy-start(bf16[1,3,768,192]{3,2,1,0:T(8,128)(2,1)S(1)} %copy.20) | copy-start | bytes 2654212
  28.9 14.5 %copy-start.34 = (bf16[1,2,128,768]{3,2,1,0:T(8,128)(2,1)S(1)}, bf16[1,2,128,768]{3,2,1,0:T(8,128)(2,1)}, u32[]{:S(2)}) copy-start(bf16[1,2,128,768]{3,2,1,0:T(8,128)(2,1)} %param.11) | copy-start | bytes 1179652
  46.3 128.8 %copy-start.80 = (s32[512]{0:T(512)}, s32[512]{0:T(512)S(1)}, u32[]{:S(2)}) copy-start(s32[512]{0:T(512)S(1)} %fusion.129) | copy-start | bytes 6148
  46.9 27.0 %copy-start.16 = (bf16[2,192,384]{2,1,0:T(8,128)(2,1)S(1)}, bf16[2,192,384]{2,1,0:T(8,128)(2,1)}, u32[]{:S(2)}) copy-start(bf16[2,192,384]{2,1,0:T(8,128)(2,1)} %constant.128.clone.order) | copy-start | bytes 884740
  73.9 12.1 %copy-start.5 = (bf16[4,16,48,384]{3,2,1,0:T(8,128)(2,1)}, bf16[4,16,48,384]{3,2,1,0:T(8,128)(2,1)S(1)}, u32[]{:S(2)}) copy-start(bf16[4,16,48,384]{3,2,1,0:T(8,128)(2,1)S(1)} %dispatch.4.refs_0_) | copy-start | bytes 7077892
  114.9 9.6 %collective-permute-start = (bf16[256,768]{0,1:T(8,128)(2,1)}, bf16[256,768]{0,1:T(8,128)(2,1)S(1)}, u32[]{:S(2)}, u32[]{:S(2)}) collective-permute-start(bf16[256,768]{0,1:T(8,128)(2,1)} %fusion.50), channel_id=1, source_target_pairs={{0,64},{1,65},{2,66},{3,67},{4,68},{5,69},{6,70},{7,71},{8,72},{9,... | collective-permute-start | bytes 1179656 | tf_op jit(solution)/shard_map/ppermute | solution.py:807
  179.1 6.0 %copy-start.28 = (f32[256,768]{0,1:T(8,128)S(1)}, f32[256,768]{0,1:T(8,128)}, u32[]{:S(2)}) copy-start(f32[256,768]{0,1:T(8,128)} %copy-done.27) | copy-start | bytes 2359300
  207.5 173.9 %copy-start.33 = (bf16[256,768]{0,1:T(8,128)(2,1)S(1)}, bf16[256,768]{0,1:T(8,128)(2,1)}, u32[]{:S(2)}) copy-start(bf16[256,768]{0,1:T(8,128)(2,1)} %copy-done.31) | copy-start | bytes 1179652
  207.5 173.9 %copy-start.41 = (f32[256,384]{0,1:T(8,128)S(1)}, f32[256,384]{0,1:T(8,128)}, u32[]{:S(2)}) copy-start(f32[256,384]{0,1:T(8,128)} %get-tuple-element.62) | copy-start | bytes 1179652
  207.5 173.9 %copy-start.43 = (f32[256,384]{0,1:T(8,128)S(1)}, f32[256,384]{0,1:T(8,128)}, u32[]{:S(2)}) copy-start(f32[256,384]{0,1:T(8,128)} %get-tuple-element.63) | copy-start | bytes 1179652
  209.6 172.1 %copy-start.63 = (f32[256]{0:T(256)S(1)}, f32[256]{0:T(256)}, u32[]{:S(2)}) copy-start(f32[256]{0:T(256)} %copy-done.62) | copy-start | bytes 3076
  209.6 172.1 %copy-start.40 = (bf16[256,768]{0,1:T(8,128)(2,1)S(1)}, bf16[256,768]{0,1:T(8,128)(2,1)}, u32[]{:S(2)}) copy-start(bf16[256,768]{0,1:T(8,128)(2,1)} %copy-done.39) | copy-start | bytes 1179652
  209.6 172.1 %copy-start.59 = (f32[256]{0:T(256)S(1)}, f32[256]{0:T(256)}, u32[]{:S(2)}) copy-start(f32[256]{0:T(256)} %copy-done.58) | copy-start | bytes 3076
  209.6 172.1 %copy-start.61 = (s32[1,2,128]{2,1,0:T(2,128)S(1)}, s32[1,2,128]{2,1,0:T(2,128)}, u32[]{:S(2)}) copy-start(s32[1,2,128]{2,1,0:T(2,128)} %param.19) | copy-start | bytes 3076
  209.6 172.1 %copy-start.68 = (f32[256]{0:T(256)S(1)}, f32[256]{0:T(256)}, u32[]{:S(2)}) copy-start(f32[256]{0:T(256)} %copy-done.67) | copy-start | bytes 3076
  209.6 173.1 %copy-start.77 = (s32[768]{0:T(1024)S(1)}, s32[768]{0:T(1024)}, u32[]{:S(2)}) copy-start(s32[768]{0:T(1024)} %copy-done.75) | copy-start | bytes 9220
  209.6 173.1 %copy-start.82 = (s32[512]{0:T(512)S(1)}, s32[512]{0:T(512)}, u32[]{:S(2)}) copy-start(s32[512]{0:T(512)} %copy-done.80) | copy-start | bytes 6148
  209.6 171.8 %collective-permute-start.1 = (bf16[256,768]{0,1:T(8,128)(2,1)S(1)}, bf16[256,768]{0,1:T(8,128)(2,1)S(1)}, u32[]{:S(2)}, u32[]{:S(2)}) collective-permute-start(bf16[256,768]{0,1:T(8,128)(2,1)S(1)} %fusion.41), channel_id=1, source_target_pairs={{64,0},{65,1},{66,2},{67,3},{68,4},{69,5},{70,6},{71,7},{72,8},{73... | collective-permute-start | bytes 1179656 | tf_op jit(solution)/shard_map/ppermute | solution.py:813
  381.6 81.5 %copy-start.45 = (bf16[256,768]{0,1:T(8,128)(2,1)}, bf16[256,768]{0,1:T(8,128)(2,1)S(1)}, u32[]{:S(2)}) copy-start(bf16[256,768]{0,1:T(8,128)(2,1)S(1)} %get-tuple-element.49) | copy-start | bytes 1179652
  384.3 27.3 %copy-start.17 = (bf16[2,192,384]{2,1,0:T(8,128)(2,1)S(1)}, bf16[2,192,384]{2,1,0:T(8,128)(2,1)}, u32[]{:S(2)}) copy-start(bf16[2,192,384]{2,1,0:T(8,128)(2,1)} %constant.128.clone.order) | copy-start | bytes 884740
  411.5 23.4 %copy-start.21 = (bf16[16,48,384]{2,1,0:T(8,128)(2,1)S(1)}, bf16[16,48,384]{2,1,0:T(8,128)(2,1)}, u32[]{:S(2)}) copy-start(bf16[16,48,384]{2,1,0:T(8,128)(2,1)} %copy-done.20) | copy-start | bytes 1769476
  467.1 13.0 %copy-start.3 = (bf16[1,3,768,192]{3,2,1,0:T(8,128)(2,1)S(1)}, bf16[1,3,768,192]{3,2,1,0:T(8,128)(2,1)}, u32[]{:S(2)}) copy-start(bf16[1,3,768,192]{3,2,1,0:T(8,128)(2,1)} %copy-done.1) | copy-start | bytes 2654212
  467.1 13.0 %copy-start.24 = (bf16[2,512,192]{2,1,0:T(8,128)(2,1)S(1)}, bf16[2,512,192]{2,1,0:T(8,128)(2,1)}, u32[]{:S(2)}) copy-start(bf16[2,512,192]{2,1,0:T(8,128)(2,1)} %copy-done.22) | copy-start | bytes 1179652
  480.1 14.7 %copy-start.74 = (s32[1024]{0:T(1024)S(1)}, s32[1024]{0:T(1024)}, u32[]{:S(2)}) copy-start(s32[1024]{0:T(1024)} %copy-done.73) | copy-start | bytes 12292
  (55 other events, 94.9 us)

commit v2 on v0

v2 whole, which is shorter than its diff:
```python
import functools

import jax
import jax.numpy as jnp
import numpy as np
from jax import lax
from jax.experimental import pallas as pl
from jax.experimental.pallas import tpu as pltpu
from jax.sharding import PartitionSpec as P

HEAD_DIM = 64
HEADS_HERE = 3
LEN = 512
MICRO = 2
ROWS = 128
D = 768
HALF = 384
EXPERTS = 32
CAP = 6
OWNERS = 16
WAVES = 3
PIECE = 16
RELAY = False
VMEM_BYTES = 60 * 1024 * 1024
MESH = pl.DeviceIdType.MESH
ANY = pl.BlockSpec(memory_space=pl.ANY)
VMEM = pl.BlockSpec(memory_space=pltpu.VMEM)


def remote_to(src, dst, send, recv, device):
    return pltpu.make_async_remote_copy(
        src_ref=src, dst_ref=dst, send_sem=send, recv_sem=recv, device_id=device, device_id_type=MESH
    )


def remote(src, dst, send, recv, axis, index):
    return remote_to(src, dst, send, recv, {axis: index})


def greet(partners):
    barrier = pltpu.get_barrier_semaphore()
    for device in partners:
        pl.semaphore_signal(barrier, inc=1, device_id=device, device_id_type=MESH)
    return lambda: pl.semaphore_wait(barrier, len(partners))


def shard_places():
    me = lax.axis_index("shard")
    y, core = lax.div(me, 2), lax.rem(me, 2)
    return me, 2 * y + (1 - core), 2 * (1 - y) + core, 2 * (1 - y) + (1 - core)


def expert_places():
    me = lax.axis_index("expert")
    return me, lax.div(me, 4), lax.rem(me, 4)


def owner_at(x, z, dx, dz):
    return lax.rem(x + dx, 4) * 4 + lax.rem(z + dz, 4)


def all_owners(x, z):
    return [{"expert": owner_at(x, z, dx, dz)} for dx in range(4) for dz in range(4) if dx or dz]


def relays():
    other = 1 - lax.axis_index("section")
    return [{"section": other}, {"section": other, "shard": shard_places()[2]}]


class Cross:
    def __init__(self, held, sems):
        self.held = held
        self.to_send, self.to_recv, self.on_send, self.on_recv = sems
        self.ways = relays()
        self.cross = {"shard": shard_places()[2]}

    def to(self, n, half, source, goal):
        if not RELAY:
            return remote_to(source, goal, self.to_send.at[half, n], self.on_recv.at[half, n], self.cross)
        return remote_to(
            source, self.held.at[half, n], self.to_send.at[half, n], self.to_recv.at[half, n], self.ways[half]
        )

    def on(self, n, half, goal):
        return remote_to(
            self.held.at[half, n], goal, self.on_send.at[half, n], self.on_recv.at[half, n], self.ways[1 - half]
        )

    def start(self, n, sources, goals):
        for half in range(2):
            self.to(n, half, sources[half], goals[half]).start()

    def wait_recv(self, n, goals):
        for half in range(2):
            if RELAY:
                self.on(n, half, goals[half]).wait_recv()
            else:
                self.to(n, half, goals[half], goals[half]).wait_recv()

    def wait_send(self, n, sources):
        for half in range(2):
            self.to(n, half, sources[half], sources[half]).wait_send()

    def pass_on(self, n, goals):
        for half in range(2):
            self.to(n, half, goals[half], goals[half]).wait_recv()
            self.on(n, half, goals[half]).start()

    def passed(self, n, goals):
        for half in range(2):
            self.on(n, half, goals[half]).wait_send()


def across():
    return relays() if RELAY else [{"shard": shard_places()[2]}]


def when_active(active, run, rest):
    mine = lax.axis_index("section") == active
    pl.when(mine)(run)
    pl.when(jnp.logical_not(mine))(rest)


def keep_old(olds, outs, sem, between):
    keeps = [pltpu.make_async_copy(old, out, sem.at[n]) for n, (old, out) in enumerate(zip(olds, outs))]
    direct = keeps if between is None else keeps[2:]
    for keep in direct:
        keep.start()

    def done():
        for keep in direct:
            keep.wait()
        if between is not None and olds:
            for n in range(2):
                for source, goal in ((olds[n], between), (between, outs[n])):
                    hop = pltpu.make_async_copy(source, goal, sem.at[n])
                    hop.start()
                    hop.wait()

    return done


def dot(a, b, dims=((1,), (0,))):
    return lax.dot_general(a, b, (dims, ((), ())), preferred_element_type=jnp.float32)


NT = ((1,), (1,))
TN = ((0,), (0,))
WIDTH = HEADS_HERE * HEAD_DIM


def rms_norm(values, gain):
    return values * lax.rsqrt(jnp.mean(values * values, axis=-1, keepdims=True) + 1e-06) * gain


def rms_norm_back(values, gain, grad):
    scale = lax.rsqrt(jnp.mean(values * values, axis=-1, keepdims=True) + 1e-06)
    unit = values * scale
    unit_grad = grad * gain
    value_grad = scale * (unit_grad - unit * jnp.mean(unit_grad * unit, axis=-1, keepdims=True))
    return value_grad, jnp.sum(grad * unit, axis=0, keepdims=True)


def fill_bias(by_offset, bias):
    for head in range(HEADS_HERE):
        spread = jnp.broadcast_to(by_offset[pl.ds(head, 1), :], (LEN, 2 * LEN))
        bias[head] = pltpu.roll(spread, LEN + 1, 1, stride=1, stride_axis=0)[:, :LEN]


def head_of(array, head):
    return array[:, head * HEAD_DIM : (head + 1) * HEAD_DIM]


def softmax_rows(queries, keys, bias):
    scores = dot(queries, keys, NT) * 0.125 + bias
    raised = jnp.exp(scores - jnp.max(scores, axis=1, keepdims=True))
    return raised / jnp.sum(raised, axis=1, keepdims=True)


def row_halves(block):
    return [block.at[pl.ds(half * ROWS // 2, ROWS // 2)] for half in range(2)]


class Gather:
    def __init__(self, rows, held, sems):
        self.rows, self.send, self.recv = rows, sems[0], sems[1]
        self.cross_link = Cross(held, sems[2:])
        self.me, self.core, self.cross, _ = shard_places()

    def piece(self, m, whose, kind):
        block = self.rows.at[m, whose]
        at = 2 * kind + m
        return remote(block, block, self.send.at[at], self.recv.at[at], "shard", self.core)

    def start(self, m):
        block = row_halves(self.rows.at[m, self.me])
        self.cross_link.start(m, block, block)
        self.near(m).start()

    def near(self, m):
        return self.piece(m, self.me, 0)

    def on(self, m):
        return self.piece(m, self.cross, 1)

    def hand_on(self, m):
        self.cross_link.wait_recv(m, row_halves(self.rows.at[m, self.cross]))
        self.on(m).start()

    def finish(self, m):
        self.near(m).wait_recv()
        self.on(m).wait_recv()

    def drain(self):
        for m in range(MICRO):
            self.cross_link.wait_send(m, row_halves(self.rows.at[m, self.me]))
            self.near(m).wait_send()
            self.on(m).wait_send()

    def goals(self, m):
        return [row_halves(self.rows.at[m, whose])[half] for half, whose in enumerate((self.me, self.cross))]

    def pass_on(self):
        for m in range(MICRO):
            self.cross_link.pass_on(m, self.goals(m))

    def passed(self):
        for m in range(MICRO):
            self.cross_link.passed(m, self.goals(m))


class HeadSum:
    def __init__(self, part, buffers, held, sems):
        self.part, self.send, self.recv = part, sems[0], sems[1]
        self.cross_link = Cross(held, sems[2:])
        self.pair, self.mine, self.theirs, self.crossed = buffers
        self.me, self.core, self.cross, self.diag = shard_places()

    def first(self, m):
        return remote(self.part.at[m, self.diag], self.theirs.at[m], self.send.at[m], self.recv.at[m], "shard", self.core)

    def second(self, m):
        return remote(
            self.part.at[m, self.core], self.mine.at[m], self.send.at[2 + m], self.recv.at[2 + m], "shard", self.core
        )

    def start(self, m):
        self.first(m).start()
        self.second(m).start()

    def cross_over(self, m):
        self.first(m).wait_recv()
        self.pair[m] = (self.part[m, self.cross].astype(jnp.float32) + self.theirs[m].astype(jnp.float32)).astype(
            jnp.bfloat16
        )
        self.cross_link.start(m, row_halves(self.pair.at[m]), row_halves(self.crossed.at[m]))

    def total(self, m):
        self.second(m).wait_recv()
        self.cross_link.wait_recv(m, row_halves(self.crossed.at[m]))
        return (
            self.part[m, self.me].astype(jnp.float32)
            + self.mine[m].astype(jnp.float32)
            + self.crossed[m].astype(jnp.float32)
        )

    def drain(self):
        for m in range(MICRO):
            self.first(m).wait_send()
            self.second(m).wait_send()
            self.cross_link.wait_send(m, row_halves(self.pair.at[m]))

    def pass_on(self):
        for m in range(MICRO):
            self.cross_link.pass_on(m, row_halves(self.crossed.at[m]))

    def passed(self):
        for m in range(MICRO):
            self.cross_link.passed(m, row_halves(self.crossed.at[m]))


SHARD_BUFFERS = (
    [pltpu.VMEM((MICRO, 4, ROWS, D), jnp.bfloat16)]
    + [pltpu.VMEM((MICRO, ROWS, D), jnp.bfloat16)] * 4
    + [pltpu.VMEM((2, MICRO, ROWS // 2, D), jnp.bfloat16)] * 2
)
SHARD_SEMS = ([pltpu.SemaphoreType.DMA((4,))] * 2 + [pltpu.SemaphoreType.DMA((2, MICRO))] * 4) * 2


def shard_group(gathered, buffers, sems):
    part, pair, mine, theirs, crossed, held, held_sum = buffers
    gather = Gather(gathered, held, sems[:6])
    heads_sum = HeadSum(part, (pair, mine, theirs, crossed), held_sum, sems[6:])
    return gather, heads_sum, part


def attend(rows, gains, qkv, wo, by_offset, outs, bias, gather, heads_sum, part):
    normed_all, packed, mixed, middle = outs
    fill_bias(by_offset, bias)
    for m in range(MICRO):
        gather.hand_on(m)
    for m in range(MICRO):
        gather.finish(m)
        x = normed_all[m].reshape(LEN, D)
        q, k, v = [dot(x, qkv[which]).astype(jnp.bfloat16) for which in range(3)]
        packed[m, 0] = q
        packed[m, 1] = k
        packed[m, 2] = v
        if m:
            heads_sum.cross_over(m - 1)
        heads = []
        for head in range(HEADS_HERE):
            chances = softmax_rows(head_of(q, head), head_of(k, head), bias[head]).astype(jnp.bfloat16)
            heads.append(dot(chances, head_of(v, head)).astype(jnp.bfloat16))
        together = jnp.concatenate(heads, axis=1)
        mixed[m] = together
        part[m] = dot(together, wo[...]).astype(jnp.bfloat16).reshape(4, ROWS, D)
        heads_sum.start(m)
    heads_sum.cross_over(MICRO - 1)
    for m in range(MICRO):
        middle[m] = rows[m].astype(jnp.float32) + heads_sum.total(m)


def attend_back(
    middle_grad, rows, gains, normed_all, packed, mixed, qkv, wo, by_offset, outs, grad_all, dqkv, bias, gather, heads_sum, part
):
    input_grad, weight_grad, offset_grad, gain_grad = outs
    me = shard_places()[0]
    for m in range(MICRO):
        grad_all[m, me] = middle_grad[m].astype(jnp.bfloat16)
        gather.start(m)
    offset_grad[...] = jnp.zeros_like(offset_grad)
    row = lax.broadcasted_iota(jnp.int32, (LEN, LEN), 0)
    column = lax.broadcasted_iota(jnp.int32, (LEN, LEN), 1)
    backwards = (row + column == LEN - 1).astype(jnp.bfloat16)
    for m in range(MICRO):
        gather.hand_on(m)
    for m in range(MICRO):
        gather.finish(m)
        grad = grad_all[m].reshape(LEN, D)
        mixed_grad = dot(grad, wo[...], NT).astype(jnp.bfloat16)
        if m:
            heads_sum.cross_over(m - 1)
        q, k, v = packed[m, 0], packed[m, 1], packed[m, 2]
        q_grads, k_grads, v_grads = [], [], []
        for head in range(HEADS_HERE):
            q_head, k_head, v_head = head_of(q, head), head_of(k, head), head_of(v, head)
            grad_head = head_of(mixed_grad, head)
            chances = softmax_rows(q_head, k_head, bias[head])
            grad_chances = dot(grad_head, v_head, NT)
            weighed = jnp.sum(chances * grad_chances, axis=1, keepdims=True)
            grad_scores = (chances * (grad_chances - weighed)).astype(jnp.bfloat16)
            q_grads.append((dot(grad_scores, k_head) * 0.125).astype(jnp.bfloat16))
            k_grads.append((dot(grad_scores, q_head, TN) * 0.125).astype(jnp.bfloat16))
            v_grads.append(dot(chances.astype(jnp.bfloat16), grad_head, TN).astype(jnp.bfloat16))
            turned = dot(backwards, grad_scores)
            wide = jnp.concatenate([turned, jnp.zeros_like(turned)], axis=1)
            aligned = pltpu.roll(wide, 0, 1, stride=1, stride_axis=0)
            offset_grad[pl.ds(head, 1), :] += jnp.sum(aligned, axis=0, keepdims=True)
        grads = [jnp.concatenate(pieces, axis=1) for pieces in (q_grads, k_grads, v_grads)]
        for which in range(3):
            dqkv[m, which] = grads[which]
        summed = dot(grads[0], qkv[0], NT) + dot(grads[1], qkv[1], NT) + dot(grads[2], qkv[2], NT)
        part[m] = summed.astype(jnp.bfloat16).reshape(4, ROWS, D)
        heads_sum.start(m)
        if m:
            heads_sum.cross_over(m)
        x = normed_all[m].reshape(LEN, D)
        for which in range(4):
            left = dqkv[m, which] if which < 3 else mixed[m]
            added = dot(left, x if which < 3 else grad, TN)
            where = pl.ds(which * WIDTH, WIDTH)
            weight_grad[where, :] = added if m == 0 else weight_grad[where, :] + added
    gain_total = jnp.zeros((1, D), jnp.float32)
    for m in range(MICRO):
        back, gain_part = rms_norm_back(rows[m].astype(jnp.float32), gains[0:1, :], heads_sum.total(m))
        input_grad[m] = (middle_grad[m] + back).astype(jnp.bfloat16)
        gain_total = gain_total + gain_part
    gain_grad[...] = jnp.broadcast_to(gain_total, (8, D))


GROUP_ROWS = 16 * PIECE
SORTED = 16 * 4
WAVE_ROWS = 4 * SORTED
PAIRS = [(dx, dz) for dx in range(4) for dz in range(4) if dx or dz]


def sorting():
    order = np.zeros((GROUP_ROWS, GROUP_ROWS), np.float32)
    for e in range(2):
        for half in range(2):
            for sender in range(16):
                for at in range(4):
                    order[(e * 2 + half) * SORTED + sender * 4 + at, sender * PIECE + half * 8 + e * 4 + at] = 1
    return jnp.asarray(order, jnp.bfloat16), jnp.asarray(order.T, jnp.bfloat16)


def sender_halves(block):
    return [block.at[pl.ds(8 * half, 8)] for half in range(2)]


class SlotsOut:
    def __init__(self, slots, arrived, held, sems):
        self.slots, self.arrived = slots, arrived
        self.send_x, self.recv_x, self.send_y, self.recv_y = sems[:4]
        self.cross_link = Cross(held, sems[4:])
        self.me, self.core, self.cross, _ = shard_places()
        self.here, self.px, self.pz = expert_places()

    def away(self, w, dx, dz):
        at = w * 16 + dx * 4 + dz
        goal = owner_at(self.px, self.pz, dx, dz)
        return remote(
            self.slots.at[w, goal],
            self.arrived.at[self.me, w, self.here],
            self.send_x.at[at],
            self.recv_x.at[at],
            "expert",
            goal,
        )

    def piece(self, w, whose, kind):
        block = self.arrived.at[whose, w]
        at = WAVES * kind + w
        return remote(block, block, self.send_y.at[at], self.recv_y.at[at], "shard", self.core)

    def near(self, w):
        return self.piece(w, self.me, 0)

    def on(self, w):
        return self.piece(w, self.cross, 1)

    def start(self, w):
        for dx, dz in PAIRS:
            self.away(w, dx, dz).start()
        self.arrived[self.me, w, self.here] = self.slots[w, self.here]

    def sent(self, w):
        for dx, dz in PAIRS:
            self.away(w, dx, dz).wait_send()

    def spread_on(self, w):
        for dx, dz in PAIRS:
            self.away(w, dx, dz).wait_recv()
        block = sender_halves(self.arrived.at[self.me, w])
        self.cross_link.start(w, block, block)
        self.near(w).start()

    def hand_on(self, w):
        self.cross_link.wait_recv(w, sender_halves(self.arrived.at[self.cross, w]))
        self.on(w).start()

    def finish(self, w):
        self.near(w).wait_recv()
        self.on(w).wait_recv()

    def drain(self):
        for w in range(WAVES):
            self.cross_link.wait_send(w, sender_halves(self.arrived.at[self.me, w]))
            self.near(w).wait_send()
            self.on(w).wait_send()

    def goals(self, w):
        return [sender_halves(self.arrived.at[whose, w])[half] for half, whose in enumerate((self.me, self.cross))]

    def pass_on(self):
        for w in range(WAVES):
            self.cross_link.pass_on(w, self.goals(w))

    def passed(self):
        for w in range(WAVES):
            self.cross_link.passed(w, self.goals(w))


class SlotsBack:
    def __init__(self, part, returned, buffers, held, sems):
        self.part, self.returned = part, returned
        self.pair, self.mine, self.theirs, self.crossed, self.total = buffers
        self.send_x, self.recv_x, self.send_y, self.recv_y = sems[:4]
        self.cross_link = Cross(held, sems[4:])
        self.me, self.core, self.cross, self.diag = shard_places()
        self.here, self.px, self.pz = expert_places()

    def to_core(self, w, whose, buffer, kind):
        at = WAVES * kind + w
        return remote(self.part.at[whose, w], buffer.at[w], self.send_y.at[at], self.recv_y.at[at], "shard", self.core)

    def first(self, w):
        return self.to_core(w, self.diag, self.theirs, 0)

    def second(self, w):
        return self.to_core(w, self.core, self.mine, 1)

    def away(self, w, dx, dz):
        at = w * 16 + dx * 4 + dz
        goal = owner_at(self.px, self.pz, dx, dz)
        return remote(
            self.total.at[w, goal],
            self.returned.at[w, self.here],
            self.send_x.at[at],
            self.recv_x.at[at],
            "expert",
            goal,
        )

    def start(self, w):
        self.first(w).start()
        self.second(w).start()

    def cross_over(self, w):
        self.first(w).wait_recv()
        self.pair[w] = (self.part[self.cross, w].astype(jnp.float32) + self.theirs[w].astype(jnp.float32)).astype(
            jnp.bfloat16
        )
        self.cross_link.start(w, sender_halves(self.pair.at[w]), sender_halves(self.crossed.at[w]))

    def send_home(self, w):
        self.second(w).wait_recv()
        self.cross_link.wait_recv(w, sender_halves(self.crossed.at[w]))
        self.total[w] = (
            self.part[self.me, w].astype(jnp.float32)
            + self.mine[w].astype(jnp.float32)
            + self.crossed[w].astype(jnp.float32)
        ).astype(jnp.bfloat16)
        for dx, dz in PAIRS:
            self.away(w, dx, dz).start()
        self.returned[w, self.here] = self.total[w, self.here]

    def finish(self):
        for w in range(WAVES):
            for dx, dz in PAIRS:
                self.away(w, dx, dz).wait_recv()

    def drain(self):
        for w in range(WAVES):
            self.first(w).wait_send()
            self.second(w).wait_send()
            self.cross_link.wait_send(w, sender_halves(self.pair.at[w]))
            for dx, dz in PAIRS:
                self.away(w, dx, dz).wait_send()

    def pass_on(self):
        for w in range(WAVES):
            self.cross_link.pass_on(w, sender_halves(self.crossed.at[w]))

    def passed(self):
        for w in range(WAVES):
            self.cross_link.passed(w, sender_halves(self.crossed.at[w]))


def to_slots(spread, rows, slots):
    stacked = jnp.concatenate([rows[:, :HALF], rows[:, HALF:]], axis=0)
    slots[...] = dot(spread, stacked).astype(jnp.bfloat16).reshape(WAVES, OWNERS, PIECE, HALF)


def from_slots(spread_t, slots):
    stacked = dot(spread_t, slots[...].reshape(WAVES * OWNERS * PIECE, HALF))
    return jnp.concatenate([stacked[: MICRO * ROWS], stacked[MICRO * ROWS :]], axis=1)


def sort_in(order, arrived, w, rows, base):
    for group in range(4):
        picked = dot(order, arrived[group, w].reshape(GROUP_ROWS, HALF)).astype(jnp.bfloat16)
        for e in range(2):
            for half in range(2):
                at = (2 * e + half) * SORTED
                rows[e, pl.ds(base + group * SORTED, SORTED), half * HALF : (half + 1) * HALF] = picked[at : at + SORTED]


def sort_out(order_t, results, part, w):
    for group in range(4):
        where = slice(group * SORTED, (group + 1) * SORTED)
        pieces = [results[e, where, half * HALF : (half + 1) * HALF] for e in range(2) for half in range(2)]
        block = dot(order_t, jnp.concatenate(pieces, axis=0)).astype(jnp.bfloat16)
        part[group, w] = block.reshape(OWNERS, PIECE, HALF)


SCALE = 0.7978845608028654
CUBIC = 0.044715


def flat(rows):
    return rows.reshape(MICRO * ROWS, D)


SLOT_SEMS = (
    [pltpu.SemaphoreType.DMA((16 * WAVES,))] * 2
    + [pltpu.SemaphoreType.DMA((2 * WAVES,))] * 2
    + [pltpu.SemaphoreType.DMA((2, WAVES))] * 4
) * 2
SLOT_BUFFERS = (
    [pltpu.VMEM((WAVES, OWNERS, PIECE, HALF), jnp.bfloat16)] * 2
    + [pltpu.VMEM((4, WAVES, OWNERS, PIECE, HALF), jnp.bfloat16)]
    + [pltpu.VMEM((WAVES, OWNERS, PIECE, HALF), jnp.bfloat16)] * 5
    + [pltpu.VMEM((2, WAVES, 8, PIECE, HALF), jnp.bfloat16)] * 2
)


def slot_exchange(arrived, buffers, sems):
    slots, returned, part, pair, mine, theirs, crossed, total, held_out, held_back = buffers
    out = SlotsOut(slots, arrived, held_out, sems[:8])
    back = SlotsBack(part, returned, (pair, mine, theirs, crossed, total), held_back, sems[8:])
    return out, back


def pipeline(out, back, beside, compute):
    out.start(0)
    beside()
    out.sent(0)
    out.start(1)
    out.spread_on(0)
    out.sent(1)
    out.start(2)
    out.spread_on(1)
    out.hand_on(0)
    out.sent(2)
    out.spread_on(2)
    out.hand_on(1)
    out.finish(0)
    compute(0)
    back.start(0)
    out.hand_on(2)
    out.finish(1)
    back.cross_over(0)
    compute(1)
    back.start(1)
    out.finish(2)
    back.cross_over(1)
    back.send_home(0)
    compute(2)
    back.start(2)
    back.send_home(1)
    back.cross_over(2)


def experts(middle, gains, router, spread, spread_t, chosen, order, order_t, inner, outer, fetched, outs, arrived, results, out, back):
    rows, normed_two, router_prob, gating, expert_rows, output = outs
    normed = rms_norm(flat(middle[...]), gains[1:2, :]).astype(jnp.bfloat16)
    normed_two[...] = normed
    to_slots(spread[...], normed, out.slots)

    def beside():
        logits = dot(normed, router[...])
        raised = jnp.exp(logits - jnp.max(logits, axis=1, keepdims=True))
        prob = raised / jnp.sum(raised, axis=1, keepdims=True)
        router_prob[...] = prob
        gating[...] = jnp.sum(prob * chosen[...], axis=1, keepdims=True)
        fetched()

    def compute(w):
        sort_in(order[...], arrived, w, rows, w * WAVE_ROWS)

        def one_expert(e, _):
            pre = dot(rows[e, pl.ds(w * WAVE_ROWS, WAVE_ROWS), :], inner[e])
            hidden = 0.5 * pre * (1 + jnp.tanh(SCALE * (pre + CUBIC * pre * pre * pre)))
            results[e] = dot(hidden.astype(jnp.bfloat16), outer[e]).astype(jnp.bfloat16)
            return 0

        lax.fori_loop(0, 2, one_expert, 0)
        sort_out(order_t[...], results, back.part, w)

    pipeline(out, back, beside, compute)
    back.send_home(WAVES - 1)
    back.finish()
    found = from_slots(spread_t[...], back.returned)
    expert_rows[...] = found.astype(jnp.bfloat16)
    output[...] = (flat(middle[...]) + gating[...] * found).astype(jnp.bfloat16).reshape(MICRO, ROWS, D)


def experts_back(
    grad_out,
    middle,
    normed_two,
    router_prob,
    gating,
    expert_rows,
    gains,
    router,
    spread,
    spread_t,
    chosen,
    order,
    order_t,
    inner,
    outer,
    fetched,
    outs,
    middle_grad,
    grad_arrived,
    scratch,
    local,
    out,
    back,
):
    inner_grad, outer_grad, router_grad, gain_grad = outs
    rows, grads, hiddens, pre_grads, results, held = scratch
    grad = flat(grad_out[...]).astype(jnp.float32)
    to_slots(spread[...], (gating[...] * grad).astype(jnp.bfloat16), out.slots)
    gate_grad = jnp.sum(grad * expert_rows[...].astype(jnp.float32), axis=1, keepdims=True)
    logit_grad = ((gate_grad * gating[...]) * (chosen[...] - router_prob[...])).astype(jnp.bfloat16)

    def beside():
        router_grad[...] = dot(logit_grad, normed_two[...], TN)
        fetched()

    def compute(w):
        base = w * WAVE_ROWS
        where = pl.ds(base, WAVE_ROWS)
        sort_in(order[...], grad_arrived, w, grads, base)

        def one_expert(e, _):
            pre = dot(rows[e, where, :], inner[e])
            squared = pre * pre
            bent = jnp.tanh(SCALE * pre * (1 + CUBIC * squared))
            slope = 0.5 * (1 + bent) + 0.5 * pre * (1 - bent * bent) * SCALE * (1 + 3 * CUBIC * squared)
            hiddens[e, where, :] = (0.5 * pre * (1 + bent)).astype(jnp.bfloat16)
            pre_grad = (dot(grads[e, where, :], outer[e], NT) * slope).astype(jnp.bfloat16)
            pre_grads[e, where, :] = pre_grad
            results[e] = dot(pre_grad, inner[e], NT).astype(jnp.bfloat16)
            return 0

        lax.fori_loop(0, 2, one_expert, 0)
        sort_out(order_t[...], results, back.part, w)

    writes = []

    def weight_grads(number, left, right, goal):
        if number:
            writes.pop().wait()

        def one_expert(e, _):
            for at in range(0, D, 256):
                held[e, at : at + 256, :] = dot(left[e, :, at : at + 256], right[e], TN)
            return 0

        lax.fori_loop(0, 2, one_expert, 0)
        write = pltpu.make_async_copy(held, goal, local.at[number])
        write.start()
        writes.append(write)

    pipeline(out, back, beside, compute)
    weight_grads(0, rows, pre_grads, inner_grad)
    back.send_home(WAVES - 1)
    weight_grads(1, hiddens, grads, outer_grad)
    back.finish()
    normed_grad = dot(logit_grad, router[...], NT) + from_slots(spread_t[...], back.returned)
    value_grad, gain_part = rms_norm_back(flat(middle[...]), gains[1:2, :], normed_grad)
    middle_grad[...] = (grad + value_grad).reshape(MICRO, ROWS, D)
    gain_grad[...] = jnp.broadcast_to(gain_part, (8, D))
    return writes


def fetch(pairs, sems, first):
    copies = [pltpu.make_async_copy(source, goal, sems.at[first + n]) for n, (source, goal) in enumerate(pairs)]
    for copy in copies:
        copy.start()

    def fetched():
        for copy in copies:
            copy.wait()

    return fetched


def over_section(source, goal, sems, m):
    other = 1 - lax.axis_index("section")
    return remote(source.at[m], goal.at[m], sems.at[0, m], sems.at[1, m], "section", other)


def greet_active(moved):
    _, px, pz = expert_places()
    core = [{"shard": shard_places()[1]}]
    peer = [] if RELAY or not moved else [{"section": 1 - lax.axis_index("section")}]
    return greet(core + across() + peer + all_owners(px, pz))


def greet_idle(moved):
    if RELAY:
        greet(relays())()
    elif moved:
        greet([{"section": 1 - lax.axis_index("section")}])()


def hand_over(stages):
    if RELAY:
        for stage in stages:
            stage.pass_on()
        for stage in stages:
            stage.passed()


SECTION_SEM = pltpu.SemaphoreType.DMA((2, MICRO))
LOCAL_SEM = pltpu.SemaphoreType.DMA((12,))
ARRIVED = pltpu.VMEM((4, WAVES, OWNERS, PIECE, HALF), jnp.bfloat16)
WEIGHTS = [pltpu.VMEM((2, D, D), jnp.bfloat16)] * 2
FORWARD_OUTS = (
    jax.ShapeDtypeStruct((MICRO, 4, ROWS, D), jnp.bfloat16),
    jax.ShapeDtypeStruct((MICRO, 3, LEN, WIDTH), jnp.bfloat16),
    jax.ShapeDtypeStruct((MICRO, LEN, WIDTH), jnp.bfloat16),
    jax.ShapeDtypeStruct((MICRO, ROWS, D), jnp.float32),
    jax.ShapeDtypeStruct((2, WAVES * WAVE_ROWS, D), jnp.bfloat16),
    jax.ShapeDtypeStruct((MICRO * ROWS, D), jnp.bfloat16),
    jax.ShapeDtypeStruct((MICRO * ROWS, EXPERTS), jnp.float32),
    jax.ShapeDtypeStruct((MICRO * ROWS, 1), jnp.float32),
    jax.ShapeDtypeStruct((MICRO * ROWS, D), jnp.bfloat16),
    jax.ShapeDtypeStruct((MICRO, ROWS, D), jnp.bfloat16),
)


def forward_kernel(active, kept, own, gains, qkv, wo, by_offset, router, spread, spread_t, chosen, order, order_t, inner, outer, *refs):
    olds, refs = refs[: 10 * kept], refs[10 * kept :]
    outs, refs = refs[:10], refs[10:]
    received, refs = refs[:kept], refs[kept:]
    bias, inner_here, outer_here, arrived, results, section, local = refs[:7]
    shard_buffers, slot_buffers, shard_sems, slot_sems = refs[7:14], refs[14:24], refs[24:36], refs[36:]
    gather, heads_sum, part = shard_group(outs[0], shard_buffers, shard_sems)
    out, back = slot_exchange(arrived, slot_buffers, slot_sems)
    incoming = received[0] if kept else own

    def run():
        ready = greet_active(kept)
        fetched = fetch([(inner, inner_here), (outer, outer_here)], local, 0)
        ready()
        me = shard_places()[0]
        for m in range(MICRO):
            if kept:
                over_section(olds[9], incoming, section, m).wait_recv()
            outs[0][m, me] = rms_norm(incoming[m].astype(jnp.float32), gains[0:1, :]).astype(jnp.bfloat16)
            gather.start(m)
        attend(incoming, gains, qkv, wo, by_offset, outs[:4], bias, gather, heads_sum, part)
        routing = (gains, router, spread, spread_t, chosen, order, order_t, inner_here, outer_here)
        experts(outs[3], *routing, fetched, outs[4:], arrived, results, out, back)
        for stage in (gather, heads_sum, out, back):
            stage.drain()

    def rest():
        done = keep_old(olds[:9], outs[:9], local, None)
        greet_idle(kept)
        if kept:
            for m in range(MICRO):
                over_section(olds[9], incoming, section, m).start()
            incoming[...] = own[...]
        hand_over((gather, heads_sum, out, back))
        if kept:
            for m in range(MICRO):
                over_section(olds[9], incoming, section, m).wait_send()
        done()

    when_active(active, run, rest)


def layer_forward(own, common, olds, active, collective_id):
    kept = olds is not None
    return pl.pallas_call(
        functools.partial(forward_kernel, active, int(kept)),
        out_shape=FORWARD_OUTS + ((jax.ShapeDtypeStruct((MICRO, ROWS, D), jnp.bfloat16),) if kept else ()),
        in_specs=[VMEM] * 11 + [ANY] * (12 if kept else 2),
        out_specs=(VMEM,) * (11 if kept else 10),
        scratch_shapes=[pltpu.VMEM((HEADS_HERE, LEN, LEN), jnp.float32)]
        + WEIGHTS
        + [ARRIVED, pltpu.VMEM((2, WAVE_ROWS, D), jnp.bfloat16), SECTION_SEM, LOCAL_SEM]
        + SHARD_BUFFERS
        + SLOT_BUFFERS
        + SHARD_SEMS
        + SLOT_SEMS,
        compiler_params=pltpu.CompilerParams(
            collective_id=collective_id, has_side_effects=True, vmem_limit_bytes=VMEM_BYTES
        ),
        name="layer_forward",
    )(own, *common, *(olds or ()))


BACKWARD_OUTS = (
    jax.ShapeDtypeStruct((2, D, D), jnp.float32),
    jax.ShapeDtypeStruct((2, D, D), jnp.float32),
    jax.ShapeDtypeStruct((EXPERTS, D), jnp.float32),
    jax.ShapeDtypeStruct((8, D), jnp.float32),
    jax.ShapeDtypeStruct((4 * WIDTH, D), jnp.float32),
    jax.ShapeDtypeStruct((8, 2 * LEN), jnp.float32),
    jax.ShapeDtypeStruct((8, D), jnp.float32),
    jax.ShapeDtypeStruct((MICRO, ROWS, D), jnp.bfloat16),
)


def backward_kernel(
    active,
    kept,
    own,
    gains,
    qkv,
    wo,
    by_offset,
    router,
    spread,
    spread_t,
    chosen,
    order,
    order_t,
    inner,
    outer,
    normed_all,
    packed,
    mixed,
    middle,
    saved_rows,
    normed_two,
    router_prob,
    gating,
    expert_rows,
    incoming,
    *refs,
):
    olds, refs = refs[: 8 * kept], refs[8 * kept :]
    outs, refs = refs[:8], refs[8:]
    received, middle_grad, grad_arrived, grad_all, dqkv, bias, inner_here, outer_here, section, local = refs[:10]
    scratch, shard_buffers, slot_buffers = refs[10:16], refs[16:23], refs[23:33]
    shard_sems, slot_sems = refs[33:45], refs[45:]
    gather, heads_sum, part = shard_group(grad_all, shard_buffers, shard_sems)
    out, back = slot_exchange(grad_arrived, slot_buffers, slot_sems)
    grad_out = received if kept else own

    def run():
        ready = greet_active(kept)
        fetched = fetch([(inner, inner_here), (outer, outer_here), (saved_rows, scratch[0])], local, 2)
        fill_bias(by_offset, bias)
        ready()
        if kept:
            for m in range(MICRO):
                over_section(olds[7], grad_out, section, m).wait_recv()
        writes = experts_back(
            grad_out,
            middle,
            normed_two,
            router_prob,
            gating,
            expert_rows,
            gains,
            router,
            spread,
            spread_t,
            chosen,
            order,
            order_t,
            inner_here,
            outer_here,
            fetched,
            outs[:4],
            middle_grad,
            grad_arrived,
            scratch,
            local,
            out,
            back,
        )
        attend_back(
            middle_grad,
            incoming,
            gains,
            normed_all,
            packed,
            mixed,
            qkv,
            wo,
            by_offset,
            (outs[7], outs[4], outs[5], outs[6]),
            grad_all,
            dqkv,
            bias,
            gather,
            heads_sum,
            part,
        )
        for stage in (out, back, gather, heads_sum):
            stage.drain()
        for write in writes:
            write.wait()

    def rest():
        done = keep_old(olds[:7], outs[:7], local, scratch[5])
        greet_idle(kept)
        if kept:
            for m in range(MICRO):
                over_section(olds[7], grad_out, section, m).start()
        hand_over((out, back, gather, heads_sum))
        if kept:
            for m in range(MICRO):
                over_section(olds[7], grad_out, section, m).wait_send()
        done()

    when_active(active, run, rest)


def layer_backward(own, common, saved, olds, active, collective_id):
    kept = olds is not None
    all_rows = pltpu.VMEM((2, WAVES * WAVE_ROWS, D), jnp.bfloat16)
    return pl.pallas_call(
        functools.partial(backward_kernel, active, int(kept)),
        out_shape=BACKWARD_OUTS,
        in_specs=[VMEM] * 11 + [ANY] * 2 + [VMEM] * 4 + [ANY] + [VMEM] * 5 + [ANY] * (8 if kept else 0),
        out_specs=(ANY, ANY) + (VMEM,) * 6,
        scratch_shapes=[
            pltpu.VMEM((MICRO, ROWS, D), jnp.bfloat16),
            pltpu.VMEM((MICRO, ROWS, D), jnp.float32),
            ARRIVED,
            pltpu.VMEM((MICRO, 4, ROWS, D), jnp.bfloat16),
            pltpu.VMEM((MICRO, 3, LEN, WIDTH), jnp.bfloat16),
            pltpu.VMEM((HEADS_HERE, LEN, LEN), jnp.float32),
        ]
        + WEIGHTS
        + [SECTION_SEM, LOCAL_SEM]
        + [all_rows] * 4
        + [pltpu.VMEM((2, WAVE_ROWS, D), jnp.bfloat16), pltpu.VMEM((2, D, D), jnp.float32)]
        + SHARD_BUFFERS
        + SLOT_BUFFERS
        + SHARD_SEMS
        + SLOT_SEMS,
        compiler_params=pltpu.CompilerParams(
            collective_id=collective_id, has_side_effects=True, vmem_limit_bytes=VMEM_BYTES
        ),
        name="layer_backward",
    )(own, *common, *saved, *(olds or ()))


def reduce_kernel(big, small, table, big_out, small_out, table_out, *refs):
    big_in, big_sum, pair, small_have, small_in, small_sum, table_in, local, sends, recvs, pair_send, pair_recv = refs
    me, core, cross, diag = shard_places()
    here, px, pz = expert_places()
    greet([{"shard": core}, {"shard": cross}] + all_owners(px, pz))()
    others = [(dx * 4 + dz, owner_at(px, pz, dx, dz)) for dx in range(4) for dz in range(4) if dx or dz]
    first = []
    for at, goal in others:
        first.append(remote(big.at[goal], big_in.at[here], sends.at[0, at], recvs.at[0, at], "expert", goal))
        first[-1].start()
        first.append(remote(table, table_in.at[here], sends.at[1, at], recvs.at[1, at], "expert", goal))
        first[-1].start()
    table_in[here] = table[...]
    near = remote(small, pair.at[0], pair_send.at[0], pair_recv.at[0], "shard", core)
    near.start()
    near.wait()
    small_have[...] = small[...] + pair[0]
    far = remote(small_have, pair.at[1], pair_send.at[1], pair_recv.at[1], "shard", cross)
    far.start()
    far.wait()
    small_have[...] = small_have[...] + pair[1]
    second = []
    for at, goal in others:
        second.append(
            remote(small_have.at[goal], small_in.at[here], sends.at[2, at], recvs.at[2, at], "expert", goal)
        )
        second[-1].start()
    small_in[here] = small_have[here]
    big_in[here] = big[here]
    for copy in first:
        copy.wait()
    big_sum[...] = jnp.sum(big_in[...].astype(jnp.float32), axis=0).astype(jnp.bfloat16)
    third = []
    for at, goal in others:
        third.append(remote(big_sum, big_out.at[here], sends.at[3, at], recvs.at[3, at], "expert", goal))
        third[-1].start()
    own = pltpu.make_async_copy(big_sum, big_out.at[here], local.at[0])
    own.start()
    for copy in second:
        copy.wait()
    small_sum[...] = jnp.sum(small_in[...], axis=0)
    for at, goal in others:
        third.append(remote(small_sum, small_out.at[here], sends.at[4, at], recvs.at[4, at], "expert", goal))
        third[-1].start()
    own_small = pltpu.make_async_copy(small_sum, small_out.at[here], local.at[1])
    own_small.start()
    table_out[...] = jnp.sum(table_in[...], axis=0)
    own.wait()
    own_small.wait()
    for copy in third:
        copy.wait()


def reduce_all(big, small, table, collective_id):
    return pl.pallas_call(
        reduce_kernel,
        out_shape=(
            jax.ShapeDtypeStruct(big.shape, big.dtype),
            jax.ShapeDtypeStruct(small.shape, small.dtype),
            jax.ShapeDtypeStruct(table.shape, table.dtype),
        ),
        in_specs=[VMEM] * 3,
        out_specs=(ANY, ANY, VMEM),
        scratch_shapes=[
            pltpu.VMEM(big.shape, big.dtype),
            pltpu.VMEM(big.shape[1:], big.dtype),
            pltpu.VMEM((2,) + small.shape, small.dtype),
            pltpu.VMEM(small.shape, small.dtype),
            pltpu.VMEM(small.shape, small.dtype),
            pltpu.VMEM(small.shape[1:], small.dtype),
            pltpu.VMEM((OWNERS,) + table.shape, table.dtype),
            pltpu.SemaphoreType.DMA((2,)),
            pltpu.SemaphoreType.DMA((5, 16)),
            pltpu.SemaphoreType.DMA((5, 16)),
            pltpu.SemaphoreType.DMA((2,)),
            pltpu.SemaphoreType.DMA((2,)),
        ],
        compiler_params=pltpu.CompilerParams(
            collective_id=collective_id, has_side_effects=True, vmem_limit_bytes=VMEM_BYTES
        ),
        name="reduce_all",
    )(big, small, table)


def bucket_of(offsets):
    distance = jnp.abs(offsets)
    far_bucket = 8 + sum(
        ((distance >= threshold).astype(jnp.int32) for threshold in (12, 16, 23, 32, 46, 64, 91))
    )
    near_far = jnp.where(distance < 8, distance, far_bucket)
    return near_far + 16 * (offsets > 0).astype(jnp.int32)


def offset_buckets():
    offsets = jnp.arange(2 * LEN, dtype=jnp.int32) - (LEN - 1)
    return (bucket_of(offsets)[:, None] == jnp.arange(32, dtype=jnp.int32)[None, :]).astype(jnp.float32)


def spread_matrices(route_ids, slot_ids):
    row = jnp.arange(WAVES * OWNERS * PIECE, dtype=jnp.int32)
    half, expert = row % 16 // 8, row % 8 // 4
    slot_row = row // (OWNERS * PIECE) * 4 + row % 4
    row_key = (half * EXPERTS + row // PIECE % OWNERS * 2 + expert) * (MICRO * CAP) + slot_row
    micro = jnp.arange(MICRO, dtype=jnp.int32)[:, None]
    token_key = (route_ids * (MICRO * CAP) + micro * CAP + slot_ids).reshape(-1)
    column_key = jnp.concatenate([token_key, token_key + EXPERTS * MICRO * CAP])
    return (
        (row_key[:, None] == column_key[None, :]).astype(jnp.bfloat16),
        (column_key[:, None] == row_key[None, :]).astype(jnp.bfloat16),
    )


def per_device(
    stream, norm_gains, attn_qkv, attn_out, rel_bias, router, expert_in, expert_out, routes, slots
):
    buckets = offset_buckets()
    by_offset = lax.dot_general(
        rel_bias[0], buckets, (((0,), (1,)), ((), ())), precision=lax.Precision.HIGHEST
    )
    by_offset = jnp.concatenate([by_offset, jnp.zeros((5, 2 * LEN), jnp.float32)], axis=0)
    chosen = (routes[0].reshape(-1)[:, None] == jnp.arange(EXPERTS, dtype=jnp.int32)[None, :]).astype(jnp.float32)
    common = (norm_gains[0], attn_qkv[0], attn_out[0], by_offset, router[0])
    common += spread_matrices(routes[0], slots[0]) + (chosen,) + sorting() + (expert_in[0], expert_out[0])
    is_first = lax.axis_index("section") == 0
    own = stream[0]

    early = layer_forward(own, common, None, 0, 0)
    *saved, output, incoming = layer_forward(own, common, early, 1, 1)
    saved = (*saved, incoming)
    late = layer_backward(own, common, saved, None, 1, 2)
    grads = layer_backward(own, common, saved, late, 0, 3)
    inner_grad, outer_grad, router_grad, gain_two, attend_grad, offset_grad, gain_one, input_grad = grads

    big = attend_grad.astype(jnp.bfloat16).reshape(OWNERS, 48, D)
    small = jnp.concatenate([router_grad, gain_one[:1], gain_two[:1]], axis=0)
    small = jnp.pad(small.reshape(-1), (0, 32768 - 34 * D))
    table = jnp.dot(offset_grad[:3], buckets, precision=lax.Precision.HIGHEST)
    table = jnp.pad(table, ((0, 5), (0, 96)))
    big, small, table = reduce_all(big, small.reshape(OWNERS, 8, 256), table, 4)
    big = big.reshape(4, WIDTH, D).astype(jnp.float32)
    small = small.reshape(-1)[: 34 * D].reshape(34, D)
    end_rows = jnp.where(is_first, input_grad, output)
    return (
        end_rows[None],
        small[32:][None],
        jnp.swapaxes(big[:3], 1, 2)[None],
        big[3][None],
        table[:3, :32].T[None],
        small[:32].T[None],
        inner_grad[None],
        outer_grad[None],
    )


def solution(mesh):
    return jax.shard_map(
        per_device,
        mesh=mesh,
        in_specs=(
            P("section", None, ("expert", "shard"), None),
            P("section", None, None),
            P("section", None, None, "shard"),
            P("section", "shard", None),
            P("section", None, "shard"),
            P("section", None, None),
            P("section", "expert", None, "shard"),
            P("section", "expert", "shard", None),
            P("section", None, ("expert", "shard")),
            P("section", None, ("expert", "shard")),
        ),
        out_specs=(
            P("section", None, ("expert", "shard"), None),
            P("section", None, None),
            P("section", None, None, "shard"),
            P("section", "shard", None),
            P("section", None, "shard"),
            P("section", None, None),
            P("section", "expert", None, "shard"),
            P("section", "expert", "shard", None),
        ),
        check_vma=False,
    )
```

time: 1730 us -> 452 us (0.26)
  waiting for transfers between devices: 775 us -> 0 us
  blocking collectives: 419 us -> 0 us
  Pallas kernels: 0 us -> 416 us
  local copies, waits for them, and re-layouts: 217 us -> 18.7 us
  matrix products: 160 us -> 1.49 us
  other arithmetic: 98.3 us -> 8.28 us
  starting transfers between devices: 37.3 us -> 0 us
    pallas_call x0 -> x5, Pallas kernels: none -> 416 us  [the longest x2 259 us: layer_backward(): pl.pallas_call(functools.partial(backward_kernel, active, int(kept)), out...]
    psum x2 -> x0, waiting for transfers between devices: 350 us -> none  [the longest x1 350 us: per_device(): lax.psum((gain_grad, router_grad), ('expert', 'shard'))]
    reduce_scatter x12 -> x0, waiting for transfers between devices: 237 us -> none  [the longest x6 118 us: expert_pass(): lax.psum_scatter(returned.astype(jnp.bfloat16), 'shard', scatter_dimensio...]
    psum x2 -> x0, blocking collectives: 206 us -> none  [the longest x1 165 us: per_device(): lax.psum((gain_grad, router_grad), ('expert', 'shard'))]
    all_to_all x7 -> x0, blocking collectives: 156 us -> none  [the longest x5 104 us: expert_pass(): lax.all_to_all(partial_value.astype(jnp.bfloat16), 'expert', split_axis=0...]
    dot_general x79 -> x2, matrix products: 156 us -> 1.49 us  [the longest x1 1.12 us: per_device(): lax.dot_general(rel_bias[0], buckets, (((0,), (1,)), ((), ())), precision...]
    all_gather x6 -> x0, waiting for transfers between devices: 109 us -> none  [expert_pass(): source = lax.all_gather(buffer, 'shard', axis=0, tiled=True)]
    reshape x14 -> x2, local copies, waits for them, and re-layouts: 87.6 us -> 0.7 us  [the longest x1 0.69 us: per_device(): big, small, table = reduce_all(big, small.reshape(OWNERS, 8, 256), table, 4)]
  transfers between devices with their start and end apart: 29 -> 0, of which waited for: 24 -> 0; matrix products, arithmetic and copies ran while one was open for 15% -> 0% of each run, Pallas kernels for 0% -> 0%
where the time goes in v2:
time: 452 us; the launch traced here: 445 us
  Pallas kernels  416 us (92%)
  local copies, waits for them, and re-layouts  18.7 us (4%)
  other arithmetic  8.28 us (2%)
    pallas_call x2, Pallas kernels, layer_backward(): pl.pallas_call(functools.partial(backward_kernel, active, int(kept)), out...  259 us
    pallas_call x2, Pallas kernels, layer_forward(): pl.pallas_call(functools.partial(forward_kernel, active, int(kept)), out_...  114 us
    pallas_call x1, Pallas kernels, reduce_all(): pl.pallas_call(reduce_kernel, out_shape=(jax.ShapeDtypeStruct(big.shape,...  41.9 us
    unnamed x28, local copies, waits for them, and re-layouts  10.4 us

profile of v2, /device:TPU:0, one launch (start us, length us, event | category | flops | bytes accessed | tf_op | source)
XLA Modules:
  0.0 445.2 jit_solution(5045335444211922721)
XLA Ops:
  0.6 0.0 copy-start.6
  0.7 0.8 broadcast_add_fusion
  1.5 1.1 compare_convert_fusion.spread_t
  2.6 1.1 compare_convert_fusion.1.spread
  3.7 1.1 convolution_bitcast_fusion
  4.8 0.6 concatenate.9.by_offset
  5.5 1.4 copy.20
  6.9 0.8 copy.21
  7.7 0.0 copy-done.6
  7.7 0.8 fusion.3.chosen
  8.5 90.5 %layer_forward.2 = (bf16[2,4,128,768]{3,2,1,0:T(8,128)(2,1)}, bf16[2,3,512,192]{3,2,1,0:T(8,128)(2,1)}, bf16[2,512,192]{2,1,0:T(8,128)(2,1)}, f32[2,128,768]{2,1...) custom-call(bf16[2,128,768]{2,1,0:T(8,128)(2,1)} %bitcast.55, ...), custom_call_target="tpu_custom_call" | custom-call | tf_op jit(solution)/shard_map/layer_forward/pallas_call | solution.py:855
  98.9 23.9 %layer_forward.3 = (bf16[2,4,128,768]{3,2,1,0:T(8,128)(2,1)}, bf16[2,3,512,192]{3,2,1,0:T(8,128)(2,1)}, bf16[2,512,192]{2,1,0:T(8,128)(2,1)}, f32[2,128,768]{2,1...) custom-call(bf16[2,128,768]{2,1,0:T(8,128)(2,1)} %bitcast.56, ...), custom_call_target="tpu_custom_call" | custom-call | tf_op jit(solution)/shard_map/layer_forward/pallas_call | solution.py:855
  122.9 16.7 %layer_backward.2 = (f32[2,768,768]{2,1,0:T(8,128)}, f32[2,768,768]{2,1,0:T(8,128)}, f32[32,768]{1,0:T(8,128)}, f32[8,768]{1,0:T(8,128)}, f32[768,768]{1,0:T(8,1...) custom-call(bf16[2,128,768]{2,1,0:T(8,128)(2,1)} %bitcast.57, f32[2,768]{1,0:T(2,128)} %bitcast.78, ...), custom_call_target="tpu_custom_call" | custom-call | tf_op jit(solution)/shard_map/layer_backward/pallas_call | solution.py:997
  139.5 242.7 %layer_backward.3 = (f32[2,768,768]{2,1,0:T(8,128)}, f32[2,768,768]{2,1,0:T(8,128)}, f32[32,768]{1,0:T(8,128)}, f32[8,768]{1,0:T(8,128)}, f32[768,768]{1,0:T(8,1...) custom-call(bf16[2,128,768]{2,1,0:T(8,128)(2,1)} %bitcast.58, f32[2,768]{1,0:T(2,128)} %bitcast.79, ...), custom_call_target="tpu_custom_call" | custom-call | tf_op jit(solution)/shard_map/layer_backward/pallas_call | solution.py:997
  382.3 0.7 slice.44
  383.0 0.7 slice.45
  383.8 0.9 pad_maximum_fusion
  384.7 0.7 reshape.269.small
  385.4 2.8 convert_element_type.95
  388.2 0.4 fusion
  388.6 0.6 pad.10.table
  389.2 41.9 %reduce_all.1 = (bf16[16,48,768]{2,1,0:T(8,128)(2,1)}, f32[16,8,256]{2,1,0:T(8,128)}, f32[8,128]{1,0:T(8,128)}) custom-call(bf16[16,48,768]{2,1,0:T(8,128)(2,1)} %bitcast.63, f32[16,8,256]{2,1,0:T(8,128)} %reshape.269.small, f32[8,128]{1,0:T(8,128)} %pad.10.table), custom_call_target="tpu_custom_call" | custom-call | tf_op jit(solution)/shard_map/reduce_all/pallas_call | solution.py:1079
  431.1 2.7 slice.57
  433.8 0.9 slice.58
  434.7 0.7 slice.55
  435.4 0.1 copy.24
  435.5 0.6 slice.48
  436.1 0.0 copy-done.7
  436.1 0.6 copy.22
  436.6 0.8 select_bitcast_fusion
  437.4 5.4 %copy.31 = f32[1,2,768,768]{3,2,1,0:T(8,128)} copy(f32[1,2,768,768]{3,2,1,0:T(8,128)} %bitcast.67) | data formatting | bytes 9437184
  442.8 2.2 copy.32
  (29 shorter events, 0.1 us)
Async XLA Ops:
  0.6 7.1 %copy-start.6 = (s32[1,2,128]{2,1,0:T(2,128)S(1)}, s32[1,2,128]{2,1,0:T(2,128)}, u32[]{:S(2)}) copy-start(s32[1,2,128]{2,1,0:T(2,128)} %param.20) | copy-start | bytes 3076
  0.6 4.8 %copy-start.1 = (bf16[1,3,768,192]{2,3,1,0:T(8,128)(2,1)S(1)}, bf16[1,3,768,192]{2,3,1,0:T(8,128)(2,1)}, u32[]{:S(2)}) copy-start(bf16[1,3,768,192]{2,3,1,0:T(8,128)(2,1)} %param.14) | copy-start | bytes 2654212
  0.7 6.2 %copy-start.5 = (bf16[1,768,32]{1,2,0:T(8,128)(2,1)S(1)}, bf16[1,768,32]{1,2,0:T(8,128)(2,1)}, u32[]{:S(2)}) copy-start(bf16[1,768,32]{1,2,0:T(8,128)(2,1)} %param.17) | copy-start | bytes 147460
  382.3 5.9 %copy-start.8 = (f32[8,1024]{1,0:T(8,128)S(1)}, f32[8,1024]{1,0:T(8,128)}, u32[]{:S(2)}) copy-start(f32[8,1024]{1,0:T(8,128)} %get-tuple-element.82) | copy-start | bytes 98308
  431.1 2.7 copy-start
  431.1 3.6 copy-start.2
  431.1 4.9 %copy-start.7 = (f32[8,128]{1,0:T(8,128)S(1)}, f32[8,128]{1,0:T(8,128)}, u32[]{:S(2)}) copy-start(f32[8,128]{1,0:T(8,128)} %get-tuple-element.85) | copy-start | bytes 12292
  431.1 5.5 %copy-start.3 = (bf16[2,128,768]{2,1,0:T(8,128)(2,1)S(1)}, bf16[2,128,768]{2,1,0:T(8,128)(2,1)}, u32[]{:S(2)}) copy-start(bf16[2,128,768]{2,1,0:T(8,128)(2,1)} %get-tuple-element.77) | copy-start | bytes 1179652
  431.1 5.5 %copy-start.4 = (bf16[2,128,768]{2,1,0:T(8,128)(2,1)S(1)}, bf16[2,128,768]{2,1,0:T(8,128)(2,1)}, u32[]{:S(2)}) copy-start(bf16[2,128,768]{2,1,0:T(8,128)(2,1)} %get-tuple-element.76) | copy-start | bytes 1179652
  436.6 6.1 %slice-start = ((s8[4718592]{0:T(1024)(128)(4,1)}), s8[4194304]{0:T(1024)(128)(4,1)S(1)}, s32[]{:S(2)}) async-start(s8[4718592]{0:T(1024)(128)(4,1)} %bitcast.64), calls=%async_computation | async-start | bytes 8388608
  437.4 5.4 %slice-start.1 = ((s8[4718592]{0:T(1024)(128)(4,1)}), s8[524288]{0:T(1024)(128)(4,1)S(1)}, s32[]{:S(2)}) async-start(s8[4718592]{0:T(1024)(128)(4,1)} %bitcast.64), calls=%async_computation.1 | async-start | bytes 1048576

commit v3 on v2

v3 whole, which is shorter than its diff:
```python
import functools

import jax
import jax.numpy as jnp
import numpy as np
from jax import lax
from jax.experimental import pallas as pl
from jax.experimental.pallas import tpu as pltpu
from jax.sharding import PartitionSpec as P

HEAD_DIM = 64
HEADS_HERE = 3
LEN = 512
MICRO = 2
ROWS = 128
D = 768
HALF = 384
EXPERTS = 32
CAP = 6
OWNERS = 16
WAVES = 3
PIECE = 16
VMEM_BYTES = 60 * 1024 * 1024
MESH = pl.DeviceIdType.MESH
ANY = pl.BlockSpec(memory_space=pl.ANY)
VMEM = pl.BlockSpec(memory_space=pltpu.VMEM)


def remote_to(src, dst, send, recv, device):
    return pltpu.make_async_remote_copy(
        src_ref=src, dst_ref=dst, send_sem=send, recv_sem=recv, device_id=device, device_id_type=MESH
    )


def remote(src, dst, send, recv, axis, index):
    return remote_to(src, dst, send, recv, {axis: index})


def greet(partners):
    barrier = pltpu.get_barrier_semaphore()
    for device in partners:
        pl.semaphore_signal(barrier, inc=1, device_id=device, device_id_type=MESH)
    return lambda: pl.semaphore_wait(barrier, len(partners))


def shard_places():
    me = lax.axis_index("shard")
    y, core = lax.div(me, 2), lax.rem(me, 2)
    return me, 2 * y + (1 - core), 2 * (1 - y) + core, 2 * (1 - y) + (1 - core)


def expert_places():
    me = lax.axis_index("expert")
    return me, lax.div(me, 4), lax.rem(me, 4)


def owner_at(x, z, dx, dz):
    return lax.rem(x + dx, 4) * 4 + lax.rem(z + dz, 4)


def all_owners(x, z):
    return [{"expert": owner_at(x, z, dx, dz)} for dx in range(4) for dz in range(4) if dx or dz]


class Cross:
    def __init__(self, sems):
        self.send, self.recv = sems
        self.device = {"shard": shard_places()[2]}

    def to(self, n, half, source, goal):
        return remote_to(source, goal, self.send.at[half, n], self.recv.at[half, n], self.device)

    def start(self, n, sources, goals):
        for half in range(2):
            self.to(n, half, sources[half], goals[half]).start()

    def wait_recv(self, n, goals):
        for half in range(2):
            self.to(n, half, goals[half], goals[half]).wait_recv()

    def wait_send(self, n, sources):
        for half in range(2):
            self.to(n, half, sources[half], sources[half]).wait_send()


def copy_all(sources, goals, sems, first=0):
    copies = [
        pltpu.make_async_copy(source, goal, sems.at[first + n]) for n, (source, goal) in enumerate(zip(sources, goals))
    ]
    for copy in copies:
        copy.start()

    def done():
        for copy in copies:
            copy.wait()

    return done


def dot(a, b, dims=((1,), (0,))):
    return lax.dot_general(a, b, (dims, ((), ())), preferred_element_type=jnp.float32)


NT = ((1,), (1,))
TN = ((0,), (0,))
WIDTH = HEADS_HERE * HEAD_DIM


def rms_norm(values, gain):
    return values * lax.rsqrt(jnp.mean(values * values, axis=-1, keepdims=True) + 1e-06) * gain


def rms_norm_back(values, gain, grad):
    scale = lax.rsqrt(jnp.mean(values * values, axis=-1, keepdims=True) + 1e-06)
    unit = values * scale
    unit_grad = grad * gain
    value_grad = scale * (unit_grad - unit * jnp.mean(unit_grad * unit, axis=-1, keepdims=True))
    return value_grad, jnp.sum(grad * unit, axis=0, keepdims=True)


def fill_bias(by_offset, bias):
    for head in range(HEADS_HERE):
        spread = jnp.broadcast_to(by_offset[pl.ds(head, 1), :], (LEN, 2 * LEN))
        bias[head] = pltpu.roll(spread, LEN + 1, 1, stride=1, stride_axis=0)[:, :LEN]


def head_of(array, head):
    return array[:, head * HEAD_DIM : (head + 1) * HEAD_DIM]


def softmax_rows(queries, keys, bias):
    scores = dot(queries, keys, NT) * 0.125 + bias
    raised = jnp.exp(scores - jnp.max(scores, axis=1, keepdims=True))
    return raised / jnp.sum(raised, axis=1, keepdims=True)


def row_halves(block):
    return [block.at[pl.ds(half * ROWS // 2, ROWS // 2)] for half in range(2)]


class Gather:
    def __init__(self, rows, sems):
        self.rows, self.send, self.recv = rows, sems[0], sems[1]
        self.cross_link = Cross(sems[2:])
        self.me, self.core, self.cross, _ = shard_places()

    def piece(self, m, whose, kind):
        block = self.rows.at[m, whose]
        at = 2 * kind + m
        return remote(block, block, self.send.at[at], self.recv.at[at], "shard", self.core)

    def start(self, m):
        block = row_halves(self.rows.at[m, self.me])
        self.cross_link.start(m, block, block)
        self.near(m).start()

    def near(self, m):
        return self.piece(m, self.me, 0)

    def on(self, m):
        return self.piece(m, self.cross, 1)

    def hand_on(self, m):
        self.cross_link.wait_recv(m, row_halves(self.rows.at[m, self.cross]))
        self.on(m).start()

    def finish(self, m):
        self.near(m).wait_recv()
        self.on(m).wait_recv()

    def drain(self):
        for m in range(MICRO):
            self.cross_link.wait_send(m, row_halves(self.rows.at[m, self.me]))
            self.near(m).wait_send()
            self.on(m).wait_send()


class HeadSum:
    def __init__(self, part, buffers, sems):
        self.part, self.send, self.recv = part, sems[0], sems[1]
        self.cross_link = Cross(sems[2:])
        self.pair, self.mine, self.theirs, self.crossed = buffers
        self.me, self.core, self.cross, self.diag = shard_places()

    def first(self, m):
        return remote(self.part.at[m, self.diag], self.theirs.at[m], self.send.at[m], self.recv.at[m], "shard", self.core)

    def second(self, m):
        return remote(
            self.part.at[m, self.core], self.mine.at[m], self.send.at[2 + m], self.recv.at[2 + m], "shard", self.core
        )

    def start(self, m):
        self.first(m).start()
        self.second(m).start()

    def cross_over(self, m):
        self.first(m).wait_recv()
        self.pair[m] = (self.part[m, self.cross].astype(jnp.float32) + self.theirs[m].astype(jnp.float32)).astype(
            jnp.bfloat16
        )
        self.cross_link.start(m, row_halves(self.pair.at[m]), row_halves(self.crossed.at[m]))

    def total(self, m):
        self.second(m).wait_recv()
        self.cross_link.wait_recv(m, row_halves(self.crossed.at[m]))
        return (
            self.part[m, self.me].astype(jnp.float32)
            + self.mine[m].astype(jnp.float32)
            + self.crossed[m].astype(jnp.float32)
        )

    def drain(self):
        for m in range(MICRO):
            self.first(m).wait_send()
            self.second(m).wait_send()
            self.cross_link.wait_send(m, row_halves(self.pair.at[m]))


SHARD_BUFFERS = (
    [pltpu.VMEM((MICRO, 4, ROWS, D), jnp.bfloat16)]
    + [pltpu.VMEM((MICRO, ROWS, D), jnp.bfloat16)] * 4
)
SHARD_SEMS = ([pltpu.SemaphoreType.DMA((4,))] * 2 + [pltpu.SemaphoreType.DMA((2, MICRO))] * 2) * 2


def shard_group(gathered, buffers, sems):
    part = buffers[0]
    gather = Gather(gathered, sems[:4])
    heads_sum = HeadSum(part, buffers[1:], sems[4:])
    return gather, heads_sum, part


def attend(rows, qkv, wo, outs, bias, gather, heads_sum, part):
    normed_all, packed, mixed, middle = outs
    for m in range(MICRO):
        gather.hand_on(m)
    for m in range(MICRO):
        gather.finish(m)
        x = normed_all[m].reshape(LEN, D)
        q, k, v = [dot(x, qkv[which], NT).astype(jnp.bfloat16) for which in range(3)]
        packed[m, 0] = q
        packed[m, 1] = k
        packed[m, 2] = v
        if m:
            heads_sum.cross_over(m - 1)
        heads = []
        for head in range(HEADS_HERE):
            chances = softmax_rows(head_of(q, head), head_of(k, head), bias[head]).astype(jnp.bfloat16)
            heads.append(dot(chances, head_of(v, head)).astype(jnp.bfloat16))
        together = jnp.concatenate(heads, axis=1)
        mixed[m] = together
        part[m] = dot(together, wo[...]).astype(jnp.bfloat16).reshape(4, ROWS, D)
        heads_sum.start(m)
    heads_sum.cross_over(MICRO - 1)
    for m in range(MICRO):
        middle[m] = rows[m].astype(jnp.float32) + heads_sum.total(m)


def attend_back(
    middle_grad, rows, gains, normed_all, packed, mixed, qkv, wo, outs, grad_all, bias, gather, heads_sum, part, beside, done
):
    input_grad, weight_grad, offset_grad, gain_grad = outs
    me = shard_places()[0]
    for m in range(MICRO):
        grad_all[m, me] = middle_grad[m].astype(jnp.bfloat16)
        gather.start(m)
    beside(0)
    offset_grad[...] = jnp.zeros_like(offset_grad)
    row = lax.broadcasted_iota(jnp.int32, (LEN, LEN), 0)
    column = lax.broadcasted_iota(jnp.int32, (LEN, LEN), 1)
    backwards = (row + column == LEN - 1).astype(jnp.bfloat16)
    for m in range(MICRO):
        gather.hand_on(m)
    beside(1)
    for m in range(MICRO):
        gather.finish(m)
        grad = grad_all[m].reshape(LEN, D)
        mixed_grad = dot(grad, wo[...], NT).astype(jnp.bfloat16)
        if m:
            heads_sum.cross_over(m - 1)
        q, k, v = packed[m, 0], packed[m, 1], packed[m, 2]
        q_grads, k_grads, v_grads = [], [], []
        for head in range(HEADS_HERE):
            q_head, k_head, v_head = head_of(q, head), head_of(k, head), head_of(v, head)
            grad_head = head_of(mixed_grad, head)
            chances = softmax_rows(q_head, k_head, bias[head])
            grad_chances = dot(grad_head, v_head, NT)
            weighed = jnp.sum(chances * grad_chances, axis=1, keepdims=True)
            grad_scores = (chances * (grad_chances - weighed)).astype(jnp.bfloat16)
            q_grads.append((dot(grad_scores, k_head) * 0.125).astype(jnp.bfloat16))
            k_grads.append((dot(grad_scores, q_head, TN) * 0.125).astype(jnp.bfloat16))
            v_grads.append(dot(chances.astype(jnp.bfloat16), grad_head, TN).astype(jnp.bfloat16))
            turned = dot(backwards, grad_scores)
            wide = jnp.concatenate([turned, jnp.zeros_like(turned)], axis=1)
            aligned = pltpu.roll(wide, 0, 1, stride=1, stride_axis=0)
            offset_grad[pl.ds(head, 1), :] += jnp.sum(aligned, axis=0, keepdims=True)
        grads = [jnp.concatenate(pieces, axis=1) for pieces in (q_grads, k_grads, v_grads)]
        summed = dot(grads[0], qkv[0]) + dot(grads[1], qkv[1]) + dot(grads[2], qkv[2])
        part[m] = summed.astype(jnp.bfloat16).reshape(4, ROWS, D)
        heads_sum.start(m)
        if m:
            heads_sum.cross_over(m)
        x = normed_all[m].reshape(LEN, D)
        for which in range(4):
            left = grads[which] if which < 3 else mixed[m]
            added = dot(left, x if which < 3 else grad, TN)
            where = pl.ds(which * WIDTH, WIDTH)
            weight_grad[where, :] = added if m == 0 else weight_grad[where, :] + added
        beside(2 + m)
    gain_total = jnp.zeros((1, D), jnp.float32)
    for m in range(MICRO):
        back, gain_part = rms_norm_back(rows[m].astype(jnp.float32), gains[0:1, :], heads_sum.total(m))
        input_grad[m] = (middle_grad[m] + back).astype(jnp.bfloat16)
        done(m)
        gain_total = gain_total + gain_part
    gain_grad[...] = gain_total


GROUP_ROWS = 16 * PIECE
SORTED = 16 * 4
WAVE_ROWS = 4 * SORTED
PAIRS = [(dx, dz) for dx in range(4) for dz in range(4) if dx or dz]


def sorting():
    order = np.zeros((GROUP_ROWS, GROUP_ROWS), np.float32)
    for e in range(2):
        for half in range(2):
            for sender in range(16):
                for at in range(4):
                    order[(e * 2 + half) * SORTED + sender * 4 + at, sender * PIECE + half * 8 + e * 4 + at] = 1
    return jnp.asarray(order, jnp.bfloat16), jnp.asarray(order.T, jnp.bfloat16)


def sender_halves(block):
    return [block.at[pl.ds(8 * half, 8)] for half in range(2)]


class SlotsOut:
    def __init__(self, slots, arrived, sems):
        self.slots, self.arrived = slots, arrived
        self.send_x, self.recv_x, self.send_y, self.recv_y = sems[:4]
        self.cross_link = Cross(sems[4:])
        self.me, self.core, self.cross, _ = shard_places()
        self.here, self.px, self.pz = expert_places()

    def away(self, w, dx, dz):
        at = w * 16 + dx * 4 + dz
        goal = owner_at(self.px, self.pz, dx, dz)
        return remote(
            self.slots.at[w, goal],
            self.arrived.at[self.me, w, self.here],
            self.send_x.at[at],
            self.recv_x.at[at],
            "expert",
            goal,
        )

    def piece(self, w, whose, kind):
        block = self.arrived.at[whose, w]
        at = WAVES * kind + w
        return remote(block, block, self.send_y.at[at], self.recv_y.at[at], "shard", self.core)

    def near(self, w):
        return self.piece(w, self.me, 0)

    def on(self, w):
        return self.piece(w, self.cross, 1)

    def start(self, w):
        for dx, dz in PAIRS:
            self.away(w, dx, dz).start()
        self.arrived[self.me, w, self.here] = self.slots[w, self.here]

    def sent(self, w):
        for dx, dz in PAIRS:
            self.away(w, dx, dz).wait_send()

    def spread_on(self, w):
        for dx, dz in PAIRS:
            self.away(w, dx, dz).wait_recv()
        block = sender_halves(self.arrived.at[self.me, w])
        self.cross_link.start(w, block, block)
        self.near(w).start()

    def hand_on(self, w):
        self.cross_link.wait_recv(w, sender_halves(self.arrived.at[self.cross, w]))
        self.on(w).start()

    def finish(self, w):
        self.near(w).wait_recv()
        self.on(w).wait_recv()

    def drain(self):
        for w in range(WAVES):
            self.cross_link.wait_send(w, sender_halves(self.arrived.at[self.me, w]))
            self.near(w).wait_send()
            self.on(w).wait_send()


class SlotsBack:
    def __init__(self, part, returned, buffers, sems):
        self.part, self.returned = part, returned
        self.pair, self.mine, self.theirs, self.crossed, self.total = buffers
        self.send_x, self.recv_x, self.send_y, self.recv_y = sems[:4]
        self.cross_link = Cross(sems[4:])
        self.me, self.core, self.cross, self.diag = shard_places()
        self.here, self.px, self.pz = expert_places()

    def to_core(self, w, whose, buffer, kind):
        at = WAVES * kind + w
        return remote(self.part.at[whose, w], buffer.at[w], self.send_y.at[at], self.recv_y.at[at], "shard", self.core)

    def first(self, w):
        return self.to_core(w, self.diag, self.theirs, 0)

    def second(self, w):
        return self.to_core(w, self.core, self.mine, 1)

    def away(self, w, dx, dz):
        at = w * 16 + dx * 4 + dz
        goal = owner_at(self.px, self.pz, dx, dz)
        return remote(
            self.total.at[w, goal],
            self.returned.at[w, self.here],
            self.send_x.at[at],
            self.recv_x.at[at],
            "expert",
            goal,
        )

    def start(self, w):
        self.first(w).start()
        self.second(w).start()

    def cross_over(self, w):
        self.first(w).wait_recv()
        self.pair[w] = (self.part[self.cross, w].astype(jnp.float32) + self.theirs[w].astype(jnp.float32)).astype(
            jnp.bfloat16
        )
        self.cross_link.start(w, sender_halves(self.pair.at[w]), sender_halves(self.crossed.at[w]))

    def send_home(self, w):
        self.second(w).wait_recv()
        self.cross_link.wait_recv(w, sender_halves(self.crossed.at[w]))
        self.total[w] = (
            self.part[self.me, w].astype(jnp.float32)
            + self.mine[w].astype(jnp.float32)
            + self.crossed[w].astype(jnp.float32)
        ).astype(jnp.bfloat16)
        for dx, dz in PAIRS:
            self.away(w, dx, dz).start()
        self.returned[w, self.here] = self.total[w, self.here]

    def finish(self):
        for w in range(WAVES):
            for dx, dz in PAIRS:
                self.away(w, dx, dz).wait_recv()

    def drain(self):
        for w in range(WAVES):
            self.first(w).wait_send()
            self.second(w).wait_send()
            self.cross_link.wait_send(w, sender_halves(self.pair.at[w]))
            for dx, dz in PAIRS:
                self.away(w, dx, dz).wait_send()


def one_hot(equal):
    return jnp.where(equal, 1.0, 0.0).astype(jnp.bfloat16)


def to_slots(token_row, slot_column, rows, slots):
    stacked = jnp.concatenate([rows[:, :HALF], rows[:, HALF:]], axis=0)
    spread = one_hot(slot_column[...] == token_row[...])
    slots[...] = dot(spread, stacked).astype(jnp.bfloat16).reshape(WAVES, OWNERS, PIECE, HALF)


def from_slots(token_column, slot_row, slots):
    spread_t = one_hot(token_column[...] == slot_row[...])
    stacked = dot(spread_t, slots[...].reshape(WAVES * OWNERS * PIECE, HALF))
    return jnp.concatenate([stacked[: MICRO * ROWS], stacked[MICRO * ROWS :]], axis=1)


def chosen_experts(route_column):
    experts_here = lax.broadcasted_iota(jnp.int32, (MICRO * ROWS, EXPERTS), 1)
    return jnp.where(route_column[...] == experts_here, 1.0, 0.0)


def sort_in(order, arrived, w, rows, base):
    for group in range(4):
        picked = dot(order, arrived[group, w].reshape(GROUP_ROWS, HALF)).astype(jnp.bfloat16)
        for e in range(2):
            for half in range(2):
                at = (2 * e + half) * SORTED
                rows[e, pl.ds(base + group * SORTED, SORTED), half * HALF : (half + 1) * HALF] = picked[at : at + SORTED]


def sort_out(order_t, results, part, w):
    for group in range(4):
        where = slice(group * SORTED, (group + 1) * SORTED)
        pieces = [results[e, where, half * HALF : (half + 1) * HALF] for e in range(2) for half in range(2)]
        block = dot(order_t, jnp.concatenate(pieces, axis=0)).astype(jnp.bfloat16)
        part[group, w] = block.reshape(OWNERS, PIECE, HALF)


SCALE = 0.7978845608028654
CUBIC = 0.044715


def flat(rows):
    return rows.reshape(MICRO * ROWS, D)


SLOT_SEMS = (
    [pltpu.SemaphoreType.DMA((16 * WAVES,))] * 2
    + [pltpu.SemaphoreType.DMA((2 * WAVES,))] * 2
    + [pltpu.SemaphoreType.DMA((2, WAVES))] * 2
) * 2
SLOT_BUFFERS = (
    [pltpu.VMEM((WAVES, OWNERS, PIECE, HALF), jnp.bfloat16)] * 2
    + [pltpu.VMEM((4, WAVES, OWNERS, PIECE, HALF), jnp.bfloat16)]
    + [pltpu.VMEM((WAVES, OWNERS, PIECE, HALF), jnp.bfloat16)] * 5
)


def slot_exchange(arrived, buffers, sems):
    slots, returned, part, *sums = buffers
    out = SlotsOut(slots, arrived, sems[:6])
    back = SlotsBack(part, returned, sums, sems[6:])
    return out, back


def pipeline(out, back, beside, compute):
    out.start(0)
    beside()
    out.sent(0)
    out.start(1)
    out.spread_on(0)
    out.sent(1)
    out.start(2)
    out.spread_on(1)
    out.hand_on(0)
    out.sent(2)
    out.spread_on(2)
    out.hand_on(1)
    out.finish(0)
    compute(0)
    back.start(0)
    out.hand_on(2)
    out.finish(1)
    back.cross_over(0)
    compute(1)
    back.start(1)
    out.finish(2)
    back.cross_over(1)
    back.send_home(0)
    compute(2)
    out.drain()
    back.start(2)
    back.send_home(1)
    back.cross_over(2)


def experts(middle, gains, router, keys, order, order_t, inner, outer, fetched, outs, arrived, results, out, back):
    rows, normed_two, router_prob, gating, expert_rows, output = outs
    token_row, token_column, slot_row, slot_column, route_column = keys
    normed = rms_norm(flat(middle[...]), gains[1:2, :]).astype(jnp.bfloat16)
    normed_two[...] = normed
    to_slots(token_row, slot_column, normed, out.slots)

    def beside():
        logits = dot(normed, router[...], NT)
        raised = jnp.exp(logits - jnp.max(logits, axis=1, keepdims=True))
        prob = raised / jnp.sum(raised, axis=1, keepdims=True)
        router_prob[...] = prob
        gating[...] = jnp.sum(prob * chosen_experts(route_column), axis=1, keepdims=True)
        fetched()

    def compute(w):
        sort_in(order[...], arrived, w, rows, w * WAVE_ROWS)

        def one_expert(e, _):
            pre = dot(rows[e, pl.ds(w * WAVE_ROWS, WAVE_ROWS), :], inner[e])
            hidden = 0.5 * pre * (1 + jnp.tanh(SCALE * (pre + CUBIC * pre * pre * pre)))
            results[e] = dot(hidden.astype(jnp.bfloat16), outer[e]).astype(jnp.bfloat16)
            return 0

        lax.fori_loop(0, 2, one_expert, 0)
        sort_out(order_t[...], results, back.part, w)

    pipeline(out, back, beside, compute)
    back.send_home(WAVES - 1)
    back.finish()
    found = from_slots(token_column, slot_row, back.returned)
    expert_rows[...] = found.astype(jnp.bfloat16)
    output[...] = (flat(middle[...]) + gating[...] * found).astype(jnp.bfloat16).reshape(MICRO, ROWS, D)


def experts_back(
    grad_out,
    middle,
    normed_two,
    router_prob,
    gating,
    expert_rows,
    gains,
    router,
    keys,
    order,
    order_t,
    inner,
    outer,
    outs,
    middle_grad,
    grad_arrived,
    scratch,
    local,
    out,
    back,
):
    inner_grad, outer_grad, router_grad, gain_grad = outs
    rows, grads, hiddens, pre_grads, results = scratch
    token_row, token_column, slot_row, slot_column, route_column = keys
    grad = flat(grad_out[...]).astype(jnp.float32)
    to_slots(token_row, slot_column, (gating[...] * grad).astype(jnp.bfloat16), out.slots)
    gate_grad = jnp.sum(grad * expert_rows[...].astype(jnp.float32), axis=1, keepdims=True)
    logit_grad = ((gate_grad * gating[...]) * (chosen_experts(route_column) - router_prob[...])).astype(jnp.bfloat16)

    def beside():
        router_grad[...] = dot(logit_grad, normed_two[...], TN)

    def compute(w):
        base = w * WAVE_ROWS
        where = pl.ds(base, WAVE_ROWS)
        sort_in(order[...], grad_arrived, w, grads, base)

        def one_expert(e, _):
            pre = dot(rows[e, where, :], inner[e])
            squared = pre * pre
            bent = jnp.tanh(SCALE * pre * (1 + CUBIC * squared))
            slope = 0.5 * (1 + bent) + 0.5 * pre * (1 - bent * bent) * SCALE * (1 + 3 * CUBIC * squared)
            hiddens[e, where, :] = (0.5 * pre * (1 + bent)).astype(jnp.bfloat16)
            pre_grad = (dot(grads[e, where, :], outer[e], NT) * slope).astype(jnp.bfloat16)
            pre_grads[e, where, :] = pre_grad
            results[e] = dot(pre_grad, inner[e], NT).astype(jnp.bfloat16)
            return 0

        lax.fori_loop(0, 2, one_expert, 0)
        sort_out(order_t[...], results, back.part, w)

    writes = []

    def weight_grads(number, left, right, held, goal):
        def one_expert(e, _):
            for at in range(0, D, 256):
                held[e, at : at + 256, :] = dot(left[e, :, at : at + 256], right[e], TN).astype(jnp.bfloat16)
            return 0

        lax.fori_loop(0, 2, one_expert, 0)
        write = pltpu.make_async_copy(held, goal, local.at[number])
        write.start()
        writes.append(write)

    pipeline(out, back, beside, compute)
    weight_grads(0, rows, pre_grads, inner, inner_grad)
    back.send_home(WAVES - 1)
    weight_grads(1, hiddens, grads, outer, outer_grad)
    back.finish()
    normed_grad = dot(logit_grad, router[...]) + from_slots(token_column, slot_row, back.returned)
    value_grad, gain_part = rms_norm_back(flat(middle[...]), gains[1:2, :], normed_grad)
    middle_grad[...] = (grad + value_grad).reshape(MICRO, ROWS, D)
    gain_grad[...] = gain_part
    return writes


def over_section(source, goal, sems, m):
    other = 1 - lax.axis_index("section")
    return remote(source.at[m], goal.at[m], sems.at[0, m], sems.at[1, m], "section", other)


def greet_all():
    _, px, pz = expert_places()
    _, core, cross, _ = shard_places()
    peer = {"section": 1 - lax.axis_index("section")}
    return greet([{"shard": core}, {"shard": cross}, peer] + all_owners(px, pz))


SECTION_SEM = pltpu.SemaphoreType.DMA((2, MICRO))
LOCAL_SEM = pltpu.SemaphoreType.DMA((4,))
ROW_BLOCK = (MICRO, ROWS, D)


class Sums:
    def __init__(self, sources, outs, buffers, sems):
        self.big, self.small, self.table, self.gain = sources
        self.big_out, self.small_out, self.table_out, self.gain_out = outs
        self.big_in, self.big_sum, self.pair, self.small_in, self.small_sum = buffers[:5]
        self.table_in, self.gain_pair, self.gain_in = buffers[5:]
        self.sends, self.recvs, self.pair_send, self.pair_recv = sems
        self.me, self.core, self.cross, _ = shard_places()
        self.here, self.px, self.pz = expert_places()

    def each(self, kind, source, goal):
        copies = []
        for dx, dz in PAIRS:
            at, owner = dx * 4 + dz, owner_at(self.px, self.pz, dx, dz)
            copies.append(
                remote(source(owner), goal, self.sends.at[kind, at], self.recvs.at[kind, at], "expert", owner)
            )
            copies[-1].start()
        return copies

    def swap(self, n, source, goal, device):
        copy = remote(source, goal, self.pair_send.at[n], self.pair_recv.at[n], "shard", device)
        copy.start()
        return copy

    def small_near(self):
        self.near = self.swap(0, self.small, self.pair.at[0], self.core)

    def small_far(self):
        self.near.wait()
        self.small[...] += self.pair[0]
        self.far = self.swap(1, self.small, self.pair.at[1], self.cross)

    def small_away(self):
        self.far.wait()
        self.small[...] += self.pair[1]
        self.second = self.each(3, lambda owner: self.small.at[owner], self.small_in.at[self.here])
        self.small_in[self.here] = self.small[self.here]

    def small_home(self):
        for copy in self.second:
            copy.wait()
        self.small_sum[...] = jnp.sum(self.small_in[...], axis=0)
        self.third = self.each(4, lambda owner: self.small_sum, self.small_out.at[self.here])
        self.small_out[self.here] = self.small_sum[...]

    def big_away(self):
        self.first = self.each(0, lambda owner: self.big.at[owner], self.big_in.at[self.here])
        self.tables = self.each(1, lambda owner: self.table, self.table_in.at[self.here])
        self.big_in[self.here] = self.big[self.here]
        self.table_in[self.here] = self.table[...]

    def finish(self):
        near = self.swap(2, self.gain, self.gain_pair.at[0], self.core)
        near.wait()
        self.gain[...] += self.gain_pair[0]
        far = self.swap(3, self.gain, self.gain_pair.at[1], self.cross)
        far.wait()
        self.gain[...] += self.gain_pair[1]
        gains = self.each(5, lambda owner: self.gain, self.gain_in.at[self.here])
        self.gain_in[self.here] = self.gain[...]
        for copy in self.first:
            copy.wait()
        self.big_sum[...] = jnp.sum(self.big_in[...].astype(jnp.float32), axis=0).astype(jnp.bfloat16)
        last = self.each(2, lambda owner: self.big_sum, self.big_out.at[self.here])
        self.big_out[self.here] = self.big_sum[...]
        for copy in self.tables:
            copy.wait()
        self.table_out[...] = jnp.sum(self.table_in[...], axis=0)
        for copy in gains:
            copy.wait()
        self.gain_out[...] = jnp.sum(self.gain_in[...], axis=0)
        for copy in self.third + last:
            copy.wait()


BIG = (OWNERS, 4 * WIDTH // OWNERS, D)
SMALL = (OWNERS, 8, 256)
TABLE = (8, 128)
SUM_SCRATCH = [
    pltpu.VMEM(BIG, jnp.bfloat16),
    pltpu.VMEM(BIG[1:], jnp.bfloat16),
    pltpu.VMEM((2,) + SMALL, jnp.float32),
    pltpu.VMEM(SMALL, jnp.float32),
    pltpu.VMEM(SMALL[1:], jnp.float32),
    pltpu.VMEM((OWNERS,) + TABLE, jnp.float32),
    pltpu.VMEM((2,) + TABLE, jnp.float32),
    pltpu.VMEM((OWNERS,) + TABLE, jnp.float32),
]
SUM_SEMS = [pltpu.SemaphoreType.DMA((6, 16))] * 2 + [pltpu.SemaphoreType.DMA((4,))] * 2
OUTS = (
    jax.ShapeDtypeStruct(ROW_BLOCK, jnp.bfloat16),
    jax.ShapeDtypeStruct(BIG, jnp.bfloat16),
    jax.ShapeDtypeStruct(SMALL, jnp.float32),
    jax.ShapeDtypeStruct(TABLE, jnp.float32),
    jax.ShapeDtypeStruct(TABLE, jnp.float32),
    jax.ShapeDtypeStruct((2, D, D), jnp.bfloat16),
    jax.ShapeDtypeStruct((2, D, D), jnp.bfloat16),
)
STATE = [
    pltpu.VMEM((MICRO, 4, ROWS, D), jnp.bfloat16),
    pltpu.VMEM((MICRO, 3, LEN, WIDTH), jnp.bfloat16),
    pltpu.VMEM((MICRO, LEN, WIDTH), jnp.bfloat16),
    pltpu.VMEM(ROW_BLOCK, jnp.float32),
    pltpu.VMEM((2, WAVES * WAVE_ROWS, D), jnp.bfloat16),
    pltpu.VMEM((MICRO * ROWS, D), jnp.bfloat16),
    pltpu.VMEM((MICRO * ROWS, EXPERTS), jnp.float32),
    pltpu.VMEM((MICRO * ROWS, 1), jnp.float32),
    pltpu.VMEM((MICRO * ROWS, D), jnp.bfloat16),
    pltpu.VMEM(ROW_BLOCK, jnp.bfloat16),
]
GRADS = [
    pltpu.VMEM(ROW_BLOCK, jnp.bfloat16),
    pltpu.VMEM(ROW_BLOCK, jnp.float32),
    pltpu.VMEM(ROW_BLOCK, jnp.bfloat16),
    pltpu.VMEM((MICRO, 4, ROWS, D), jnp.bfloat16),
    pltpu.VMEM((4 * WIDTH, D), jnp.float32),
    pltpu.VMEM((8, 2 * LEN), jnp.float32),
    pltpu.VMEM((EXPERTS, D), jnp.float32),
    pltpu.VMEM((1, D), jnp.float32),
    pltpu.VMEM((1, D), jnp.float32),
    pltpu.VMEM(BIG, jnp.bfloat16),
    pltpu.VMEM(SMALL, jnp.float32),
    pltpu.VMEM(TABLE, jnp.float32),
    pltpu.VMEM(TABLE, jnp.float32),
]
WORK = (
    [
        pltpu.VMEM(ROW_BLOCK, jnp.bfloat16),
        pltpu.VMEM((HEADS_HERE, LEN, LEN), jnp.float32),
        pltpu.VMEM((2, D, D), jnp.bfloat16),
        pltpu.VMEM((2, D, D), jnp.bfloat16),
        pltpu.VMEM((4, WAVES, OWNERS, PIECE, HALF), jnp.bfloat16),
        SECTION_SEM,
        SECTION_SEM,
        LOCAL_SEM,
    ]
    + [pltpu.VMEM((2, WAVES * WAVE_ROWS, D), jnp.bfloat16)] * 3
    + [pltpu.VMEM((2, WAVE_ROWS, D), jnp.bfloat16)]
)
INPUTS = 14


def layers_kernel(
    own,
    gains,
    qkv,
    wo,
    by_offset,
    router,
    token_row,
    token_column,
    slot_row,
    slot_column,
    route_column,
    order,
    order_t,
    buckets,
    inner,
    outer,
    *refs,
):
    outs, refs = refs[:7], refs[7:]
    state, refs = refs[:10], refs[10:]
    grads, refs = refs[:13], refs[13:]
    incoming, bias, inner_here, outer_here, arrived, section, section_back, local = refs[:8]
    wide, refs = refs[8:12], refs[12:]
    shard_buffers, slot_buffers, refs = refs[:5], refs[5:13], refs[13:]
    shard_sems, slot_sems, refs = refs[:8], refs[8:20], refs[20:]
    normed_all, packed, mixed, middle, rows, normed_two, router_prob, gating, expert_rows, output = state
    grad_out, middle_grad, input_grad, grad_all, weight_grad, offset_grad, router_grad, gain_one, gain_two = grads[:9]
    sources = grads[9:]
    grads_wide, hiddens, pre_grads, results = wide
    gather, heads_sum, part = shard_group(normed_all, shard_buffers, shard_sems)
    gather_back, heads_sum_back, _ = shard_group(grad_all, shard_buffers, shard_sems)
    out, back = slot_exchange(arrived, slot_buffers, slot_sems)
    sums = Sums(sources, outs[1:5], refs[:8], refs[8:])
    keys = (token_row, token_column, slot_row, slot_column, route_column)
    first = lax.axis_index("section") == 0
    second = jnp.logical_not(first)
    me = shard_places()[0]

    ready = greet_all()
    fetched = copy_all((inner, outer), (inner_here, outer_here), local, 2)
    fill_bias(by_offset, bias)
    ready()

    for m in range(MICRO):

        @pl.when(first)
        def _(m=m):
            incoming[m] = own[m]

        @pl.when(second)
        def _(m=m):
            over_section(output, incoming, section, m).wait_recv()

        normed_all[m, me] = rms_norm(incoming[m].astype(jnp.float32), gains[0:1, :]).astype(jnp.bfloat16)
        gather.start(m)
    attend(incoming, qkv, wo, state[:4], bias, gather, heads_sum, part)
    experts(
        middle, gains, router, keys, order, order_t, inner_here, outer_here, fetched, state[4:], arrived, results, out, back
    )
    for stage in (gather, heads_sum, back):
        stage.drain()

    for m in range(MICRO):

        @pl.when(first)
        def _(m=m):
            over_section(output, incoming, section, m).start()

        @pl.when(second)
        def _(m=m):
            outs[0][m] = output[m]
            grad_out[m] = own[m]

    @pl.when(first)
    def _():
        for m in range(MICRO):
            over_section(input_grad, grad_out, section_back, m).wait_recv()

    writes = experts_back(
        grad_out,
        middle,
        normed_two,
        router_prob,
        gating,
        expert_rows,
        gains,
        router,
        keys,
        order,
        order_t,
        inner_here,
        outer_here,
        (outs[5], outs[6], router_grad, gain_two),
        middle_grad,
        arrived,
        (rows, grads_wide, hiddens, pre_grads, results),
        local,
        out,
        back,
    )

    def beside(step):
        if step == 0:
            small = sources[1]
            extra = jnp.concatenate([gain_two[...], jnp.zeros((7, D), jnp.float32)], axis=0)
            for group in range(5):
                block = router_grad[group * 8 : group * 8 + 8, :] if group < 4 else extra
                for third in range(3):
                    small[group * 3 + third] = block[:, third * 256 : (third + 1) * 256]
            small[15] = jnp.zeros(SMALL[1:], jnp.float32)
            sums.small_near()
        if step == 1:
            sums.small_far()
        if step == 2:
            sums.small_away()
        if step == 3:
            sources[0][...] = weight_grad[...].astype(jnp.bfloat16).reshape(BIG)
            sources[2][...] = lax.dot_general(
                offset_grad[...], buckets[...], (((1,), (0,)), ((), ())), precision=lax.Precision.HIGHEST
            )
            sums.small_home()
            sums.big_away()

    def done(m):
        @pl.when(first)
        def _():
            outs[0][m] = input_grad[m]

        @pl.when(second)
        def _():
            over_section(input_grad, grad_out, section_back, m).start()

    attend_back(
        middle_grad,
        incoming,
        gains,
        normed_all,
        packed,
        mixed,
        qkv,
        wo,
        (input_grad, weight_grad, offset_grad, gain_one),
        grad_all,
        bias,
        gather_back,
        heads_sum_back,
        part,
        beside,
        done,
    )
    pieces = [gain_one[:, at : at + 128] for at in range(0, D, 128)]
    sources[3][...] = jnp.concatenate(pieces + [jnp.zeros((2, 128), jnp.float32)], axis=0)
    sums.finish()
    for stage in (back, gather_back, heads_sum_back):
        stage.drain()
    for m in range(MICRO):

        @pl.when(first)
        def _(m=m):
            over_section(output, incoming, section, m).wait_send()

        @pl.when(second)
        def _(m=m):
            over_section(input_grad, grad_out, section_back, m).wait_send()

    for write in writes:
        write.wait()


def both_layers(*arrays):
    return pl.pallas_call(
        layers_kernel,
        out_shape=OUTS,
        in_specs=[VMEM] * INPUTS + [ANY] * 2,
        out_specs=(VMEM,) * 5 + (ANY,) * 2,
        scratch_shapes=STATE
        + GRADS
        + WORK
        + SHARD_BUFFERS
        + SLOT_BUFFERS
        + SHARD_SEMS
        + SLOT_SEMS
        + SUM_SCRATCH
        + SUM_SEMS,
        compiler_params=pltpu.CompilerParams(collective_id=0, has_side_effects=True, vmem_limit_bytes=VMEM_BYTES),
        name="both_layers",
    )(*arrays)


def bucket_of(offsets):
    distance = jnp.abs(offsets)
    far_bucket = 8 + sum(
        ((distance >= threshold).astype(jnp.int32) for threshold in (12, 16, 23, 32, 46, 64, 91))
    )
    near_far = jnp.where(distance < 8, distance, far_bucket)
    return near_far + 16 * (offsets > 0).astype(jnp.int32)


def offset_buckets():
    offsets = jnp.arange(2 * LEN, dtype=jnp.int32) - (LEN - 1)
    return (bucket_of(offsets)[:, None] == jnp.arange(32, dtype=jnp.int32)[None, :]).astype(jnp.float32)


def slot_keys():
    row = np.arange(WAVES * OWNERS * PIECE)
    half, expert = row % 16 // 8, row % 8 // 4
    slot_row = row // (OWNERS * PIECE) * 4 + row % 4
    return ((half * EXPERTS + row // PIECE % OWNERS * 2 + expert) * (MICRO * CAP) + slot_row).astype(np.int32)


def token_keys(route_ids, slot_ids):
    micro = jnp.arange(MICRO, dtype=jnp.int32)[:, None]
    key = (route_ids * (MICRO * CAP) + micro * CAP + slot_ids).reshape(-1)
    return jnp.concatenate([key, key + EXPERTS * MICRO * CAP])


def per_device(
    stream, norm_gains, attn_qkv, attn_out, rel_bias, router, expert_in, expert_out, routes, slots
):
    buckets = offset_buckets()
    by_offset = lax.dot_general(
        rel_bias[0], buckets, (((0,), (1,)), ((), ())), precision=lax.Precision.HIGHEST
    )
    by_offset = jnp.concatenate([by_offset, jnp.zeros((5, 2 * LEN), jnp.float32)], axis=0)
    tokens, slot_rows = token_keys(routes[0], slots[0]), jnp.asarray(slot_keys())
    common = (norm_gains[0], jnp.swapaxes(attn_qkv[0], 1, 2), attn_out[0], by_offset, router[0].T)
    common += (tokens[None, :], tokens[:, None], slot_rows[None, :], slot_rows[:, None], routes[0].reshape(-1, 1))
    common += sorting() + (jnp.pad(buckets, ((0, 0), (0, 96))), expert_in[0], expert_out[0])
    end_rows, big, small, table, gain_one, inner_grad, outer_grad = both_layers(stream[0], *common)

    big = big.reshape(4, WIDTH, D).astype(jnp.float32)
    small = jnp.swapaxes(small[:15].reshape(5, 3, 8, 256), 1, 2).reshape(40, D)
    return (
        end_rows[None],
        jnp.concatenate([gain_one[:6].reshape(1, D), small[32:33]], axis=0)[None],
        jnp.swapaxes(big[:3], 1, 2)[None],
        big[3][None],
        table[:3, :32].T[None],
        small[:32].T[None],
        inner_grad.astype(jnp.float32)[None],
        outer_grad.astype(jnp.float32)[None],
    )


def solution(mesh):
    return jax.shard_map(
        per_device,
        mesh=mesh,
        in_specs=(
            P("section", None, ("expert", "shard"), None),
            P("section", None, None),
            P("section", None, None, "shard"),
            P("section", "shard", None),
            P("section", None, "shard"),
            P("section", None, None),
            P("section", "expert", None, "shard"),
            P("section", "expert", "shard", None),
            P("section", None, ("expert", "shard")),
            P("section", None, ("expert", "shard")),
        ),
        out_specs=(
            P("section", None, ("expert", "shard"), None),
            P("section", None, None),
            P("section", None, None, "shard"),
            P("section", "shard", None),
            P("section", None, "shard"),
            P("section", None, None),
            P("section", "expert", None, "shard"),
            P("section", "expert", "shard", None),
        ),
        check_vma=False,
    )
```

time: 452 us -> 384 us (0.85)
  Pallas kernels: 416 us -> 358 us
  local copies, waits for them, and re-layouts: 18.7 us -> 7.21 us
    pallas_call x5 -> x1, Pallas kernels: 416 us -> 358 us  [both_layers(): pl.pallas_call(layers_kernel, out_shape=OUTS, in_specs=[VMEM] * INPUTS +...]
    unnamed x28 -> x16, local copies, waits for them, and re-layouts: 10.4 us -> 1.34 us
    broadcast_in_dim x1 -> x2, other arithmetic: 0.79 us -> 7.64 us  [the longest x1 7.03 us: per_device(): outer_grad.astype(jnp.float32)[None]]
    convert_element_type x4 -> x0, other arithmetic: 5.7 us -> none  [the longest x1 2.79 us: per_device(): big = attend_grad.astype(jnp.bfloat16).reshape(OWNERS, 48, D)]
where the time goes in v3:
time: 384 us; the launch traced here: 377 us
  Pallas kernels  358 us (93%)
  other arithmetic  9.49 us (2%)
  local copies, waits for them, and re-layouts  7.21 us (2%)
    pallas_call x1, Pallas kernels, both_layers(): pl.pallas_call(layers_kernel, out_shape=OUTS, in_specs=[VMEM] * INPUTS +...  358 us

profile of v3, /device:TPU:0, one launch (start us, length us, event | category | flops | bytes accessed | tf_op | source)
XLA Modules:
  0.0 377.3 jit_solution(450536912214207952)
XLA Ops:
  0.6 0.8 broadcast_add_fusion
  1.4 0.0 copy-start.3
  1.4 0.9 copy.22.token_column
  2.3 0.2 iota_compare_fusion
  2.5 0.8 pad_convert_fusion.buckets
  3.4 1.1 convolution_bitcast_fusion
  4.5 0.6 concatenate.9.by_offset
  5.1 1.5 copy.23.route_column
  6.6 0.0 copy-done.3
  6.6 358.4 %both_layers.1 = (bf16[2,128,768]{2,1,0:T(8,128)(2,1)}, bf16[16,48,768]{2,1,0:T(8,128)(2,1)}, f32[16,8,256]{2,1,0:T(8,128)}, f32[8,128]{1,0:T(8,128)}, f32[8,128...) custom-call(bf16[2,128,768]{2,1,0:T(8,128)(2,1)} %bitcast.72, f32[2,768]{1,0:T(2,128)} %bitcast.80, ...), custom_call_target="tpu_custom_call" | custom-call | tf_op jit(solution)/shard_map/both_layers/pallas_call | solution.py:1009
  365.1 0.0 copy-start.2
  365.1 0.0 copy-start.4
  365.1 0.0 copy-start
  365.1 7.0 %bitcast_convert_fusion = (f32[1,2,768,768]{3,2,1,0:T(8,128)}, f32[1,2,768,768]{3,2,1,0:T(8,128)}) fusion(bf16[2,768,768]{2,1,0:T(8,128)(2,1)} %get-tuple-element.21, bf16[2,768,768]{2,1,0:T(8,128)(2,1)} %get-tuple-element.20), kind=kLoop, calls=%fused_computation | loop fusion | flops 2359296 | bytes 14155776 | tf_op jit(solution)/shard_map/broadcast_in_dim | solution.py:1079
  372.1 0.0 copy-done.2
  372.1 0.0 copy-done.4
  372.2 0.6 maximum_bitcast_fusion
  372.8 0.0 copy-done
  372.8 0.0 copy-start.5
  372.8 0.0 copy-start.1
  372.8 1.4 slice.41
  374.2 0.9 slice.42
  375.0 0.6 slice.43
  375.7 0.0 copy-done.5
  375.7 0.6 copy.24
  376.2 0.0 copy-done.1
  376.2 0.7 copy.34
  (8 shorter events, 0.0 us)
Async XLA Ops:
  1.4 5.2 %copy-start.3 = (s32[512]{0:T(512)}, s32[512]{0:T(512)S(1)}, u32[]{:S(2)}) copy-start(s32[512]{0:T(512)S(1)} %pad_add_fusion) | copy-start | bytes 6148
  365.1 7.1 %copy-start.2 = (f32[16,8,256]{2,1,0:T(8,128)S(1)}, f32[16,8,256]{2,1,0:T(8,128)}, u32[]{:S(2)}) copy-start(f32[16,8,256]{2,1,0:T(8,128)} %get-tuple-element.17) | copy-start | bytes 393220
  365.1 7.1 %copy-start.4 = (f32[8,128]{1,0:T(8,128)S(1)}, f32[8,128]{1,0:T(8,128)}, u32[]{:S(2)}) copy-start(f32[8,128]{1,0:T(8,128)} %get-tuple-element.16) | copy-start | bytes 12292
  365.1 7.7 %copy-start = (bf16[16,48,768]{2,1,0:T(8,128)(2,1)S(1)}, bf16[16,48,768]{2,1,0:T(8,128)(2,1)}, u32[]{:S(2)}) copy-start(bf16[16,48,768]{2,1,0:T(8,128)(2,1)} %get-tuple-element.18) | copy-start | bytes 3538948
  372.8 2.9 copy-start.5
  372.8 3.5 copy-start.1

commit v4 on v3

--- a/solution.py
+++ b/solution.py
@@ -258,7 +258,7 @@
 
 
 def attend_back(
-    middle_grad, rows, gains, normed_all, packed, mixed, qkv, wo, outs, grad_all, bias, gather, heads_sum, part, beside, done
+    middle_grad, rows, gains, normed_all, packed, mixed, qkv, wo, outs, grad_all, dqkv, bias, gather, heads_sum, part, beside, done
 ):
     input_grad, weight_grad, offset_grad, gain_grad = outs
     me = shard_places()[0]
@@ -296,18 +296,22 @@
             aligned = pltpu.roll(wide, 0, 1, stride=1, stride_axis=0)
             offset_grad[pl.ds(head, 1), :] += jnp.sum(aligned, axis=0, keepdims=True)
         grads = [jnp.concatenate(pieces, axis=1) for pieces in (q_grads, k_grads, v_grads)]
+        for which in range(3):
+            dqkv[m, which] = grads[which]
         summed = dot(grads[0], qkv[0]) + dot(grads[1], qkv[1]) + dot(grads[2], qkv[2])
         part[m] = summed.astype(jnp.bfloat16).reshape(4, ROWS, D)
         heads_sum.start(m)
         if m:
             heads_sum.cross_over(m)
-        x = normed_all[m].reshape(LEN, D)
-        for which in range(4):
-            left = grads[which] if which < 3 else mixed[m]
-            added = dot(left, x if which < 3 else grad, TN)
-            where = pl.ds(which * WIDTH, WIDTH)
-            weight_grad[where, :] = added if m == 0 else weight_grad[where, :] + added
-        beside(2 + m)
+        if m == 0:
+            beside(2)
+    both = MICRO * LEN
+    for which in range(4):
+        left = (dqkv[:, which] if which < 3 else mixed[...]).reshape(both, WIDTH)
+        right = (normed_all if which < 3 else grad_all)[...].reshape(both, D)
+        owners = slice(which * 4, which * 4 + 4)
+        weight_grad[owners] = dot(left, right, TN).astype(jnp.bfloat16).reshape(4, WIDTH // 4, D)
+    beside(3)
     gain_total = jnp.zeros((1, D), jnp.float32)
     for m in range(MICRO):
         back, gain_part = rms_norm_back(rows[m].astype(jnp.float32), gains[0:1, :], heads_sum.total(m))
@@ -483,9 +487,10 @@
     return jnp.concatenate([stacked[: MICRO * ROWS], stacked[MICRO * ROWS :]], axis=1)
 
 
-def chosen_experts(route_column):
-    experts_here = lax.broadcasted_iota(jnp.int32, (MICRO * ROWS, EXPERTS), 1)
-    return jnp.where(route_column[...] == experts_here, 1.0, 0.0)
+def chosen_experts(token_column):
+    key = token_column[: MICRO * ROWS, :]
+    start = lax.broadcasted_iota(jnp.int32, (MICRO * ROWS, EXPERTS), 1) * (MICRO * CAP)
+    return jnp.where(jnp.logical_and(key >= start, key < start + MICRO * CAP), 1.0, 0.0)
 
 
 def sort_in(order, arrived, w, rows, base):
@@ -565,7 +570,7 @@
 
 def experts(middle, gains, router, keys, order, order_t, inner, outer, fetched, outs, arrived, results, out, back):
     rows, normed_two, router_prob, gating, expert_rows, output = outs
-    token_row, token_column, slot_row, slot_column, route_column = keys
+    token_row, token_column, slot_row, slot_column = keys
     normed = rms_norm(flat(middle[...]), gains[1:2, :]).astype(jnp.bfloat16)
     normed_two[...] = normed
     to_slots(token_row, slot_column, normed, out.slots)
@@ -575,7 +580,7 @@
         raised = jnp.exp(logits - jnp.max(logits, axis=1, keepdims=True))
         prob = raised / jnp.sum(raised, axis=1, keepdims=True)
         router_prob[...] = prob
-        gating[...] = jnp.sum(prob * chosen_experts(route_column), axis=1, keepdims=True)
+        gating[...] = jnp.sum(prob * chosen_experts(token_column), axis=1, keepdims=True)
         fetched()
 
     def compute(w):
@@ -622,11 +627,11 @@
 ):
     inner_grad, outer_grad, router_grad, gain_grad = outs
     rows, grads, hiddens, pre_grads, results = scratch
-    token_row, token_column, slot_row, slot_column, route_column = keys
+    token_row, token_column, slot_row, slot_column = keys
     grad = flat(grad_out[...]).astype(jnp.float32)
     to_slots(token_row, slot_column, (gating[...] * grad).astype(jnp.bfloat16), out.slots)
     gate_grad = jnp.sum(grad * expert_rows[...].astype(jnp.float32), axis=1, keepdims=True)
-    logit_grad = ((gate_grad * gating[...]) * (chosen_experts(route_column) - router_prob[...])).astype(jnp.bfloat16)
+    logit_grad = ((gate_grad * gating[...]) * (chosen_experts(token_column) - router_prob[...])).astype(jnp.bfloat16)
 
     def beside():
         router_grad[...] = dot(logit_grad, normed_two[...], TN)
@@ -808,7 +813,7 @@
     pltpu.VMEM(ROW_BLOCK, jnp.float32),
     pltpu.VMEM(ROW_BLOCK, jnp.bfloat16),
     pltpu.VMEM((MICRO, 4, ROWS, D), jnp.bfloat16),
-    pltpu.VMEM((4 * WIDTH, D), jnp.float32),
+    pltpu.VMEM((MICRO, 3, LEN, WIDTH), jnp.bfloat16),
     pltpu.VMEM((8, 2 * LEN), jnp.float32),
     pltpu.VMEM((EXPERTS, D), jnp.float32),
     pltpu.VMEM((1, D), jnp.float32),
@@ -832,7 +837,7 @@
     + [pltpu.VMEM((2, WAVES * WAVE_ROWS, D), jnp.bfloat16)] * 3
     + [pltpu.VMEM((2, WAVE_ROWS, D), jnp.bfloat16)]
 )
-INPUTS = 14
+INPUTS = 13
 
 
 def layers_kernel(
@@ -840,13 +845,12 @@
     gains,
     qkv,
     wo,
-    by_offset,
+    rel_table,
     router,
     token_row,
     token_column,
     slot_row,
     slot_column,
-    route_column,
     order,
     order_t,
     buckets,
@@ -862,21 +866,24 @@
     shard_buffers, slot_buffers, refs = refs[:5], refs[5:13], refs[13:]
     shard_sems, slot_sems, refs = refs[:8], refs[8:20], refs[20:]
     normed_all, packed, mixed, middle, rows, normed_two, router_prob, gating, expert_rows, output = state
-    grad_out, middle_grad, input_grad, grad_all, weight_grad, offset_grad, router_grad, gain_one, gain_two = grads[:9]
+    grad_out, middle_grad, input_grad, grad_all, dqkv, offset_grad, router_grad, gain_one, gain_two = grads[:9]
     sources = grads[9:]
     grads_wide, hiddens, pre_grads, results = wide
     gather, heads_sum, part = shard_group(normed_all, shard_buffers, shard_sems)
     gather_back, heads_sum_back, _ = shard_group(grad_all, shard_buffers, shard_sems)
     out, back = slot_exchange(arrived, slot_buffers, slot_sems)
     sums = Sums(sources, outs[1:5], refs[:8], refs[8:])
-    keys = (token_row, token_column, slot_row, slot_column, route_column)
+    keys = (token_row, token_column, slot_row, slot_column)
     first = lax.axis_index("section") == 0
     second = jnp.logical_not(first)
     me = shard_places()[0]
 
     ready = greet_all()
     fetched = copy_all((inner, outer), (inner_here, outer_here), local, 2)
-    fill_bias(by_offset, bias)
+    offset_grad[...] = lax.dot_general(
+        rel_table[...], buckets[...], (NT, ((), ())), precision=lax.Precision.HIGHEST
+    )
+    fill_bias(offset_grad, bias)
     ready()
 
     for m in range(MICRO):
@@ -952,7 +959,6 @@
         if step == 2:
             sums.small_away()
         if step == 3:
-            sources[0][...] = weight_grad[...].astype(jnp.bfloat16).reshape(BIG)
             sources[2][...] = lax.dot_general(
                 offset_grad[...], buckets[...], (((1,), (0,)), ((), ())), precision=lax.Precision.HIGHEST
             )
@@ -977,8 +983,9 @@
         mixed,
         qkv,
         wo,
-        (input_grad, weight_grad, offset_grad, gain_one),
+        (input_grad, sources[0], offset_grad, gain_one),
         grad_all,
+        dqkv,
         bias,
         gather_back,
         heads_sum_back,
@@ -1025,18 +1032,12 @@
     )(*arrays)
 
 
-def bucket_of(offsets):
-    distance = jnp.abs(offsets)
-    far_bucket = 8 + sum(
-        ((distance >= threshold).astype(jnp.int32) for threshold in (12, 16, 23, 32, 46, 64, 91))
-    )
-    near_far = jnp.where(distance < 8, distance, far_bucket)
-    return near_far + 16 * (offsets > 0).astype(jnp.int32)
-
-
 def offset_buckets():
-    offsets = jnp.arange(2 * LEN, dtype=jnp.int32) - (LEN - 1)
-    return (bucket_of(offsets)[:, None] == jnp.arange(32, dtype=jnp.int32)[None, :]).astype(jnp.float32)
+    offsets = np.arange(2 * LEN) - (LEN - 1)
+    distance = np.abs(offsets)
+    far_bucket = 8 + sum((distance >= threshold).astype(np.int32) for threshold in (12, 16, 23, 32, 46, 64, 91))
+    bucket = np.where(distance < 8, distance, far_bucket) + 16 * (offsets > 0)
+    return jnp.asarray(bucket[:, None] == np.arange(128)[None, :], jnp.float32)
 
 
 def slot_keys():
@@ -1055,15 +1056,11 @@
 def per_device(
     stream, norm_gains, attn_qkv, attn_out, rel_bias, router, expert_in, expert_out, routes, slots
 ):
-    buckets = offset_buckets()
-    by_offset = lax.dot_general(
-        rel_bias[0], buckets, (((0,), (1,)), ((), ())), precision=lax.Precision.HIGHEST
-    )
-    by_offset = jnp.concatenate([by_offset, jnp.zeros((5, 2 * LEN), jnp.float32)], axis=0)
+    rel_table = jnp.pad(rel_bias[0].T, ((0, 5), (0, 96)))
     tokens, slot_rows = token_keys(routes[0], slots[0]), jnp.asarray(slot_keys())
-    common = (norm_gains[0], jnp.swapaxes(attn_qkv[0], 1, 2), attn_out[0], by_offset, router[0].T)
-    common += (tokens[None, :], tokens[:, None], slot_rows[None, :], slot_rows[:, None], routes[0].reshape(-1, 1))
-    common += sorting() + (jnp.pad(buckets, ((0, 0), (0, 96))), expert_in[0], expert_out[0])
+    common = (norm_gains[0], jnp.swapaxes(attn_qkv[0], 1, 2), attn_out[0], rel_table, router[0].T)
+    common += (tokens[None, :], tokens[:, None], slot_rows[None, :], slot_rows[:, None])
+    common += sorting() + (offset_buckets(), expert_in[0], expert_out[0])
     end_rows, big, small, table, gain_one, inner_grad, outer_grad = both_layers(stream[0], *common)
 
     big = big.reshape(4, WIDTH, D).astype(jnp.float32)

time: 384 us -> 377 us (0.982)
  no operation moved by 1% of the time
where the time goes in v4:
time: 377 us; the launch traced here: 370 us
  Pallas kernels  355 us (94%)
  other arithmetic  8.42 us (2%)
  local copies, waits for them, and re-layouts  6.38 us (2%)
    pallas_call x1, Pallas kernels, both_layers(): pl.pallas_call(layers_kernel, out_shape=OUTS, in_specs=[VMEM] * INPUTS +...  355 us

profile of v4, /device:TPU:0, one launch (start us, length us, event | category | flops | bytes accessed | tf_op | source)
XLA Modules:
  0.0 370.5 jit_solution(8074508322291490831)
XLA Ops:
  0.6 0.8 broadcast_add_fusion
  1.4 0.0 copy-start.3
  1.4 0.9 copy.23.token_column
  2.3 0.7 copy.30
  3.0 0.6 pad.4.rel_table
  3.6 0.0 copy-done.3
  3.6 354.7 %both_layers.1 = (bf16[2,128,768]{2,1,0:T(8,128)(2,1)}, bf16[16,48,768]{2,1,0:T(8,128)(2,1)}, f32[16,8,256]{2,1,0:T(8,128)}, f32[8,128]{1,0:T(8,128)}, f32[8,128...) custom-call(bf16[2,128,768]{2,1,0:T(8,128)(2,1)} %bitcast.71, f32[2,768]{1,0:T(2,128)} %bitcast.80, ...), custom_call_target="tpu_custom_call" | custom-call | tf_op jit(solution)/shard_map/both_layers/pallas_call | solution.py:1016
  358.3 0.0 copy-start.2
  358.3 0.0 copy-start.4
  358.3 0.0 copy-start
  358.3 7.0 %bitcast_convert_fusion = (f32[1,2,768,768]{3,2,1,0:T(8,128)}, f32[1,2,768,768]{3,2,1,0:T(8,128)}) fusion(bf16[2,768,768]{2,1,0:T(8,128)(2,1)} %get-tuple-element.21, bf16[2,768,768]{2,1,0:T(8,128)(2,1)} %get-tuple-element.20), kind=kLoop, calls=%fused_computation | loop fusion | flops 2359296 | bytes 14155776 | tf_op jit(solution)/shard_map/broadcast_in_dim | solution.py:1076
  365.4 0.0 copy-done.2
  365.4 0.0 copy-done.4
  365.4 0.6 maximum_bitcast_fusion
  366.0 0.0 copy-done
  366.0 0.0 copy-start.5
  366.0 0.0 copy-start.1
  366.0 1.4 slice.41
  367.4 0.9 slice.42
  368.3 0.6 slice.43
  368.9 0.0 copy-done.5
  368.9 0.6 copy.24
  369.5 0.0 copy-done.1
  369.5 0.7 copy.32
  (7 shorter events, 0.0 us)
Async XLA Ops:
  1.4 2.2 copy-start.3
  358.3 7.1 %copy-start.2 = (f32[16,8,256]{2,1,0:T(8,128)S(1)}, f32[16,8,256]{2,1,0:T(8,128)}, u32[]{:S(2)}) copy-start(f32[16,8,256]{2,1,0:T(8,128)} %get-tuple-element.17) | copy-start | bytes 393220
  358.3 7.1 %copy-start.4 = (f32[8,128]{1,0:T(8,128)S(1)}, f32[8,128]{1,0:T(8,128)}, u32[]{:S(2)}) copy-start(f32[8,128]{1,0:T(8,128)} %get-tuple-element.16) | copy-start | bytes 12292
  358.3 7.7 %copy-start = (bf16[16,48,768]{2,1,0:T(8,128)(2,1)S(1)}, bf16[16,48,768]{2,1,0:T(8,128)(2,1)}, u32[]{:S(2)}) copy-start(bf16[16,48,768]{2,1,0:T(8,128)(2,1)} %get-tuple-element.18) | copy-start | bytes 3538948
  366.0 2.9 copy-start.5
  366.0 3.5 copy-start.1
